TPU v7x, 256 devices: a whole 4x4x8 slice. The times are simulated.
256 devices in a mesh: depth: 32 (over x_lo, z, core), tile: 8 (over x_hi, y).
Axes of the slice: x: 4 (x_hi: 2, x_lo: 2; x = x_hi * 2 + x_lo), y: 4, z: 8, core: 2. Of those that a mesh axis runs over, the one named last changes fastest.
Arguments:
- density: bfloat16 [3, 256, 16, 4096], P(None, 'depth', 'tile'), may hold values from 0 to 1
- material_weight: float32 [4, 3], replicated, may hold values from 0.3 to 3
- color_table: int32 [4, 4, 256], replicated, may hold values from 0 to 255
Outputs:
- pixels: float32 [4, 4, 16, 4096], P(None, None, 'tile', 'depth')
Inputs may be any that keep to these rules, and one draw needn't show every extreme that they name: `color_table`: levels of a transfer function, 255 meaning full.
All inputs are finite; a program needn't handle non-finite values.
Results may differ from a plain program's by a relative error of at most 0.0003.
Values may be sent and summed in bfloat16 or wider, within the bound.
No kernel may reach another device: no remote copies, remote signals or barrier semaphores. Data moves between devices by JAX's collectives and lax.ppermute only.
A program may use at most 128 MiB of HBM per device.

v0:
```python
import jax
import jax.numpy as jnp
from jax import lax
from jax.sharding import PartitionSpec as P


def padded_2(cells, sides, width):
    for axis, dim in sides:
        count = lax.axis_size(axis)
        ends = count - 1
        head = lax.slice_in_dim(cells, 0, width, axis=dim)
        tail = lax.slice_in_dim(cells, cells.shape[dim] - width, cells.shape[dim], axis=dim)
        cells = jnp.concatenate(
            [
                lax.ppermute(tail, axis, [(i, (i + 1) % count) for i in range(ends)]),
                cells,
                lax.ppermute(head, axis, [((i + 1) % count, i) for i in range(ends)]),
            ],
            axis=dim,
        )
    return cells


def entering(part, axis, combine, identity):
    place = lax.axis_index(axis)
    gathered = lax.all_gather(part, axis)
    state = jnp.zeros_like(part) + jnp.asarray(identity, part.dtype)

    def one(turn, state):
        return combine(state, lax.dynamic_index_in_dim(gathered, turn, 0, False))

    return lax.fori_loop(0, place, one, state)


def shade_samples(middle, slope_z, slope_y, slope_x, material_weight, color_table, depth_total):
    highest = lax.Precision.HIGHEST
    atten = jnp.dot(material_weight, middle, precision=highest)
    grad_z = jnp.dot(material_weight, slope_z, precision=highest)
    grad_y = jnp.dot(material_weight, slope_y, precision=highest)
    grad_x = jnp.dot(material_weight, slope_x, precision=highest)
    slope_sq = grad_z * grad_z + grad_y * grad_y + grad_x * grad_x
    shading = 0.3 + 0.7 * jnp.abs(0.8 * grad_z + 0.48 * grad_y + 0.36 * grad_x) / jnp.sqrt(
        slope_sq + 1.0
    )
    gate_term = slope_sq / (1.0 + slope_sq)
    table_level = 255.0 * (1.0 - jnp.exp(-0.5 * atten))
    bin_centers = jnp.arange(color_table.shape[2], dtype=jnp.float32)[:, None]
    looked = []
    for energy in range(material_weight.shape[0]):
        hat_weights = jnp.maximum(
            0.0, 1.0 - jnp.abs(table_level[energy][None, :] - bin_centers)
        ).astype(jnp.bfloat16)
        looked.append(
            jnp.dot(
                color_table[energy].astype(jnp.bfloat16),
                hat_weights,
                preferred_element_type=jnp.float32,
            )
        )
    colour = jnp.stack(looked) / 255.0
    opacity = colour[:, 3] * gate_term * (6.0 / depth_total)
    emission = opacity[:, None] * colour[:, :3] * shading[:, None]
    return (emission, 1.0 - opacity)


def multiply(earlier, later):
    return earlier * later


def body(density, material_weight, color_table):
    mats, planes, lines, columns = density.shape
    energies = material_weight.shape[0]
    depth_total = planes * lax.axis_size("depth")
    padded = padded_2(density, (("depth", 1), ("tile", 2)), 1)
    widened = jnp.pad(padded.astype(jnp.float32), ((0, 0), (0, 0), (0, 0), (1, 1)))
    middle = widened[:, 1:-1, 1:-1, 1:-1]
    slope_z = (widened[:, 2:, 1:-1, 1:-1] - widened[:, :-2, 1:-1, 1:-1]) * 0.5
    slope_y = (widened[:, 1:-1, 2:, 1:-1] - widened[:, 1:-1, :-2, 1:-1]) * 0.5
    slope_x = (widened[:, 1:-1, 1:-1, 2:] - widened[:, 1:-1, 1:-1, :-2]) * 0.5
    stacked = jnp.stack([middle, slope_z, slope_y, slope_x])
    stacked = stacked.reshape(4, mats, planes * lines, columns).transpose(2, 0, 1, 3)

    def per_line(fields):
        return shade_samples(
            fields[0], fields[1], fields[2], fields[3], material_weight, color_table, depth_total
        )

    emission, transmit = lax.map(per_line, stacked)
    emission = emission.reshape(planes, lines, energies, 3, columns)
    transmit = transmit.reshape(planes, lines, energies, columns)
    inclusive = jnp.cumprod(transmit, axis=0)
    exclusive = jnp.concatenate([jnp.ones_like(inclusive[:1]), inclusive[:-1]], axis=0)
    brick_color = jnp.sum(exclusive[:, :, :, None, :] * emission, axis=0).transpose(1, 2, 0, 3)
    brick_keep = inclusive[-1].transpose(1, 0, 2)
    ahead = entering(brick_keep, "depth", multiply, jnp.ones_like(brick_keep))
    terms = jnp.concatenate(
        [ahead[:, None] * brick_color, (ahead * (1.0 - brick_keep))[:, None]], axis=1
    )
    return lax.psum_scatter(terms, "depth", scatter_dimension=3, tiled=True)


def solution(mesh):
    return jax.shard_map(
        body,
        mesh=mesh,
        in_specs=(P(None, "depth", "tile", None), P(), P()),
        out_specs=P(None, None, "tile", "depth"),
        check_vma=False,
    )
```

profile of v0, /device:TPU:4, one launch (start us, length us, event | category | flops | bytes accessed | tf_op | source)
XLA Modules:
  0.0 473.2 jit_solution(15269013509191295450)
XLA Ops:
  7.4 1.7 collective-permute-start
  9.2 1.3 collective-permute-start.1
  10.5 1.4 constant_dynamic-update-slice_fusion.1
  11.9 2.1 collective-permute-done.1
  14.1 1.9 fusion.45
  15.9 3.5 collective-permute-start.2
  19.4 6.0 %collective-permute-start.3 = (bf16[3,10,1,4096]{3,2,1,0:T(2,128)(2,1)S(1)}, bf16[3,10,1,4096]{3,2,1,0:T(2,128)(2,1)S(1)}, u32[]{:S(2)}, u32[]{:S(2)}) collective-permute-start(bf16[3,10,1,4096]{3,2,1,0:T(2,128)(2,1)S(1)} %get-tuple-element.166), channel_id=1, source_target_pairs={{1,0},{2,1},{3,2},{4,3},{5,4},{6,5},{7,6},{9,8},{10,9},{11,10},{12... | collective-permute-start | bytes 737288 | tf_op jit(solution)/shard_map/ppermute | solution.py:17
  26.2 7.7 %collective-permute-done.2 = bf16[3,10,1,4096]{3,2,1,0:T(2,128)(2,1)S(1)} collective-permute-done((bf16[3,10,1,4096]{3,2,1,0:T(2,128)(2,1)}, bf16[3,10,1,4096]{3,2,1,0:T(2,128)(2,1)S(1)}, u32[]{:S(2)}, u32[]{:S(2)}) %collective-permute-start.2) | collective-permute-done | bytes 245792 | tf_op jit(solution)/shard_map/ppermute | solution.py:15
  33.9 1.5 collective-permute-done.3
  35.4 1.5 maximum_convert_fusion.8
  36.9 3.2 fusion.44
  42.4 2.5 maximum_bitcast_fusion
  44.9 138.0 %while.24 = (s32[]{:T(128)}, f32[16,4,3,4096]{3,2,1,0:T(4,128)}, f32[16,4,4096]{2,1,0:T(4,128)S(1)}, f32[16,4,3,4096]{3,2,1,0:T(4,128)}, f32[4,3]{1,0:T(4,128)S(...) while((s32[]{:T(128)}, f32[16,4,3,4096]{3,2,1,0:T(4,128)}, ...), condition=%wide.region_1.2_spmd, body=%wide.region_0.1_spmd.sunk | while | flops 57704448 | bytes 2826645 | solution.py:88
  60.1 1.1 fusion.84
  68.7 1.1 fusion.84
  129.1 1.1 fusion.84
  146.3 1.1 fusion.84
  184.4 4.2 multiply_reduce_fusion
  188.6 67.7 %all-gather.3.cloned.1.call-done = f32[128,2,4096]{2,1,0:T(2,128)} async-done(((f32[4,2,4096]{2,1,0:T(2,128)}), f32[128,2,4096]{2,1,0:T(2,128)}) %all-gather.3.cloned.1.call-update) | async-done | bytes 4194320 | tf_op jit(solution)/shard_map/all_gather | solution.py:26
  256.9 22.4 %copy.26 = f32[4,4,2,4096]{2,1,0,3:T(4,128)} copy(f32[4,4,2,4096]{3,1,0,2:T(4,128)S(1)} %pad_maximum_fusion) | data formatting | bytes 1048576
  279.4 38.1 %reshape.34 = f32[4096,32]{1,0:T(8,128)} reshape(f32[4096,4,4,2]{3,2,1,0:T(4,128)} %bitcast.147) | data formatting | bytes 1048576
  317.5 145.7 %reduce-scatter.4.cloned.1.call-done = f32[128,32]{1,0:T(8,128)} async-done(((f32[4096,32]{1,0:T(8,128)}), f32[128,32]{1,0:T(8,128)}) %reduce-scatter.4.cloned.1.call-update) | async-done | bytes 16400
  463.1 2.1 reshape.35
  465.2 1.2 copy.27
  (233 shorter events, 138.6 us)
Async XLA Ops:
  6.5 249.7 %all-gather.3.cloned.1.call-start = ((), (), s32[]{:S(2)}) async-start(), calls=%async_computation.1 | async-start | bytes 4325376 | tf_op jit(solution)/shard_map/all_gather | solution.py:26
  7.4 3.1 collective-permute-start
  9.2 4.8 %collective-permute-start.1 = (bf16[3,1,2,4096]{3,2,1,0:T(2,128)(2,1)S(1)}, bf16[3,1,2,4096]{3,2,1,0:T(2,128)(2,1)S(1)}, u32[]{:S(2)}, u32[]{:S(2)}) collective-permute-start(bf16[3,1,2,4096]{3,2,1,0:T(2,128)(2,1)S(1)} %get-tuple-element.167), channel_id=1, source_target_pairs={{8,0},{16,8},{24,16},{32,24},{40,32},{48,40},{56,48},{64,56},{72,6... | collective-permute-start | bytes 147464 | tf_op jit(solution)/shard_map/ppermute | solution.py:17
  15.9 17.9 %collective-permute-start.2 = (bf16[3,10,1,4096]{3,2,1,0:T(2,128)(2,1)}, bf16[3,10,1,4096]{3,2,1,0:T(2,128)(2,1)S(1)}, u32[]{:S(2)}, u32[]{:S(2)}) collective-permute-start(bf16[3,10,1,4096]{3,2,1,0:T(2,128)(2,1)} %get-tuple-element.165), channel_id=1, source_target_pairs={{0,1},{1,2},{2,3},{3,4},{4,5},{5,6},{6,7},{8,9},{9,10},{10,11},{11... | collective-permute-start | bytes 737288 | tf_op jit(solution)/shard_map/ppermute | solution.py:15
  19.4 16.0 %collective-permute-start.3 = (bf16[3,10,1,4096]{3,2,1,0:T(2,128)(2,1)S(1)}, bf16[3,10,1,4096]{3,2,1,0:T(2,128)(2,1)S(1)}, u32[]{:S(2)}, u32[]{:S(2)}) collective-permute-start(bf16[3,10,1,4096]{3,2,1,0:T(2,128)(2,1)S(1)} %get-tuple-element.166), channel_id=1, source_target_pairs={{1,0},{2,1},{3,2},{4,3},{5,4},{6,5},{7,6},{9,8},{10,9},{11,10},{12... | collective-permute-start | bytes 737288 | tf_op jit(solution)/shard_map/ppermute | solution.py:17
  42.4 2.5 copy-start
  183.9 279.2 %reduce-scatter.4.cloned.1.call-start = ((), (), s32[]{:S(2)}) async-start(), calls=%async_computation.2 | async-start | bytes 2162688
Sparse Core Ops, SparseCore 0:
  184.0 72.1 all-gather.2
  317.6 145.4 reduce-scatter.3
where the time goes:
time: 477 us; the launch traced here: 473 us
  waiting for transfers between devices  225 us (47%)
  matrix products  119 us (25%)
  local copies, waits for them, and re-layouts  73.2 us (15%)
  other arithmetic  28.8 us (6%)
  between operations  13.6 us (3%)
  starting transfers between devices  12.7 us (3%)
    unnamed x3, waiting for transfers between devices  146 us
    all_gather x1, waiting for transfers between devices, entering(): gathered = lax.all_gather(part, axis)  67.7 us
    unnamed x8, local copies, waits for them, and re-layouts  65.1 us
    dot_general x64, matrix products, shade_samples(): jnp.dot(color_table[energy].astype(jnp.bfloat16), hat_weights, preferred_...  48.4 us
    dot_general x16, matrix products, shade_samples(): grad_x = jnp.dot(material_weight, slope_x, precision=highest)  18.2 us
    dot_general x16, matrix products, shade_samples(): atten = jnp.dot(material_weight, middle, precision=highest)  17.8 us
    dot_general x16, matrix products, shade_samples(): grad_y = jnp.dot(material_weight, slope_y, precision=highest)  17.6 us
    dot_general x16, matrix products, shade_samples(): grad_z = jnp.dot(material_weight, slope_z, precision=highest)  17.4 us
  transfers between devices with their start and end apart: 6, of which 5 were waited for; matrix products, arithmetic and copies ran while one was open for 1% of the time, Pallas kernels for 0%

commit v1 on v0

v1 whole, which is shorter than its diff:
```python
import functools

import jax
import jax.numpy as jnp
from jax import lax
from jax.experimental import pallas as pl
from jax.experimental.pallas import tpu as pltpu
from jax.sharding import PartitionSpec as P

LANES = 128
ROWS = 8


def shifted(axis, part, step):
    count = lax.axis_size(axis)
    pairs = [(i, i + step) for i in range(count) if 0 <= i + step < count]
    return lax.ppermute(part, axis, pairs)


def render(depth_total, weight, table, cells, above, below, front, back, out, field, slope_x):
    mats, planes, lines, blocks, _ = cells.shape
    energies = weight.shape[0]
    lane = lax.broadcasted_iota(jnp.int32, (blocks, LANES), 1)
    block = lax.broadcasted_iota(jnp.int32, (blocks, LANES), 0)
    zero = jnp.zeros((blocks, LANES), jnp.float32)

    def widen(plane, _):
        for m in range(mats):
            field[m, plane + 1, 0] = above[m, plane].astype(jnp.float32)
            field[m, plane + 1, lines + 1] = below[m, plane].astype(jnp.float32)
            for y in range(lines):
                here = cells[m, plane, y].astype(jnp.float32)
                field[m, plane + 1, y + 1] = here
                before = jnp.where(block == 0, zero, pltpu.roll(here, 1, 0))
                after = jnp.where(block == blocks - 1, zero, pltpu.roll(here, blocks - 1, 0))
                left = pltpu.roll(jnp.where(lane == LANES - 1, before, here), 1, 1)
                right = pltpu.roll(jnp.where(lane == 0, after, here), LANES - 1, 1)
                slope_x[m, plane, y] = (right - left) * 0.5
        return 0

    lax.fori_loop(0, planes, widen, 0)
    for m in range(mats):
        for y in range(lines):
            field[m, 0, y + 1] = front[m, y].astype(jnp.float32)
            field[m, planes + 1, y + 1] = back[m, y].astype(jnp.float32)

    groups = blocks // ROWS
    kinds = 4 * energies * lines

    def chunk(step, _):
        y, group = step // groups, step % groups
        rows = pl.ds(pl.multiple_of(group * ROWS, ROWS), ROWS)
        light = [[jnp.zeros((ROWS, LANES), jnp.float32) for _ in range(4)] for _ in range(energies)]
        keep = [jnp.ones((ROWS, LANES), jnp.float32) for _ in range(energies)]
        for plane in range(planes):
            middle = [field[m, plane + 1, y + 1, rows] for m in range(mats)]
            dz = [(field[m, plane + 2, y + 1, rows] - field[m, plane, y + 1, rows]) * 0.5 for m in range(mats)]
            dy = [(field[m, plane + 1, y + 2, rows] - field[m, plane + 1, y, rows]) * 0.5 for m in range(mats)]
            dx = [slope_x[m, plane, y, rows] for m in range(mats)]
            for e in range(energies):
                mix = lambda parts: sum(weight[e, m] * parts[m] for m in range(1, mats)) + weight[e, 0] * parts[0]
                grad_z, grad_y, grad_x = mix(dz), mix(dy), mix(dx)
                slope_sq = grad_z * grad_z + grad_y * grad_y + grad_x * grad_x
                root = lax.rsqrt(slope_sq + 1.0)
                shading = 0.3 + 0.7 * jnp.abs(0.8 * grad_z + 0.48 * grad_y + 0.36 * grad_x) * root
                gate = slope_sq * root * root
                level = 255.0 * (1.0 - jnp.exp(-0.5 * mix(middle)))
                bin_ = level.astype(jnp.int32)
                over = level - bin_.astype(jnp.float32)
                first = (1.0 - over).astype(jnp.bfloat16).astype(jnp.float32)
                second = over.astype(jnp.bfloat16).astype(jnp.float32)
                high = bin_ >= LANES
                spot = bin_ & (LANES - 1)

                def look(row):
                    pick = lambda r: jnp.take_along_axis(
                        jnp.broadcast_to(table[r : r + 1, :], (ROWS, LANES)), spot, axis=1, mode="promise_in_bounds"
                    )
                    return jnp.where(high, pick(row + 1), pick(row))

                here, next_ = look(4 * e), look(4 * e + 2)
                level_of = lambda word, c: (lax.shift_right_logical(word, 8 * c) & 255).astype(jnp.float32)
                hue = [first * level_of(here, c) + second * level_of(next_, c) for c in range(4)]
                opacity = hue[3] * (gate * (6.0 / (255.0 * depth_total)))
                taken = keep[e] * opacity
                keep[e] = keep[e] - taken
                lit = taken * shading
                for c in range(3):
                    light[e][c] = light[e][c] + lit * hue[c]
                light[e][3] = light[e][3] + taken
        base = group * (ROWS * kinds) + y
        for e in range(energies):
            for c in range(4):
                value = light[e][c] * (1.0 / 255.0) if c < 3 else light[e][c]
                out[pl.ds(base + (c * energies + e) * lines, ROWS, stride=kinds), :] = value
        return 0

    lax.fori_loop(0, lines * groups, chunk, 0)


def composite(parts, out):
    bricks, kinds, _ = parts.shape
    energies, channels, lines, _ = out.shape
    per = kinds // channels

    def one(brick, state):
        keep, total = state
        new = [total[c] + keep * parts[brick, c * per : (c + 1) * per, :] for c in range(channels)]
        return keep * (1.0 - parts[brick, (channels - 1) * per :, :]), tuple(new)

    zero = jnp.zeros((per, LANES), jnp.float32)
    _, total = lax.fori_loop(0, bricks, one, (zero + 1.0, (zero,) * channels))
    for c in range(channels):
        for e in range(energies):
            out[e, c] = total[c][e * lines : (e + 1) * lines, :]


def packed_table(color_table):
    energies, channels, bins = color_table.shape
    word = color_table[:, 0]
    for c in range(1, channels):
        word = word | (color_table[:, c] << (8 * c))
    after = jnp.concatenate([word[:, 1:], jnp.zeros_like(word[:, :1])], axis=1)
    return jnp.concatenate([word, after], axis=1).reshape(energies * 2 * bins // LANES, LANES)


def body(density, material_weight, color_table):
    mats, planes, lines, columns = density.shape
    energies = material_weight.shape[0]
    blocks = columns // LANES
    depth = lax.axis_size("depth")
    cells = density.reshape(mats, planes, lines, blocks, LANES)
    above = shifted("tile", cells[:, :, lines - 1], 1)
    below = shifted("tile", cells[:, :, 0], -1)
    front = shifted("depth", cells[:, planes - 1], 1)
    back = shifted("depth", cells[:, 0], -1)
    kinds = 4 * energies * lines
    vmem = pl.BlockSpec(memory_space=pltpu.VMEM)
    parts = pl.pallas_call(
        functools.partial(render, planes * depth),
        out_shape=jax.ShapeDtypeStruct((blocks * kinds, LANES), jnp.float32),
        in_specs=[pl.BlockSpec(memory_space=pltpu.SMEM)] + [vmem] * 6,
        out_specs=vmem,
        scratch_shapes=[
            pltpu.VMEM((mats, planes + 2, lines + 2, blocks, LANES), jnp.float32),
            pltpu.VMEM((mats, planes, lines, blocks, LANES), jnp.float32),
        ],
        compiler_params=pltpu.CompilerParams(vmem_limit_bytes=32 * 2**20),
        name="render",
    )(material_weight, packed_table(color_table), cells, above, below, front, back)
    parts = lax.all_to_all(parts.reshape(blocks, kinds, LANES), "depth", 0, 0, tiled=True)
    return pl.pallas_call(
        composite,
        out_shape=jax.ShapeDtypeStruct((energies, 4, lines, columns // depth), jnp.float32),
        in_specs=[vmem],
        out_specs=vmem,
        name="composite",
    )(parts)


def solution(mesh):
    return jax.shard_map(
        body,
        mesh=mesh,
        in_specs=(P(None, "depth", "tile", None), P(), P()),
        out_specs=P(None, None, "tile", "depth"),
        check_vma=False,
    )
```

time: 477 us -> 58.4 us (0.12)
  the two profiles are of different devices: /device:TPU:4 before, /device:TPU:24 now
where the time goes in v1:
time: 58.4 us; the launch traced here: 58.1 us
  blocking collectives  27.3 us (47%)
  starting transfers between devices  10.8 us (18%)
  waiting for transfers between devices  10.8 us (18%)
  Pallas kernels  7.32 us (13%)
  local copies, waits for them, and re-layouts  1.56 us (3%)
    all_to_all x1, blocking collectives, body(): lax.all_to_all(parts.reshape(blocks, kinds, LANES), 'depth', 0, 0, tiled=...  27.3 us
    ppermute x4, waiting for transfers between devices, shifted(): return lax.ppermute(part, axis, pairs)  10.8 us
    ppermute x4, starting transfers between devices, shifted(): return lax.ppermute(part, axis, pairs)  10.8 us
    pallas_call x1, Pallas kernels, body(): pl.pallas_call(functools.partial(render, planes * depth), out_shape=jax.S...  5.5 us
    pallas_call x1, Pallas kernels, body(): pl.pallas_call(composite, out_shape=jax.ShapeDtypeStruct((energies, 4, li...  1.82 us
    reshape x1, local copies, waits for them, and re-layouts, body(): cells = density.reshape(mats, planes, lines, blocks, LANES)  1.29 us
  transfers between devices with their start and end apart: 4, of which 2 were waited for; matrix products, arithmetic and copies ran while one was open for 0% of the time, Pallas kernels for 0%

profile of v1, /device:TPU:24, one launch (start us, length us, event | category | flops | bytes accessed | tf_op | source)
XLA Modules:
  0.0 58.1 jit_solution(13622179557541211108)
XLA Ops:
  0.0 1.3 %reshape.21.cells = bf16[3,8,2,32,128]{4,3,2,1,0:T(8,128)(2,1)S(1)} reshape(bf16[3,8,2,4096]{3,2,1,0:T(2,128)(2,1)} %param.3) | data formatting | bytes 786432 | tf_op jit(solution)/shard_map/reshape | solution.py:132
  1.3 1.3 %collective-permute-start.3 = (bf16[3,2,32,128]{3,2,1,0:T(8,128)(2,1)S(1)}, bf16[3,2,32,128]{3,2,1,0:T(8,128)(2,1)S(1)}, u32[]{:S(2)}, u32[]{:S(2)}) collective-permute-start(bf16[3,2,32,128]{3,2,1,0:T(8,128)(2,1)S(1)} %get-tuple-element.5), channel_id=1, source_target_pairs={{8,0},{16,8},{24,16},{32,24},{40,32},{48,40},{56,48},{64,56},{72,6... | collective-permute-start | bytes 147464 | tf_op jit(solution)/shard_map/ppermute | solution.py:17
  2.6 3.0 %collective-permute-start.2 = (bf16[3,2,32,128]{3,2,1,0:T(8,128)(2,1)S(1)}, bf16[3,2,32,128]{3,2,1,0:T(8,128)(2,1)S(1)}, u32[]{:S(2)}, u32[]{:S(2)}) collective-permute-start(bf16[3,2,32,128]{3,2,1,0:T(8,128)(2,1)S(1)} %get-tuple-element.6), channel_id=1, source_target_pairs={{0,8},{8,16},{16,24},{24,32},{32,40},{40,48},{48,56},{56,64},{64,7... | collective-permute-start | bytes 147464 | tf_op jit(solution)/shard_map/ppermute | solution.py:17
  5.7 4.6 %collective-permute-start = (bf16[3,8,32,128]{3,2,0,1:T(8,128)(2,1)S(1)}, bf16[3,8,32,128]{3,2,0,1:T(8,128)(2,1)S(1)}, u32[]{:S(2)}, u32[]{:S(2)}) collective-permute-start(bf16[3,8,32,128]{3,2,0,1:T(8,128)(2,1)S(1)} %bitcast.20), channel_id=1, source_target_pairs={{0,1},{1,2},{2,3},{3,4},{4,5},{5,6},{6,7},{8,9},{9,10},{10,11},{11... | collective-permute-start | bytes 589832 | tf_op jit(solution)/shard_map/ppermute | solution.py:17
  10.3 0.0 copy-start.1
  10.3 1.9 %collective-permute-start.1 = (bf16[3,8,32,128]{3,2,0,1:T(8,128)(2,1)S(1)}, bf16[3,8,32,128]{3,2,0,1:T(8,128)(2,1)S(1)}, u32[]{:S(2)}, u32[]{:S(2)}) collective-permute-start(bf16[3,8,32,128]{3,2,0,1:T(8,128)(2,1)S(1)} %bitcast.21), channel_id=1, source_target_pairs={{1,0},{2,1},{3,2},{4,3},{5,4},{6,5},{7,6},{9,8},{10,9},{11,10},{12... | collective-permute-start | bytes 589832 | tf_op jit(solution)/shard_map/ppermute | solution.py:17
  12.3 0.1 pad.2.clone
  12.3 0.0 copy-done.1
  12.4 0.1 slice.36
  12.5 3.0 %collective-permute-done = bf16[3,8,32,128]{3,2,0,1:T(8,128)(2,1)S(1)} collective-permute-done((bf16[3,8,32,128]{3,2,0,1:T(8,128)(2,1)S(1)}, bf16[3,8,32,128]{3,2,0,1:T(8,128)(2,1)S(1)}, u32[]{:S(2)}, u32[]{:S(2)}) %collective-permute-start) | collective-permute-done | bytes 196640 | tf_op jit(solution)/shard_map/ppermute | solution.py:17
  15.5 0.0 copy-start
  15.5 7.9 %collective-permute-done.1 = bf16[3,8,32,128]{3,2,0,1:T(8,128)(2,1)S(1)} collective-permute-done((bf16[3,8,32,128]{3,2,0,1:T(8,128)(2,1)S(1)}, bf16[3,8,32,128]{3,2,0,1:T(8,128)(2,1)S(1)}, u32[]{:S(2)}, u32[]{:S(2)}) %collective-permute-start.1) | collective-permute-done | bytes 196640 | tf_op jit(solution)/shard_map/ppermute | solution.py:17
  23.4 0.0 collective-permute-done.3.back
  23.4 0.0 collective-permute-done.2.front
  23.4 0.0 copy-done
  23.4 5.5 %render.1 = f32[1024,128]{1,0:T(8,128)S(1)} custom-call(f32[4,3]{1,0:T(4,128)S(1)} %copy-done, s32[16,128]{1,0:T(8,128)S(1)} %reshape.18.table, bf16[3,8,2,32,128]{4,3,2,1,0:T(8,128)(2,1)S(1)} %reshape.21.cells, bf16[3,8,32,128]{3,2,1,0:T(8,128)(2,1)S(1)} %copy.10.above, bf16[3,8,32,128]{3,2,1,0:T(8,128)(2,1)S(1)} %copy.11.below, ...), custom_call_target="tpu_custom_call" | custom-call | tf_op jit(solution)/shard_map/render/pallas_call | solution.py:139
  28.9 27.3 %all_to_all.5.parts = f32[32,32,128]{2,1,0:T(8,128)} all-to-all(f32[32,32,128]{2,1,0:T(8,128)S(1)} %bitcast.19), channel_id=1, replica_groups=mesh['depth'=32,'tile'=8] {'depth'}, dimensions={0} | all-to-all | bytes 1048576 | tf_op jit(solution)/shard_map/all_to_all | solution.py:151
  56.2 1.8 %composite.1 = f32[4,4,2,128]{3,2,1,0:T(2,128)} custom-call(f32[32,32,128]{2,1,0:T(8,128)} %all_to_all.5.parts), custom_call_target="tpu_custom_call" | custom-call | tf_op jit(solution)/shard_map/composite/pallas_call | solution.py:152
  (10 shorter events, 0.1 us)
Async XLA Ops:
  1.3 22.0 %collective-permute-start.3 = (bf16[3,2,32,128]{3,2,1,0:T(8,128)(2,1)S(1)}, bf16[3,2,32,128]{3,2,1,0:T(8,128)(2,1)S(1)}, u32[]{:S(2)}, u32[]{:S(2)}) collective-permute-start(bf16[3,2,32,128]{3,2,1,0:T(8,128)(2,1)S(1)} %get-tuple-element.5), channel_id=1, source_target_pairs={{8,0},{16,8},{24,16},{32,24},{40,32},{48,40},{56,48},{64,56},{72,6... | collective-permute-start | bytes 147464 | tf_op jit(solution)/shard_map/ppermute | solution.py:17
  2.6 20.8 %collective-permute-start.2 = (bf16[3,2,32,128]{3,2,1,0:T(8,128)(2,1)S(1)}, bf16[3,2,32,128]{3,2,1,0:T(8,128)(2,1)S(1)}, u32[]{:S(2)}, u32[]{:S(2)}) collective-permute-start(bf16[3,2,32,128]{3,2,1,0:T(8,128)(2,1)S(1)} %get-tuple-element.6), channel_id=1, source_target_pairs={{0,8},{8,16},{16,24},{24,32},{32,40},{40,48},{48,56},{56,64},{64,7... | collective-permute-start | bytes 147464 | tf_op jit(solution)/shard_map/ppermute | solution.py:17
  5.7 9.7 %collective-permute-start = (bf16[3,8,32,128]{3,2,0,1:T(8,128)(2,1)S(1)}, bf16[3,8,32,128]{3,2,0,1:T(8,128)(2,1)S(1)}, u32[]{:S(2)}, u32[]{:S(2)}) collective-permute-start(bf16[3,8,32,128]{3,2,0,1:T(8,128)(2,1)S(1)} %bitcast.20), channel_id=1, source_target_pairs={{0,1},{1,2},{2,3},{3,4},{4,5},{5,6},{6,7},{8,9},{9,10},{10,11},{11... | collective-permute-start | bytes 589832 | tf_op jit(solution)/shard_map/ppermute | solution.py:17
  10.3 2.0 %copy-start.1 = (s32[4,4,256]{2,1,0:T(4,128)S(1)}, s32[4,4,256]{2,1,0:T(4,128)}, u32[]{:S(2)}) copy-start(s32[4,4,256]{2,1,0:T(4,128)} %param.5) | copy-start | bytes 49156
  10.3 13.0 %collective-permute-start.1 = (bf16[3,8,32,128]{3,2,0,1:T(8,128)(2,1)S(1)}, bf16[3,8,32,128]{3,2,0,1:T(8,128)(2,1)S(1)}, u32[]{:S(2)}, u32[]{:S(2)}) collective-permute-start(bf16[3,8,32,128]{3,2,0,1:T(8,128)(2,1)S(1)} %bitcast.21), channel_id=1, source_target_pairs={{1,0},{2,1},{3,2},{4,3},{5,4},{6,5},{7,6},{9,8},{10,9},{11,10},{12... | collective-permute-start | bytes 589832 | tf_op jit(solution)/shard_map/ppermute | solution.py:17
  15.5 7.9 %copy-start = (f32[4,3]{1,0:T(4,128)S(1)}, f32[4,3]{1,0:T(4,128)}, u32[]{:S(2)}) copy-start(f32[4,3]{1,0:T(4,128)} %weight.1) | copy-start | bytes 148

commit v2 on v1

--- a/solution.py
+++ b/solution.py
@@ -11,23 +11,34 @@
 ROWS = 8
 
 
-def shifted(axis, part, step):
-    count = lax.axis_size(axis)
-    pairs = [(i, i + step) for i in range(count) if 0 <= i + step < count]
-    return lax.ppermute(part, axis, pairs)
-
-
-def render(depth_total, weight, table, cells, above, below, front, back, out, field, slope_x):
+def facing(cells, axis, dim):
+    count, last = lax.axis_size(axis), cells.shape[dim] - 1
+    odd = lax.axis_index(axis) % 2
+    pick = lambda at: lax.dynamic_index_in_dim(cells, at, dim, keepdims=False)
+    low = [(i, i + 1) for i in range(0, count - 1, 2)]
+    high = [(i, i + 1) for i in range(1, count - 1, 2)]
+    both = lambda pairs: pairs + [(j, i) for i, j in pairs]
+    return (
+        lax.ppermute(pick(last * (1 - odd)), axis, both(low)),
+        lax.ppermute(pick(last * odd), axis, both(high)),
+    )
+
+
+def render(depth_total, weight, table, cells, tile_a, tile_b, depth_a, depth_b, kept, sent, field, slope_x, image):
     mats, planes, lines, blocks, _ = cells.shape
     energies = weight.shape[0]
     lane = lax.broadcasted_iota(jnp.int32, (blocks, LANES), 1)
     block = lax.broadcasted_iota(jnp.int32, (blocks, LANES), 0)
     zero = jnp.zeros((blocks, LANES), jnp.float32)
 
+    tile_odd, depth_odd = lax.axis_index("tile") % 2, lax.axis_index("depth") % 2
+    beside_a = (lines + 1) * (1 - tile_odd)
+    beside_b = (lines + 1) * tile_odd
+
     def widen(plane, _):
         for m in range(mats):
-            field[m, plane + 1, 0] = above[m, plane].astype(jnp.float32)
-            field[m, plane + 1, lines + 1] = below[m, plane].astype(jnp.float32)
+            field[m, plane + 1, beside_a] = tile_a[m, plane].astype(jnp.float32)
+            field[m, plane + 1, beside_b] = tile_b[m, plane].astype(jnp.float32)
             for y in range(lines):
                 here = cells[m, plane, y].astype(jnp.float32)
                 field[m, plane + 1, y + 1] = here
@@ -41,8 +52,8 @@
     lax.fori_loop(0, planes, widen, 0)
     for m in range(mats):
         for y in range(lines):
-            field[m, 0, y + 1] = front[m, y].astype(jnp.float32)
-            field[m, planes + 1, y + 1] = back[m, y].astype(jnp.float32)
+            field[m, (planes + 1) * (1 - depth_odd), y + 1] = depth_a[m, y].astype(jnp.float32)
+            field[m, (planes + 1) * depth_odd, y + 1] = depth_b[m, y].astype(jnp.float32)
 
     groups = blocks // ROWS
     kinds = 4 * energies * lines
@@ -92,10 +103,36 @@
         for e in range(energies):
             for c in range(4):
                 value = light[e][c] * (1.0 / 255.0) if c < 3 else light[e][c]
-                out[pl.ds(base + (c * energies + e) * lines, ROWS, stride=kinds), :] = value
+                image[pl.ds(base + (c * energies + e) * lines, ROWS, stride=kinds), :] = value
         return 0
 
     lax.fori_loop(0, lines * groups, chunk, 0)
+
+    def part(pair, _):
+        for target, parity in ((kept, depth_odd), (sent, 1 - depth_odd)):
+            start = pl.multiple_of((2 * pair + parity) * kinds, kinds)
+            target[pair] = image[pl.ds(start, kinds), :]
+        return 0
+
+    lax.fori_loop(0, blocks // 2, part, 0)
+
+
+def over(front, back, per):
+    clear = 1.0 - front[-per:, :]
+    return [front[i : i + per, :] + clear * back[i : i + per, :] for i in range(0, front.shape[0], per)]
+
+
+def join(per, mine, other, out):
+    odd = lax.axis_index("depth") % 2
+
+    def one(pair, _):
+        a, b = mine[pair], other[pair]
+        front, back = jnp.where(odd == 0, a, b), jnp.where(odd == 0, b, a)
+        for i, value in enumerate(over(front, back, per)):
+            out[pair, i * per : (i + 1) * per, :] = value
+        return 0
+
+    lax.fori_loop(0, mine.shape[0], one, 0)
 
 
 def composite(parts, out):
@@ -103,13 +140,12 @@
     energies, channels, lines, _ = out.shape
     per = kinds // channels
 
-    def one(brick, state):
-        keep, total = state
-        new = [total[c] + keep * parts[brick, c * per : (c + 1) * per, :] for c in range(channels)]
-        return keep * (1.0 - parts[brick, (channels - 1) * per :, :]), tuple(new)
-
-    zero = jnp.zeros((per, LANES), jnp.float32)
-    _, total = lax.fori_loop(0, bricks, one, (zero + 1.0, (zero,) * channels))
+    keep = jnp.ones((per, LANES), jnp.float32)
+    total = [jnp.zeros((per, LANES), jnp.float32) for _ in range(channels)]
+    for brick in range(bricks):
+        part = [parts[brick, c * per : (c + 1) * per, :] for c in range(channels)]
+        total = [total[c] + keep * part[c] for c in range(channels)]
+        keep = keep * (1.0 - part[channels - 1])
     for c in range(channels):
         for e in range(energies):
             out[e, c] = total[c][e * lines : (e + 1) * lines, :]
@@ -130,25 +166,31 @@
     blocks = columns // LANES
     depth = lax.axis_size("depth")
     cells = density.reshape(mats, planes, lines, blocks, LANES)
-    above = shifted("tile", cells[:, :, lines - 1], 1)
-    below = shifted("tile", cells[:, :, 0], -1)
-    front = shifted("depth", cells[:, planes - 1], 1)
-    back = shifted("depth", cells[:, 0], -1)
+    tile_a, tile_b = facing(cells, "tile", 2)
+    depth_a, depth_b = facing(cells, "depth", 1)
     kinds = 4 * energies * lines
+    pairs = blocks // 2
     vmem = pl.BlockSpec(memory_space=pltpu.VMEM)
-    parts = pl.pallas_call(
+    half = jax.ShapeDtypeStruct((pairs, kinds, LANES), jnp.float32)
+    kept, sent = pl.pallas_call(
         functools.partial(render, planes * depth),
-        out_shape=jax.ShapeDtypeStruct((blocks * kinds, LANES), jnp.float32),
+        out_shape=(half, half),
         in_specs=[pl.BlockSpec(memory_space=pltpu.SMEM)] + [vmem] * 6,
-        out_specs=vmem,
+        out_specs=(vmem, vmem),
         scratch_shapes=[
             pltpu.VMEM((mats, planes + 2, lines + 2, blocks, LANES), jnp.float32),
             pltpu.VMEM((mats, planes, lines, blocks, LANES), jnp.float32),
+            pltpu.VMEM((blocks * kinds, LANES), jnp.float32),
         ],
         compiler_params=pltpu.CompilerParams(vmem_limit_bytes=32 * 2**20),
         name="render",
-    )(material_weight, packed_table(color_table), cells, above, below, front, back)
-    parts = lax.all_to_all(parts.reshape(blocks, kinds, LANES), "depth", 0, 0, tiled=True)
+    )(material_weight, packed_table(color_table), cells, tile_a, tile_b, depth_a, depth_b)
+    other = lax.ppermute(sent, "depth", [(i, i ^ 1) for i in range(depth)])
+    joined = pl.pallas_call(
+        functools.partial(join, energies * lines), out_shape=half, in_specs=[vmem, vmem], out_specs=vmem, name="join"
+    )(kept, other)
+    same_core = [[2 * i + c for i in range(depth // 2)] for c in range(2)]
+    parts = lax.all_to_all(joined, "depth", 0, 0, axis_index_groups=same_core, tiled=True)
     return pl.pallas_call(
         composite,
         out_shape=jax.ShapeDtypeStruct((energies, 4, lines, columns // depth), jnp.float32),

time: 58.4 us -> 49.3 us (0.84)
  the two profiles are of different devices: /device:TPU:24 before, /device:TPU:4 now
where the time goes in v2:
time: 49.3 us; the launch traced here: 48.7 us
  blocking collectives  18.9 us (38%)
  starting transfers between devices  9.18 us (19%)
  Pallas kernels  9.08 us (18%)
  waiting for transfers between devices  8.52 us (17%)
  local copies, waits for them, and re-layouts  2.89 us (6%)
    all_to_all x1, blocking collectives, body(): lax.all_to_all(joined, 'depth', 0, 0, axis_index_groups=same_core, tiled=...  18.9 us
    ppermute x2, waiting for transfers between devices, facing(): lax.ppermute(pick(last * odd), axis, both(high))  6.98 us
    pallas_call x1, Pallas kernels, body(): pl.pallas_call(functools.partial(render, planes * depth), out_shape=(half...  5.64 us
    ppermute x2, starting transfers between devices, facing(): lax.ppermute(pick(last * odd), axis, both(high))  5.53 us
    ppermute x2, starting transfers between devices, facing(): lax.ppermute(pick(last * (1 - odd)), axis, both(low))  3.65 us
    pallas_call x1, Pallas kernels, body(): pl.pallas_call(functools.partial(join, energies * lines), out_shape=half,...  1.86 us
    pallas_call x1, Pallas kernels, body(): pl.pallas_call(composite, out_shape=jax.ShapeDtypeStruct((energies, 4, li...  1.58 us
    ppermute x1, waiting for transfers between devices, body(): other = lax.ppermute(sent, 'depth', [(i, i ^ 1) for i in range(depth)])  1.53 us
  transfers between devices with their start and end apart: 5, of which 2 were waited for; matrix products, arithmetic and copies ran while one was open for 0% of the time, Pallas kernels for 0%

profile of v2, /device:TPU:4, one launch (start us, length us, event | category | flops | bytes accessed | tf_op | source)
XLA Modules:
  0.0 48.7 jit_solution(5886431007173607568)
XLA Ops:
  0.0 1.3 %reshape.16.cells = bf16[3,8,2,32,128]{4,3,2,1,0:T(8,128)(2,1)S(1)} reshape(bf16[3,8,2,4096]{3,2,1,0:T(2,128)(2,1)} %param.3) | data formatting | bytes 786432 | tf_op jit(solution)/shard_map/reshape | solution.py:168
  1.3 0.7 %collective-permute-start.3 = (bf16[3,2,32,128]{3,2,1,0:T(8,128)(2,1)S(1)}, bf16[3,2,32,128]{3,2,1,0:T(8,128)(2,1)S(1)}, u32[]{:S(2)}, u32[]{:S(2)}) collective-permute-start(bf16[3,2,32,128]{3,2,1,0:T(8,128)(2,1)S(1)} %get-tuple-element.9), channel_id=1, source_target_pairs={{8,16},{24,32},{40,48},{56,64},{72,80},{88,96},{104,112},{120,128}... | collective-permute-start | bytes 147464 | tf_op jit(solution)/shard_map/ppermute | solution.py:23
  2.0 3.4 %collective-permute-start.2 = (bf16[3,2,32,128]{3,2,1,0:T(8,128)(2,1)S(1)}, bf16[3,2,32,128]{3,2,1,0:T(8,128)(2,1)S(1)}, u32[]{:S(2)}, u32[]{:S(2)}) collective-permute-start(bf16[3,2,32,128]{3,2,1,0:T(8,128)(2,1)S(1)} %get-tuple-element.10), channel_id=1, source_target_pairs={{0,8},{16,24},{32,40},{48,56},{64,72},{80,88},{96,104},{112,120},{... | collective-permute-start | bytes 147464 | tf_op jit(solution)/shard_map/ppermute | solution.py:22
  5.4 0.0 copy-start.3
  5.4 4.9 %collective-permute-start.1 = (bf16[3,8,32,128]{3,2,1,0:T(8,128)(2,1)S(1)}, bf16[3,8,32,128]{3,2,1,0:T(8,128)(2,1)S(1)}, u32[]{:S(2)}, u32[]{:S(2)}) collective-permute-start(bf16[3,8,32,128]{3,2,1,0:T(8,128)(2,1)S(1)} %get-tuple-element.11), channel_id=1, source_target_pairs={{1,2},{3,4},{5,6},{2,1},{4,3},{6,5},{9,10},{11,12},{13,14},{10,9},... | collective-permute-start | bytes 589832 | tf_op jit(solution)/shard_map/ppermute | solution.py:23
  10.3 0.3 collective-permute-start
  10.6 0.1 pad.2.clone
  10.6 0.0 copy-done.3
  10.7 0.1 slice.20
  10.7 0.0 copy-start.1
  10.8 0.0 collective-permute-done.3.depth_b
  10.8 0.0 collective-permute-done.2.depth_a
  10.8 7.0 %collective-permute-done.1.tile_b = bf16[3,8,32,128]{3,2,1,0:T(8,128)(2,1)S(1)} collective-permute-done((bf16[3,8,32,128]{3,2,1,0:T(8,128)(2,1)S(1)}, bf16[3,8,32,128]{3,2,1,0:T(8,128)(2,1)S(1)}, u32[]{:S(2)}, u32[]{:S(2)}) %collective-permute-start.1) | collective-permute-done | bytes 196640 | tf_op jit(solution)/shard_map/ppermute | solution.py:23
  17.8 0.0 collective-permute-done.tile_a
  17.8 0.0 copy-done.1
  17.8 5.6 %render.1 = (f32[16,32,128]{2,1,0:T(8,128)S(1)}, f32[16,32,128]{2,1,0:T(8,128)S(1)}) custom-call(f32[4,3]{1,0:T(4,128)S(1)} %copy-done.1, s32[16,128]{1,0:T(8,128)S(1)} %reshape.15.table, bf16[3,8,2,32,128]{4,3,2,1,0:T(8,128)(2,1)S(1)} %reshape.16.cells, bf16[3,8,32,128]{3,2,1,0:T(8,128)(2,1)S(1)} %collective-permute-done.tile_a, ...), custom_call_target="tpu_custom_call" | custom-call | tf_op jit(solution)/shard_map/render/pallas_call | solution.py:175
  23.4 0.0 copy-start
  23.4 0.7 %copy-done = f32[16,32,128]{2,1,0:T(8,128)} copy-done((f32[16,32,128]{2,1,0:T(8,128)}, f32[16,32,128]{2,1,0:T(8,128)S(1)}, u32[]{:S(2)}) %copy-start) | copy-done | bytes 262168
  24.1 0.0 collective-permute-start.4
  24.1 1.5 %collective-permute-done.4.other = f32[16,32,128]{2,1,0:T(8,128)S(1)} collective-permute-done((f32[16,32,128]{2,1,0:T(8,128)S(1)}, f32[16,32,128]{2,1,0:T(8,128)S(1)}, u32[]{:S(2)}, u32[]{:S(2)}) %collective-permute-start.4) | collective-permute-done | bytes 262176 | tf_op jit(solution)/shard_map/ppermute | solution.py:188
  25.7 0.7 %copy-done.2 = f32[16,32,128]{2,1,0:T(8,128)} copy-done((f32[16,32,128]{2,1,0:T(8,128)}, f32[16,32,128]{2,1,0:T(8,128)S(1)}, u32[]{:S(2)}) %copy-start.2) | copy-done | bytes 262168
  26.4 1.9 %join.1 = f32[16,32,128]{2,1,0:T(8,128)} custom-call(f32[16,32,128]{2,1,0:T(8,128)} %copy-done, f32[16,32,128]{2,1,0:T(8,128)} %copy-done.2), custom_call_target="tpu_custom_call" | custom-call | tf_op jit(solution)/shard_map/join/pallas_call | solution.py:189
  28.2 18.9 %all_to_all.5.parts = f32[16,32,128]{2,1,0:T(8,128)} all-to-all(f32[16,32,128]{2,1,0:T(8,128)} %join.1), channel_id=1, replica_groups={{0,16,32,48,64,80,96,112,128,144,160,176,192,208,224,240},{8,24,40,56,7..., dimensions={0} | all-to-all | bytes 524288 | tf_op jit(solution)/shard_map/all_to_all | solution.py:193
  47.1 1.6 %composite.1 = f32[4,4,2,128]{3,2,1,0:T(2,128)} custom-call(f32[16,32,128]{2,1,0:T(8,128)} %all_to_all.5.parts), custom_call_target="tpu_custom_call" | custom-call | tf_op jit(solution)/shard_map/composite/pallas_call | solution.py:194
  (7 shorter events, 0.1 us)
Async XLA Ops:
  1.3 9.4 %collective-permute-start.3 = (bf16[3,2,32,128]{3,2,1,0:T(8,128)(2,1)S(1)}, bf16[3,2,32,128]{3,2,1,0:T(8,128)(2,1)S(1)}, u32[]{:S(2)}, u32[]{:S(2)}) collective-permute-start(bf16[3,2,32,128]{3,2,1,0:T(8,128)(2,1)S(1)} %get-tuple-element.9), channel_id=1, source_target_pairs={{8,16},{24,32},{40,48},{56,64},{72,80},{88,96},{104,112},{120,128}... | collective-permute-start | bytes 147464 | tf_op jit(solution)/shard_map/ppermute | solution.py:23
  2.0 8.8 %collective-permute-start.2 = (bf16[3,2,32,128]{3,2,1,0:T(8,128)(2,1)S(1)}, bf16[3,2,32,128]{3,2,1,0:T(8,128)(2,1)S(1)}, u32[]{:S(2)}, u32[]{:S(2)}) collective-permute-start(bf16[3,2,32,128]{3,2,1,0:T(8,128)(2,1)S(1)} %get-tuple-element.10), channel_id=1, source_target_pairs={{0,8},{16,24},{32,40},{48,56},{64,72},{80,88},{96,104},{112,120},{... | collective-permute-start | bytes 147464 | tf_op jit(solution)/shard_map/ppermute | solution.py:22
  5.4 5.3 %copy-start.3 = (s32[4,4,256]{2,1,0:T(4,128)S(1)}, s32[4,4,256]{2,1,0:T(4,128)}, u32[]{:S(2)}) copy-start(s32[4,4,256]{2,1,0:T(4,128)} %param.5) | copy-start | bytes 49156
  5.4 12.4 %collective-permute-start.1 = (bf16[3,8,32,128]{3,2,1,0:T(8,128)(2,1)S(1)}, bf16[3,8,32,128]{3,2,1,0:T(8,128)(2,1)S(1)}, u32[]{:S(2)}, u32[]{:S(2)}) collective-permute-start(bf16[3,8,32,128]{3,2,1,0:T(8,128)(2,1)S(1)} %get-tuple-element.11), channel_id=1, source_target_pairs={{1,2},{3,4},{5,6},{2,1},{4,3},{6,5},{9,10},{11,12},{13,14},{10,9},... | collective-permute-start | bytes 589832 | tf_op jit(solution)/shard_map/ppermute | solution.py:23
  10.3 7.5 %collective-permute-start = (bf16[3,8,32,128]{3,2,1,0:T(8,128)(2,1)S(1)}, bf16[3,8,32,128]{3,2,1,0:T(8,128)(2,1)S(1)}, u32[]{:S(2)}, u32[]{:S(2)}) collective-permute-start(bf16[3,8,32,128]{3,2,1,0:T(8,128)(2,1)S(1)} %get-tuple-element.12), channel_id=1, source_target_pairs={{0,1},{2,3},{4,5},{6,7},{1,0},{3,2},{5,4},{7,6},{8,9},{10,11},{12,... | collective-permute-start | bytes 589832 | tf_op jit(solution)/shard_map/ppermute | solution.py:22
  10.7 7.0 %copy-start.1 = (f32[4,3]{1,0:T(4,128)S(1)}, f32[4,3]{1,0:T(4,128)}, u32[]{:S(2)}) copy-start(f32[4,3]{1,0:T(4,128)} %weight.1) | copy-start | bytes 148
  23.4 0.7 %copy-start = (f32[16,32,128]{2,1,0:T(8,128)}, f32[16,32,128]{2,1,0:T(8,128)S(1)}, u32[]{:S(2)}) copy-start(f32[16,32,128]{2,1,0:T(8,128)S(1)} %get-tuple-element.7.mine) | copy-start | bytes 786436
  24.1 1.5 %collective-permute-start.4 = (f32[16,32,128]{2,1,0:T(8,128)S(1)}, f32[16,32,128]{2,1,0:T(8,128)S(1)}, u32[]{:S(2)}, u32[]{:S(2)}) collective-permute-start(f32[16,32,128]{2,1,0:T(8,128)S(1)} %get-tuple-element.8), channel_id=1, source_target_pairs={{0,8},{8,0},{16,24},{24,16},{32,40},{40,32},{48,56},{56,48},{64,72... | collective-permute-start | bytes 786440 | tf_op jit(solution)/shard_map/ppermute | solution.py:188
  25.6 0.7 %copy-start.2 = (f32[16,32,128]{2,1,0:T(8,128)}, f32[16,32,128]{2,1,0:T(8,128)S(1)}, u32[]{:S(2)}) copy-start(f32[16,32,128]{2,1,0:T(8,128)S(1)} %collective-permute-done.4.other) | copy-start | bytes 786436

commit v3 on v2

v3 whole, which is shorter than its diff:
```python
import functools

import jax
import jax.numpy as jnp
from jax import lax
from jax.experimental import pallas as pl
from jax.experimental.pallas import tpu as pltpu
from jax.sharding import PartitionSpec as P

LANES = 128
ROWS = 8


def facing(cells, axis, dim):
    count, last = lax.axis_size(axis), cells.shape[dim] - 1
    odd = lax.axis_index(axis) % 2
    pick = lambda at: lax.dynamic_index_in_dim(cells, at, dim, keepdims=False)
    low = [(i, i + 1) for i in range(0, count - 1, 2)]
    high = [(i, i + 1) for i in range(1, count - 1, 2)]
    both = lambda pairs: pairs + [(j, i) for i, j in pairs]
    return (
        lax.ppermute(pick(last * (1 - odd)), axis, both(low)),
        lax.ppermute(pick(last * odd), axis, both(high)),
    )


def mix(weights, parts):
    total = weights[0] * parts[0]
    for weight, part in zip(weights[1:], parts[1:]):
        total = total + weight * part
    return total


def lookup(depth_total, weight, table, cells, hues, field, slope_x):
    mats, planes, lines, blocks, _ = cells.shape
    energies = weight.shape[0]
    groups = blocks // ROWS
    lane = lax.broadcasted_iota(jnp.int32, (blocks, LANES), 1)
    block = lax.broadcasted_iota(jnp.int32, (blocks, LANES), 0)
    zero = jnp.zeros((blocks, LANES), jnp.float32)

    def widen(plane, _):
        for m in range(mats):
            for y in range(lines):
                here = cells[m, plane, y].astype(jnp.float32)
                field[m, plane, y] = here
                before = jnp.where(block == 0, zero, pltpu.roll(here, 1, 0))
                after = jnp.where(block == blocks - 1, zero, pltpu.roll(here, blocks - 1, 0))
                left = pltpu.roll(jnp.where(lane == LANES - 1, before, here), 1, 1)
                right = pltpu.roll(jnp.where(lane == 0, after, here), LANES - 1, 1)
                slope_x[m, plane, y] = right - left
        return 0

    lax.fori_loop(0, planes, widen, 0)

    def chunk(step, _):
        y, group = step // groups, step % groups
        rows = pl.ds(pl.multiple_of(group * ROWS, ROWS), ROWS)
        for plane in range(planes):
            middle = [field[m, plane, y, rows] for m in range(mats)]
            for e in range(energies):
                level = 255.0 * (1.0 - jnp.exp(-0.5 * mix([weight[e, m] for m in range(mats)], middle)))
                bin_ = level.astype(jnp.int32)
                past = level - bin_.astype(jnp.float32)
                first = (1.0 - past).astype(jnp.bfloat16).astype(jnp.float32)
                second = past.astype(jnp.bfloat16).astype(jnp.float32)
                high = bin_ >= LANES
                spot = bin_ & (LANES - 1)

                def look(row):
                    pick = lambda r: jnp.take_along_axis(
                        jnp.broadcast_to(table[r : r + 1, :], (ROWS, LANES)), spot, axis=1, mode="promise_in_bounds"
                    )
                    return jnp.where(high, pick(row + 1), pick(row))

                here, next_ = look(4 * e), look(4 * e + 2)
                level_of = lambda word, c: (lax.shift_right_logical(word, 8 * c) & 255).astype(jnp.float32)
                for c in range(4):
                    hue = first * level_of(here, c) + second * level_of(next_, c)
                    hues[plane, step, 4 * e + c] = hue if c < 3 else hue * (6.0 / (255.0 * depth_total))
        return 0

    lax.fori_loop(0, lines * groups, chunk, 0)


def shade(weight, hues, field, slope_x, depth_a, depth_b, tile_a, tile_b, kept, sent, image):
    mats, planes, lines, blocks, _ = field.shape
    energies = weight.shape[0]
    groups = blocks // ROWS
    kinds = 4 * energies * lines
    tile_odd, depth_odd = lax.axis_index("tile") % 2, lax.axis_index("depth") % 2
    wide = lambda ref, *at: ref[at].astype(jnp.float32)

    def chunk(group, _):
        rows = pl.ds(pl.multiple_of(group * ROWS, ROWS), ROWS)
        for y in range(lines):
            light = [[jnp.zeros((ROWS, LANES), jnp.float32) for _ in range(4)] for _ in range(energies)]
            keep = [jnp.ones((ROWS, LANES), jnp.float32) for _ in range(energies)]
            near, far = [], []
            for m in range(mats):
                a, b = depth_a[m, y, rows], depth_b[m, y, rows]
                near.append(jnp.where(depth_odd == 1, a, b))
                far.append(jnp.where(depth_odd == 1, b, a))
            for plane in range(planes):
                dx, dy, dz = [], [], []
                for m in range(mats):
                    before = near[m] if plane == 0 else field[m, plane - 1, y, rows]
                    after = far[m] if plane == planes - 1 else field[m, plane + 1, y, rows]
                    dz.append(after - before)
                    a, b = tile_a[m, plane, rows], tile_b[m, plane, rows]
                    above = jnp.where(tile_odd == 1, a, b) if y == 0 else field[m, plane, y - 1, rows]
                    below = jnp.where(tile_odd == 1, b, a) if y == lines - 1 else field[m, plane, y + 1, rows]
                    dy.append(below - above)
                    dx.append(slope_x[m, plane, y, rows])
                for e in range(energies):
                    half = [0.5 * weight[e, m] for m in range(mats)]
                    grad_z, grad_y, grad_x = mix(half, dz), mix(half, dy), mix(half, dx)
                    slope_sq = grad_z * grad_z + grad_y * grad_y + grad_x * grad_x
                    root = lax.rsqrt(slope_sq + 1.0)
                    shading = 0.3 + jnp.abs(0.56 * grad_z + 0.336 * grad_y + 0.252 * grad_x) * root
                    hue = [hues[plane, y * groups + group, 4 * e + c] for c in range(4)]
                    taken = keep[e] * (hue[3] * (slope_sq * (root * root)))
                    keep[e] = keep[e] - taken
                    lit = taken * shading
                    for c in range(3):
                        light[e][c] = light[e][c] + lit * hue[c]
                    light[e][3] = light[e][3] + taken
            base = group * (ROWS * kinds) + y
            for e in range(energies):
                for c in range(4):
                    value = light[e][c] * (1.0 / 255.0) if c < 3 else light[e][c]
                    image[pl.ds(base + (c * energies + e) * lines, ROWS, stride=kinds), :] = value
        return 0

    lax.fori_loop(0, groups, chunk, 0)

    def part(pair, _):
        for target, parity in ((kept, depth_odd), (sent, 1 - depth_odd)):
            start = pl.multiple_of((2 * pair + parity) * kinds, kinds)
            target[pair] = image[pl.ds(start, kinds), :]
        return 0

    lax.fori_loop(0, blocks // 2, part, 0)


def join(per, mine, other, out):
    odd = lax.axis_index("depth") % 2
    for pair in range(mine.shape[0]):
        a, b = mine[pair], other[pair]
        front, back = jnp.where(odd == 0, a, b), jnp.where(odd == 0, b, a)
        clear = 1.0 - front[-per:, :]
        for i in range(0, front.shape[0], per):
            out[pair, i : i + per, :] = front[i : i + per, :] + clear * back[i : i + per, :]


def composite(parts, out):
    bricks, kinds, _ = parts.shape
    energies, channels, lines, _ = out.shape
    per = kinds // channels

    keep = jnp.ones((per, LANES), jnp.float32)
    total = [jnp.zeros((per, LANES), jnp.float32) for _ in range(channels)]
    for brick in range(bricks):
        part = [parts[brick, c * per : (c + 1) * per, :] for c in range(channels)]
        total = [total[c] + keep * part[c] for c in range(channels)]
        keep = keep * (1.0 - part[channels - 1])
    for c in range(channels):
        for e in range(energies):
            out[e, c] = total[c][e * lines : (e + 1) * lines, :]


def packed_table(color_table):
    energies, channels, bins = color_table.shape
    word = color_table[:, 0]
    for c in range(1, channels):
        word = word | (color_table[:, c] << (8 * c))
    after = jnp.concatenate([word[:, 1:], jnp.zeros_like(word[:, :1])], axis=1)
    return jnp.concatenate([word, after], axis=1).reshape(energies * 2 * bins // LANES, LANES)


def limit(mib):
    return pltpu.CompilerParams(vmem_limit_bytes=mib * 2**20)


def body(density, material_weight, color_table):
    mats, planes, lines, columns = density.shape
    energies = material_weight.shape[0]
    blocks = columns // LANES
    depth = lax.axis_size("depth")
    kinds = 4 * energies * lines
    pairs = blocks // 2
    smem, vmem = pl.BlockSpec(memory_space=pltpu.SMEM), pl.BlockSpec(memory_space=pltpu.VMEM)
    real = lambda *shape: jax.ShapeDtypeStruct(shape, jnp.float32)

    cells = density.reshape(mats, planes, lines, blocks, LANES)
    depth_a, depth_b = facing(cells, "depth", 1)
    tile_a, tile_b = facing(cells, "tile", 2)
    hues, field, slope_x = pl.pallas_call(
        functools.partial(lookup, planes * depth),
        out_shape=(
            real(planes, lines * blocks // ROWS, 4 * energies, ROWS, LANES),
            real(*cells.shape),
            real(*cells.shape),
        ),
        in_specs=[smem, vmem, vmem],
        out_specs=(vmem, vmem, vmem),
        compiler_params=limit(8),
        cost_estimate=pl.CostEstimate(flops=4_000_000_000, bytes_accessed=8_000_000, transcendentals=300_000),
        name="lookup",
    )(material_weight, packed_table(color_table), cells)
    kept, sent = pl.pallas_call(
        shade,
        out_shape=(real(pairs, kinds, LANES),) * 2,
        in_specs=[smem] + [vmem] * 7,
        out_specs=(vmem, vmem),
        scratch_shapes=[pltpu.VMEM((blocks * kinds, LANES), jnp.float32)],
        compiler_params=limit(8),
        name="shade",
    )(material_weight, hues, field, slope_x, depth_a, depth_b, tile_a, tile_b)
    other = lax.ppermute(sent, "depth", [(i, i ^ 1) for i in range(depth)])
    joined = pl.pallas_call(
        functools.partial(join, energies * lines),
        out_shape=real(pairs, kinds, LANES),
        in_specs=[vmem, vmem],
        out_specs=vmem,
        compiler_params=limit(2),
        name="join",
    )(kept, other)
    same_core = [[2 * i + c for i in range(depth // 2)] for c in range(2)]
    parts = lax.all_to_all(joined, "depth", 0, 0, axis_index_groups=same_core, tiled=True)
    return pl.pallas_call(
        composite,
        out_shape=real(energies, 4, lines, columns // depth),
        in_specs=[vmem],
        out_specs=vmem,
        compiler_params=limit(2),
        name="composite",
    )(parts)


def solution(mesh):
    return jax.shard_map(
        body,
        mesh=mesh,
        in_specs=(P(None, "depth", "tile", None), P(), P()),
        out_specs=P(None, None, "tile", "depth"),
        check_vma=False,
    )
```

time: 49.3 us -> 41.8 us (0.85)
  waiting for transfers between devices: 8.52 us -> 2.95 us
  Pallas kernels: 9.08 us -> 7.27 us
  other arithmetic: 0.03 us -> 0.89 us
  local copies, waits for them, and re-layouts: 2.89 us -> 2.17 us
    ppermute x2, waiting for transfers between devices: 6.98 us -> 1.43 us  [facing(): lax.ppermute(pick(last * odd), axis, both(high))]
    pallas_call x3 -> x4, Pallas kernels: 9.08 us -> 7.27 us  [the longest x1 4 us: body(): pl.pallas_call(functools.partial(lookup, planes * depth), out_shape=(real...]
    or x1, other arithmetic: 0.02 us -> 0.88 us  [packed_table(): word = word | color_table[:, c] << 8 * c]
    unnamed x9 -> x3, local copies, waits for them, and re-layouts: 1.4 us -> 0.68 us
  transfers between devices with their start and end apart: 5 -> 5, of which waited for: 2 -> 2; matrix products, arithmetic and copies ran while one was open for 0% -> 3% of each run, Pallas kernels for 0% -> 10%
where the time goes in v3:
time: 41.8 us; the launch traced here: 41.3 us
  blocking collectives  18.6 us (44%)
  starting transfers between devices  9.27 us (22%)
  Pallas kernels  7.27 us (17%)
  waiting for transfers between devices  2.95 us (7%)
  local copies, waits for them, and re-layouts  2.17 us (5%)
  other arithmetic  0.89 us (2%)
    all_to_all x1, blocking collectives, body(): lax.all_to_all(joined, 'depth', 0, 0, axis_index_groups=same_core, tiled=...  18.6 us
    ppermute x2, starting transfers between devices, facing(): lax.ppermute(pick(last * odd), axis, both(high))  5.53 us
    pallas_call x1, Pallas kernels, body(): pl.pallas_call(functools.partial(lookup, planes * depth), out_shape=(real...  4 us
    ppermute x2, starting transfers between devices, facing(): lax.ppermute(pick(last * (1 - odd)), axis, both(low))  3.65 us
    pallas_call x1, Pallas kernels, body(): pl.pallas_call(shade, out_shape=(real(pairs, kinds, LANES),) * 2, in_spec...  2.59 us
    ppermute x1, waiting for transfers between devices, body(): other = lax.ppermute(sent, 'depth', [(i, i ^ 1) for i in range(depth)])  1.52 us
    ppermute x2, waiting for transfers between devices, facing(): lax.ppermute(pick(last * odd), axis, both(high))  1.43 us
    reshape x1, local copies, waits for them, and re-layouts, body(): cells = density.reshape(mats, planes, lines, blocks, LANES)  1.29 us
  transfers between devices with their start and end apart: 5, of which 2 were waited for; matrix products, arithmetic and copies ran while one was open for 3% of the time, Pallas kernels for 10%

profile of v3, /device:TPU:4, one launch (start us, length us, event | category | flops | bytes accessed | tf_op | source)
XLA Modules:
  0.0 41.3 jit_solution(1492817546431234850)
XLA Ops:
  0.0 1.3 %reshape.16.cells = bf16[3,8,2,32,128]{4,3,2,1,0:T(8,128)(2,1)S(1)} reshape(bf16[3,8,2,4096]{3,2,1,0:T(2,128)(2,1)} %param.3) | data formatting | bytes 786432 | tf_op jit(solution)/shard_map/reshape | solution.py:195
  1.3 0.7 %collective-permute-start.1 = (bf16[3,2,32,128]{3,2,1,0:T(8,128)(2,1)S(1)}, bf16[3,2,32,128]{3,2,1,0:T(8,128)(2,1)S(1)}, u32[]{:S(2)}, u32[]{:S(2)}) collective-permute-start(bf16[3,2,32,128]{3,2,1,0:T(8,128)(2,1)S(1)} %get-tuple-element.17), channel_id=1, source_target_pairs={{8,16},{24,32},{40,48},{56,64},{72,80},{88,96},{104,112},{120,128}... | collective-permute-start | bytes 147464 | tf_op jit(solution)/shard_map/ppermute | solution.py:23
  2.0 3.4 %collective-permute-start = (bf16[3,2,32,128]{3,2,1,0:T(8,128)(2,1)S(1)}, bf16[3,2,32,128]{3,2,1,0:T(8,128)(2,1)S(1)}, u32[]{:S(2)}, u32[]{:S(2)}) collective-permute-start(bf16[3,2,32,128]{3,2,1,0:T(8,128)(2,1)S(1)} %get-tuple-element.18), channel_id=1, source_target_pairs={{0,8},{16,24},{32,40},{48,56},{64,72},{80,88},{96,104},{112,120},{... | collective-permute-start | bytes 147464 | tf_op jit(solution)/shard_map/ppermute | solution.py:22
  5.4 4.9 %collective-permute-start.3 = (bf16[3,8,32,128]{3,2,1,0:T(8,128)(2,1)S(1)}, bf16[3,8,32,128]{3,2,1,0:T(8,128)(2,1)S(1)}, u32[]{:S(2)}, u32[]{:S(2)}) collective-permute-start(bf16[3,8,32,128]{3,2,1,0:T(8,128)(2,1)S(1)} %get-tuple-element.15), channel_id=1, source_target_pairs={{1,2},{3,4},{5,6},{2,1},{4,3},{6,5},{9,10},{11,12},{13,14},{10,9},... | collective-permute-start | bytes 589832 | tf_op jit(solution)/shard_map/ppermute | solution.py:23
  10.3 0.3 collective-permute-start.2
  10.6 0.1 pad.2.clone
  10.6 0.9 %shift-left_or_fusion = s32[4,1,256]{2,1,0:T(1,128)S(1)} fusion(s32[4,4,256]{2,1,0:T(4,128)} %param.5), kind=kLoop, calls=%fused_computation.6 | loop fusion | flops 6144 | bytes 20480 | tf_op jit(solution)/shard_map/or | solution.py:176
  11.5 0.1 slice.20
  11.6 0.0 copy-start
  11.6 0.7 %copy-done = f32[4,3]{1,0:T(4,128)S(1)} copy-done((f32[4,3]{1,0:T(4,128)S(1)}, f32[4,3]{1,0:T(4,128)}, u32[]{:S(2)}) %copy-start) | copy-done | bytes 72
  12.3 4.0 %lookup.1 = (f32[8,8,16,8,128]{4,3,2,1,0:T(8,128)S(1)}, f32[3,8,2,32,128]{4,3,2,1,0:T(8,128)S(1)}, f32[3,8,2,32,128]{4,3,2,1,0:T(8,128)S(1)}) custom-call(f32[4,3]{1,0:T(4,128)S(1)} %copy-done, s32[16,128]{1,0:T(8,128)S(1)} %reshape.15.table, bf16[3,8,2,32,128]{4,3,2,1,0:T(8,128)(2,1)S(1)} %reshape.16.cells), custom_call_target="tpu_custom_call" | custom-call | flops 4000000000 | bytes 8000000 | tf_op jit(solution)/shard_map/lookup/pallas_call | solution.py:198
  16.3 0.0 collective-permute-done.1.depth_b
  16.3 0.0 collective-permute-done.depth_a
  16.3 1.4 %collective-permute-done.3.tile_b = bf16[3,8,32,128]{3,2,1,0:T(8,128)(2,1)S(1)} collective-permute-done((bf16[3,8,32,128]{3,2,1,0:T(8,128)(2,1)S(1)}, bf16[3,8,32,128]{3,2,1,0:T(8,128)(2,1)S(1)}, u32[]{:S(2)}, u32[]{:S(2)}) %collective-permute-start.3) | collective-permute-done | bytes 196640 | tf_op jit(solution)/shard_map/ppermute | solution.py:23
  17.8 0.0 collective-permute-done.2.tile_a
  17.8 2.6 %shade.1 = (f32[16,32,128]{2,1,0:T(8,128)S(1)}, f32[16,32,128]{2,1,0:T(8,128)S(1)}) custom-call(f32[4,3]{1,0:T(4,128)S(1)} %copy-done, f32[8,8,16,8,128]{4,3,2,1,0:T(8,128)S(1)} %get-tuple-element.10.hues, f32[3,8,2,32,128]{4,3,2,1,0:T(8,128)S(1)} %get-tuple-element.11.field, f32[3,8,2,32,128]{4,3,2,1,0:T(8,128)S(1)} %get-tuple-element.12.slope_x, ...), custom_call_target="tpu_custom_call" | custom-call | tf_op jit(solution)/shard_map/shade/pallas_call | solution.py:211
  20.4 0.1 collective-permute-start.4
  20.5 1.5 %collective-permute-done.4.other = f32[16,32,128]{2,1,0:T(8,128)S(1)} collective-permute-done((f32[16,32,128]{2,1,0:T(8,128)S(1)}, f32[16,32,128]{2,1,0:T(8,128)S(1)}, u32[]{:S(2)}, u32[]{:S(2)}) %collective-permute-start.4) | collective-permute-done | bytes 262176 | tf_op jit(solution)/shard_map/ppermute | solution.py:220
  22.0 0.1 join.1
  22.0 18.6 %all_to_all.5.parts = f32[16,32,128]{2,1,0:T(8,128)S(1)} all-to-all(f32[16,32,128]{2,1,0:T(8,128)S(1)} %join.1), channel_id=1, replica_groups={{0,16,32,48,64,80,96,112,128,144,160,176,192,208,224,240},{8,24,40,56,7..., dimensions={0} | all-to-all | bytes 524288 | tf_op jit(solution)/shard_map/all_to_all | solution.py:230
  40.7 0.6 %composite.1 = f32[4,4,2,128]{3,2,1,0:T(2,128)} custom-call(f32[16,32,128]{2,1,0:T(8,128)S(1)} %all_to_all.5.parts), custom_call_target="tpu_custom_call" | custom-call | tf_op jit(solution)/shard_map/composite/pallas_call | solution.py:231
  (5 shorter events, 0.1 us)
Async XLA Ops:
  1.3 15.0 %collective-permute-start.1 = (bf16[3,2,32,128]{3,2,1,0:T(8,128)(2,1)S(1)}, bf16[3,2,32,128]{3,2,1,0:T(8,128)(2,1)S(1)}, u32[]{:S(2)}, u32[]{:S(2)}) collective-permute-start(bf16[3,2,32,128]{3,2,1,0:T(8,128)(2,1)S(1)} %get-tuple-element.17), channel_id=1, source_target_pairs={{8,16},{24,32},{40,48},{56,64},{72,80},{88,96},{104,112},{120,128}... | collective-permute-start | bytes 147464 | tf_op jit(solution)/shard_map/ppermute | solution.py:23
  2.0 14.3 %collective-permute-start = (bf16[3,2,32,128]{3,2,1,0:T(8,128)(2,1)S(1)}, bf16[3,2,32,128]{3,2,1,0:T(8,128)(2,1)S(1)}, u32[]{:S(2)}, u32[]{:S(2)}) collective-permute-start(bf16[3,2,32,128]{3,2,1,0:T(8,128)(2,1)S(1)} %get-tuple-element.18), channel_id=1, source_target_pairs={{0,8},{16,24},{32,40},{48,56},{64,72},{80,88},{96,104},{112,120},{... | collective-permute-start | bytes 147464 | tf_op jit(solution)/shard_map/ppermute | solution.py:22
  5.4 12.4 %collective-permute-start.3 = (bf16[3,8,32,128]{3,2,1,0:T(8,128)(2,1)S(1)}, bf16[3,8,32,128]{3,2,1,0:T(8,128)(2,1)S(1)}, u32[]{:S(2)}, u32[]{:S(2)}) collective-permute-start(bf16[3,8,32,128]{3,2,1,0:T(8,128)(2,1)S(1)} %get-tuple-element.15), channel_id=1, source_target_pairs={{1,2},{3,4},{5,6},{2,1},{4,3},{6,5},{9,10},{11,12},{13,14},{10,9},... | collective-permute-start | bytes 589832 | tf_op jit(solution)/shard_map/ppermute | solution.py:23
  10.3 7.5 %collective-permute-start.2 = (bf16[3,8,32,128]{3,2,1,0:T(8,128)(2,1)S(1)}, bf16[3,8,32,128]{3,2,1,0:T(8,128)(2,1)S(1)}, u32[]{:S(2)}, u32[]{:S(2)}) collective-permute-start(bf16[3,8,32,128]{3,2,1,0:T(8,128)(2,1)S(1)} %get-tuple-element.16), channel_id=1, source_target_pairs={{0,1},{2,3},{4,5},{6,7},{1,0},{3,2},{5,4},{7,6},{8,9},{10,11},{12,... | collective-permute-start | bytes 589832 | tf_op jit(solution)/shard_map/ppermute | solution.py:22
  11.6 0.7 %copy-start = (f32[4,3]{1,0:T(4,128)S(1)}, f32[4,3]{1,0:T(4,128)}, u32[]{:S(2)}) copy-start(f32[4,3]{1,0:T(4,128)} %weight.3) | copy-start | bytes 148
  20.4 1.6 %collective-permute-start.4 = (f32[16,32,128]{2,1,0:T(8,128)S(1)}, f32[16,32,128]{2,1,0:T(8,128)S(1)}, u32[]{:S(2)}, u32[]{:S(2)}) collective-permute-start(f32[16,32,128]{2,1,0:T(8,128)S(1)} %get-tuple-element.14), channel_id=1, source_target_pairs={{0,8},{8,0},{16,24},{24,16},{32,40},{40,32},{48,56},{56,48},{64,72... | collective-permute-start | bytes 786440 | tf_op jit(solution)/shard_map/ppermute | solution.py:220

commit v4 on v3

--- a/solution.py
+++ b/solution.py
@@ -11,17 +11,14 @@
 ROWS = 8
 
 
-def facing(cells, axis, dim):
-    count, last = lax.axis_size(axis), cells.shape[dim] - 1
+def partners(axis, start):
+    count = lax.axis_size(axis)
+    return [p for i in range(start, count - 1, 2) for p in ((i, i + 1), (i + 1, i))]
+
+
+def end(axis, high, last):
     odd = lax.axis_index(axis) % 2
-    pick = lambda at: lax.dynamic_index_in_dim(cells, at, dim, keepdims=False)
-    low = [(i, i + 1) for i in range(0, count - 1, 2)]
-    high = [(i, i + 1) for i in range(1, count - 1, 2)]
-    both = lambda pairs: pairs + [(j, i) for i, j in pairs]
-    return (
-        lax.ppermute(pick(last * (1 - odd)), axis, both(low)),
-        lax.ppermute(pick(last * odd), axis, both(high)),
-    )
+    return last * odd if high else last * (1 - odd)
 
 
 def mix(weights, parts):
@@ -31,15 +28,17 @@
     return total
 
 
-def lookup(depth_total, weight, table, cells, hues, field, slope_x):
+def widen(cells, field, slope_x, low, high):
     mats, planes, lines, blocks, _ = cells.shape
-    energies = weight.shape[0]
-    groups = blocks // ROWS
     lane = lax.broadcasted_iota(jnp.int32, (blocks, LANES), 1)
     block = lax.broadcasted_iota(jnp.int32, (blocks, LANES), 0)
     zero = jnp.zeros((blocks, LANES), jnp.float32)
-
-    def widen(plane, _):
+    for m in range(mats):
+        for y in range(lines):
+            low[m, y] = cells[m, end("depth", False, planes - 1), y]
+            high[m, y] = cells[m, end("depth", True, planes - 1), y]
+
+    def one(plane, _):
         for m in range(mats):
             for y in range(lines):
                 here = cells[m, plane, y].astype(jnp.float32)
@@ -51,7 +50,24 @@
                 slope_x[m, plane, y] = right - left
         return 0
 
-    lax.fori_loop(0, planes, widen, 0)
+    lax.fori_loop(0, planes, one, 0)
+
+
+def lookup(depth_total, weight, color_table, field, hues, factor, table):
+    mats, planes, lines, blocks, _ = field.shape
+    groups = blocks // ROWS
+    energies, channels, bins = color_table.shape
+
+    channel = lax.broadcasted_iota(jnp.int32, (channels, bins), 0)
+    words = [jnp.sum(color_table[e] << (8 * channel), axis=0, keepdims=True) for e in range(energies)]
+    word = jnp.concatenate(words + words[: ROWS - energies], axis=0)
+    next_word = pltpu.roll(word, bins - 1, 1)
+    for e in range(energies):
+        for i in range(bins // LANES):
+            table[4 * e + i : 4 * e + i + 1, :] = word[e : e + 1, i * LANES : (i + 1) * LANES]
+            table[4 * e + 2 + i : 4 * e + 3 + i, :] = next_word[e : e + 1, i * LANES : (i + 1) * LANES]
+        for m in range(mats):
+            factor[mats * e + m] = jnp.broadcast_to(weight[e : e + 1, m : m + 1], (ROWS, LANES))
 
     def chunk(step, _):
         y, group = step // groups, step % groups
@@ -59,7 +75,7 @@
         for plane in range(planes):
             middle = [field[m, plane, y, rows] for m in range(mats)]
             for e in range(energies):
-                level = 255.0 * (1.0 - jnp.exp(-0.5 * mix([weight[e, m] for m in range(mats)], middle)))
+                level = 255.0 * (1.0 - jnp.exp(-0.5 * mix([factor[mats * e + m] for m in range(mats)], middle)))
                 bin_ = level.astype(jnp.int32)
                 past = level - bin_.astype(jnp.float32)
                 first = (1.0 - past).astype(jnp.bfloat16).astype(jnp.float32)
@@ -83,13 +99,12 @@
     lax.fori_loop(0, lines * groups, chunk, 0)
 
 
-def shade(weight, hues, field, slope_x, depth_a, depth_b, tile_a, tile_b, kept, sent, image):
+def shade(factor, hues, field, slope_x, depth_a, depth_b, tile_a, tile_b, kept, sent, image):
     mats, planes, lines, blocks, _ = field.shape
-    energies = weight.shape[0]
+    energies = factor.shape[0] // mats
     groups = blocks // ROWS
     kinds = 4 * energies * lines
     tile_odd, depth_odd = lax.axis_index("tile") % 2, lax.axis_index("depth") % 2
-    wide = lambda ref, *at: ref[at].astype(jnp.float32)
 
     def chunk(group, _):
         rows = pl.ds(pl.multiple_of(group * ROWS, ROWS), ROWS)
@@ -113,7 +128,7 @@
                     dy.append(below - above)
                     dx.append(slope_x[m, plane, y, rows])
                 for e in range(energies):
-                    half = [0.5 * weight[e, m] for m in range(mats)]
+                    half = [0.5 * factor[mats * e + m] for m in range(mats)]
                     grad_z, grad_y, grad_x = mix(half, dz), mix(half, dy), mix(half, dx)
                     slope_sq = grad_z * grad_z + grad_y * grad_y + grad_x * grad_x
                     root = lax.rsqrt(slope_sq + 1.0)
@@ -169,15 +184,6 @@
             out[e, c] = total[c][e * lines : (e + 1) * lines, :]
 
 
-def packed_table(color_table):
-    energies, channels, bins = color_table.shape
-    word = color_table[:, 0]
-    for c in range(1, channels):
-        word = word | (color_table[:, c] << (8 * c))
-    after = jnp.concatenate([word[:, 1:], jnp.zeros_like(word[:, :1])], axis=1)
-    return jnp.concatenate([word, after], axis=1).reshape(energies * 2 * bins // LANES, LANES)
-
-
 def limit(mib):
     return pltpu.CompilerParams(vmem_limit_bytes=mib * 2**20)
 
@@ -189,34 +195,47 @@
     depth = lax.axis_size("depth")
     kinds = 4 * energies * lines
     pairs = blocks // 2
-    smem, vmem = pl.BlockSpec(memory_space=pltpu.SMEM), pl.BlockSpec(memory_space=pltpu.VMEM)
+    vmem = pl.BlockSpec(memory_space=pltpu.VMEM)
     real = lambda *shape: jax.ShapeDtypeStruct(shape, jnp.float32)
+    short = lambda *shape: jax.ShapeDtypeStruct(shape, density.dtype)
 
     cells = density.reshape(mats, planes, lines, blocks, LANES)
-    depth_a, depth_b = facing(cells, "depth", 1)
-    tile_a, tile_b = facing(cells, "tile", 2)
-    hues, field, slope_x = pl.pallas_call(
+    row = lambda high: lax.dynamic_index_in_dim(cells, end("tile", high, lines - 1), 2, keepdims=False)
+    tile_a = lax.ppermute(row(False), "tile", partners("tile", 0))
+    tile_b = lax.ppermute(row(True), "tile", partners("tile", 1))
+    field, slope_x, low, high = pl.pallas_call(
+        widen,
+        out_shape=(real(*cells.shape),) * 2 + (short(mats, lines, blocks, LANES),) * 2,
+        in_specs=[vmem],
+        out_specs=(vmem,) * 4,
+        compiler_params=limit(4),
+        cost_estimate=pl.CostEstimate(flops=1_000_000_000, bytes_accessed=2_000_000, transcendentals=0),
+        name="widen",
+    )(cells)
+    depth_a = lax.ppermute(low, "depth", partners("depth", 0))
+    depth_b = lax.ppermute(high, "depth", partners("depth", 1))
+    hues, factor = pl.pallas_call(
         functools.partial(lookup, planes * depth),
         out_shape=(
             real(planes, lines * blocks // ROWS, 4 * energies, ROWS, LANES),
-            real(*cells.shape),
-            real(*cells.shape),
+            real(energies * mats, ROWS, LANES),
         ),
-        in_specs=[smem, vmem, vmem],
-        out_specs=(vmem, vmem, vmem),
+        in_specs=[vmem] * 3,
+        out_specs=(vmem,) * 2,
+        scratch_shapes=[pltpu.VMEM((energies * 2 * color_table.shape[2] // LANES, LANES), jnp.int32)],
         compiler_params=limit(8),
         cost_estimate=pl.CostEstimate(flops=4_000_000_000, bytes_accessed=8_000_000, transcendentals=300_000),
         name="lookup",
-    )(material_weight, packed_table(color_table), cells)
+    )(material_weight, color_table, field)
     kept, sent = pl.pallas_call(
         shade,
         out_shape=(real(pairs, kinds, LANES),) * 2,
-        in_specs=[smem] + [vmem] * 7,
+        in_specs=[vmem] * 8,
         out_specs=(vmem, vmem),
         scratch_shapes=[pltpu.VMEM((blocks * kinds, LANES), jnp.float32)],
         compiler_params=limit(8),
         name="shade",
-    )(material_weight, hues, field, slope_x, depth_a, depth_b, tile_a, tile_b)
+    )(factor, hues, field, slope_x, depth_a, depth_b, tile_a, tile_b)
     other = lax.ppermute(sent, "depth", [(i, i ^ 1) for i in range(depth)])
     joined = pl.pallas_call(
         functools.partial(join, energies * lines),

time: 41.8 us -> 39.4 us (0.943)
  starting transfers between devices: 9.27 us -> 6.7 us
  blocking collectives: 18.6 us -> 20.4 us
  Pallas kernels: 7.27 us -> 6.37 us
  other arithmetic: 0.89 us -> 0 us
  waiting for transfers between devices: 2.95 us -> 3.78 us
  local copies, waits for them, and re-layouts: 2.17 us -> 1.36 us
    ppermute x4, starting transfers between devices: 9.18 us -> 5.9 us  [the longest x1 4.87 us: body(): tile_b = lax.ppermute(row(True), 'tile', partners('tile', 1))]
    all_to_all x1, blocking collectives: 18.6 us -> 20.4 us  [body(): lax.all_to_all(joined, 'depth', 0, 0, axis_index_groups=same_core, tiled=...]
    pallas_call x1, Pallas kernels: 4 us -> 2.74 us  [body(): pl.pallas_call(functools.partial(lookup, planes * depth), out_shape=(real...]
    ppermute x4, waiting for transfers between devices: 1.43 us -> 2.62 us  [the longest x1 2.61 us: body(): tile_b = lax.ppermute(row(True), 'tile', partners('tile', 1))]
    or x1 -> x0, other arithmetic: 0.88 us -> none  [packed_table(): word = word | color_table[:, c] << 8 * c]
    pallas_call x0 -> x1, Pallas kernels: none -> 0.81 us  [body(): pl.pallas_call(widen, out_shape=(real(*cells.shape),) * 2 + (short(mats,...]
    ppermute x1, starting transfers between devices: 0.09 us -> 0.79 us  [body(): other = lax.ppermute(sent, 'depth', [(i, i ^ 1) for i in range(depth)])]
    unnamed x3 -> x4, local copies, waits for them, and re-layouts: 0.68 us -> 0.01 us
  transfers between devices with their start and end apart: 5 -> 5, of which waited for: 2 -> 2; matrix products, arithmetic and copies ran while one was open for 3% -> 0% of each run, Pallas kernels for 10% -> 9%
where the time goes in v4:
time: 39.4 us; the launch traced here: 38.7 us
  blocking collectives  20.4 us (52%)
  starting transfers between devices  6.7 us (17%)
  Pallas kernels  6.37 us (16%)
  waiting for transfers between devices  3.78 us (10%)
  local copies, waits for them, and re-layouts  1.36 us (3%)
    all_to_all x1, blocking collectives, body(): lax.all_to_all(joined, 'depth', 0, 0, axis_index_groups=same_core, tiled=...  20.4 us
    ppermute x1, starting transfers between devices, body(): tile_b = lax.ppermute(row(True), 'tile', partners('tile', 1))  4.87 us
    pallas_call x1, Pallas kernels, body(): pl.pallas_call(functools.partial(lookup, planes * depth), out_shape=(real...  2.74 us
    ppermute x1, waiting for transfers between devices, body(): tile_b = lax.ppermute(row(True), 'tile', partners('tile', 1))  2.61 us
    pallas_call x1, Pallas kernels, body(): pl.pallas_call(shade, out_shape=(real(pairs, kinds, LANES),) * 2, in_spec...  2.13 us
    reshape x1, local copies, waits for them, and re-layouts, body(): cells = density.reshape(mats, planes, lines, blocks, LANES)  1.32 us
    ppermute x1, waiting for transfers between devices, body(): other = lax.ppermute(sent, 'depth', [(i, i ^ 1) for i in range(depth)])  1.16 us
    pallas_call x1, Pallas kernels, body(): pl.pallas_call(widen, out_shape=(real(*cells.shape),) * 2 + (short(mats,...  0.81 us
  transfers between devices with their start and end apart: 5, of which 2 were waited for; matrix products, arithmetic and copies ran while one was open for 0% of the time, Pallas kernels for 9%

profile of v4, /device:TPU:4, one launch (start us, length us, event | category | flops | bytes accessed | tf_op | source)
XLA Modules:
  0.0 38.7 jit_solution(1859561133503969840)
XLA Ops:
  0.0 0.0 copy-start
  0.0 0.0 copy-start.1
  0.0 1.3 %reshape.3.cells = bf16[3,8,2,32,128]{4,3,2,1,0:T(8,128)(2,1)S(1)} reshape(bf16[3,8,2,4096]{3,2,1,0:T(2,128)(2,1)} %param.3) | data formatting | bytes 786432 | tf_op jit(solution)/shard_map/reshape | solution.py:202
  1.4 4.9 %collective-permute-start.3 = (bf16[3,8,32,128]{3,2,1,0:T(8,128)(2,1)S(1)}, bf16[3,8,32,128]{3,2,1,0:T(8,128)(2,1)S(1)}, u32[]{:S(2)}, u32[]{:S(2)}) collective-permute-start(bf16[3,8,32,128]{3,2,1,0:T(8,128)(2,1)S(1)} %get-tuple-element.21), channel_id=1, source_target_pairs={{1,2},{2,1},{3,4},{4,3},{5,6},{6,5},{9,10},{10,9},{11,12},{12,11},... | collective-permute-start | bytes 589832 | tf_op jit(solution)/shard_map/ppermute | solution.py:205
  6.3 0.3 collective-permute-start.2
  6.5 0.8 %widen.1 = (f32[3,8,2,32,128]{4,3,2,1,0:T(8,128)S(1)}, f32[3,8,2,32,128]{4,3,2,1,0:T(8,128)S(1)}, bf16[3,2,32,128]{3,2,1,0:T(8,128)(2,1)S(1)}, bf16[3,2,32,128]{3,2,1,0:T(8,128)(2,1)S(1)}) custom-call(bf16[3,8,2,32,128]{4,3,2,1,0:T(8,128)(2,1)S(1)} %reshape.3.cells), custom_call_target="tpu_custom_call" | custom-call | flops 1000000000 | bytes 2000000 | tf_op jit(solution)/shard_map/widen/pallas_call | solution.py:206
  7.4 0.1 collective-permute-start
  7.5 0.7 %collective-permute-start.1 = (bf16[3,2,32,128]{3,2,1,0:T(8,128)(2,1)S(1)}, bf16[3,2,32,128]{3,2,1,0:T(8,128)(2,1)S(1)}, u32[]{:S(2)}, u32[]{:S(2)}) collective-permute-start(bf16[3,2,32,128]{3,2,1,0:T(8,128)(2,1)S(1)} %get-tuple-element.18), channel_id=1, source_target_pairs={{8,16},{16,8},{24,32},{32,24},{40,48},{48,40},{56,64},{64,56},{72,... | collective-permute-start | bytes 147464 | tf_op jit(solution)/shard_map/ppermute | solution.py:216
  8.1 0.0 copy-done
  8.1 0.0 copy-done.1
  8.2 2.7 %lookup.1 = (f32[8,8,16,8,128]{4,3,2,1,0:T(8,128)S(1)}, f32[12,8,128]{2,1,0:T(8,128)S(1)}) custom-call(f32[4,3]{1,0:T(4,128)S(1)} %copy-done.1, s32[4,4,256]{2,1,0:T(4,128)S(1)} %copy-done, f32[3,8,2,32,128]{4,3,2,1,0:T(8,128)S(1)} %get-tuple-element.13.field), custom_call_target="tpu_custom_call" | custom-call | flops 4000000000 | bytes 8000000 | tf_op jit(solution)/shard_map/lookup/pallas_call | solution.py:217
  10.9 0.0 collective-permute-done.depth_a
  10.9 0.0 collective-permute-done.1.depth_b
  10.9 2.6 %collective-permute-done.3.tile_b = bf16[3,8,32,128]{3,2,1,0:T(8,128)(2,1)S(1)} collective-permute-done((bf16[3,8,32,128]{3,2,1,0:T(8,128)(2,1)S(1)}, bf16[3,8,32,128]{3,2,1,0:T(8,128)(2,1)S(1)}, u32[]{:S(2)}, u32[]{:S(2)}) %collective-permute-start.3) | collective-permute-done | bytes 196640 | tf_op jit(solution)/shard_map/ppermute | solution.py:205
  13.5 0.0 collective-permute-done.2.tile_a
  13.5 2.1 %shade.1 = (f32[16,32,128]{2,1,0:T(8,128)S(1)}, f32[16,32,128]{2,1,0:T(8,128)S(1)}) custom-call(f32[12,8,128]{2,1,0:T(8,128)S(1)} %get-tuple-element.14.factor, f32[8,8,16,8,128]{4,3,2,1,0:T(8,128)S(1)} %get-tuple-element.15.hues, f32[3,8,2,32,128]{4,3,2,1,0:T(8,128)S(1)} %get-tuple-element.13.field, f32[3,8,2,32,128]{4,3,2,1,0:T(8,128)S(1)} %get-tuple-element.16.slope_x, ...), custom_call_target="tpu_custom_call" | custom-call | tf_op jit(solution)/shard_map/shade/pallas_call | solution.py:230
  15.7 0.8 %collective-permute-start.4 = (f32[16,32,128]{2,1,0:T(8,128)S(1)}, f32[16,32,128]{2,1,0:T(8,128)S(1)}, u32[]{:S(2)}, u32[]{:S(2)}) collective-permute-start(f32[16,32,128]{2,1,0:T(8,128)S(1)} %get-tuple-element.20), channel_id=1, source_target_pairs={{0,8},{8,0},{16,24},{24,16},{32,40},{40,32},{48,56},{56,48},{64,72... | collective-permute-start | bytes 786440 | tf_op jit(solution)/shard_map/ppermute | solution.py:239
  16.5 1.2 %collective-permute-done.4.other = f32[16,32,128]{2,1,0:T(8,128)S(1)} collective-permute-done((f32[16,32,128]{2,1,0:T(8,128)S(1)}, f32[16,32,128]{2,1,0:T(8,128)S(1)}, u32[]{:S(2)}, u32[]{:S(2)}) %collective-permute-start.4) | collective-permute-done | bytes 262176 | tf_op jit(solution)/shard_map/ppermute | solution.py:239
  17.7 20.4 %all_to_all.5.parts = f32[16,32,128]{2,1,0:T(8,128)S(1)} all-to-all(f32[16,32,128]{2,1,0:T(8,128)S(1)} %join.1), channel_id=1, replica_groups={{0,16,32,48,64,80,96,112,128,144,160,176,192,208,224,240},{8,24,40,56,7..., dimensions={0} | all-to-all | bytes 524288 | tf_op jit(solution)/shard_map/all_to_all | solution.py:249
  38.1 0.6 %composite.1 = f32[4,4,2,128]{3,2,1,0:T(2,128)} custom-call(f32[16,32,128]{2,1,0:T(8,128)S(1)} %all_to_all.5.parts), custom_call_target="tpu_custom_call" | custom-call | tf_op jit(solution)/shard_map/composite/pallas_call | solution.py:250
  (2 shorter events, 0.1 us)
Async XLA Ops:
  0.0 8.1 %copy-start = (s32[4,4,256]{2,1,0:T(4,128)S(1)}, s32[4,4,256]{2,1,0:T(4,128)}, u32[]{:S(2)}) copy-start(s32[4,4,256]{2,1,0:T(4,128)} %color_table.1) | copy-start | bytes 49156
  0.0 8.1 %copy-start.1 = (f32[4,3]{1,0:T(4,128)S(1)}, f32[4,3]{1,0:T(4,128)}, u32[]{:S(2)}) copy-start(f32[4,3]{1,0:T(4,128)} %weight.1) | copy-start | bytes 148
  1.4 12.1 %collective-permute-start.3 = (bf16[3,8,32,128]{3,2,1,0:T(8,128)(2,1)S(1)}, bf16[3,8,32,128]{3,2,1,0:T(8,128)(2,1)S(1)}, u32[]{:S(2)}, u32[]{:S(2)}) collective-permute-start(bf16[3,8,32,128]{3,2,1,0:T(8,128)(2,1)S(1)} %get-tuple-element.21), channel_id=1, source_target_pairs={{1,2},{2,1},{3,4},{4,3},{5,6},{6,5},{9,10},{10,9},{11,12},{12,11},... | collective-permute-start | bytes 589832 | tf_op jit(solution)/shard_map/ppermute | solution.py:205
  6.3 7.3 %collective-permute-start.2 = (bf16[3,8,32,128]{3,2,1,0:T(8,128)(2,1)S(1)}, bf16[3,8,32,128]{3,2,1,0:T(8,128)(2,1)S(1)}, u32[]{:S(2)}, u32[]{:S(2)}) collective-permute-start(bf16[3,8,32,128]{3,2,1,0:T(8,128)(2,1)S(1)} %get-tuple-element.22), channel_id=1, source_target_pairs={{0,1},{1,0},{2,3},{3,2},{4,5},{5,4},{6,7},{7,6},{8,9},{9,8},{10,11... | collective-permute-start | bytes 589832 | tf_op jit(solution)/shard_map/ppermute | solution.py:204
  7.4 3.5 %collective-permute-start = (bf16[3,2,32,128]{3,2,1,0:T(8,128)(2,1)S(1)}, bf16[3,2,32,128]{3,2,1,0:T(8,128)(2,1)S(1)}, u32[]{:S(2)}, u32[]{:S(2)}) collective-permute-start(bf16[3,2,32,128]{3,2,1,0:T(8,128)(2,1)S(1)} %get-tuple-element.17), channel_id=1, source_target_pairs={{0,8},{8,0},{16,24},{24,16},{32,40},{40,32},{48,56},{56,48},{64,72... | collective-permute-start | bytes 147464 | tf_op jit(solution)/shard_map/ppermute | solution.py:215
  7.5 3.5 %collective-permute-start.1 = (bf16[3,2,32,128]{3,2,1,0:T(8,128)(2,1)S(1)}, bf16[3,2,32,128]{3,2,1,0:T(8,128)(2,1)S(1)}, u32[]{:S(2)}, u32[]{:S(2)}) collective-permute-start(bf16[3,2,32,128]{3,2,1,0:T(8,128)(2,1)S(1)} %get-tuple-element.18), channel_id=1, source_target_pairs={{8,16},{16,8},{24,32},{32,24},{40,48},{48,40},{56,64},{64,56},{72,... | collective-permute-start | bytes 147464 | tf_op jit(solution)/shard_map/ppermute | solution.py:216
  15.7 2.0 %collective-permute-start.4 = (f32[16,32,128]{2,1,0:T(8,128)S(1)}, f32[16,32,128]{2,1,0:T(8,128)S(1)}, u32[]{:S(2)}, u32[]{:S(2)}) collective-permute-start(f32[16,32,128]{2,1,0:T(8,128)S(1)} %get-tuple-element.20), channel_id=1, source_target_pairs={{0,8},{8,0},{16,24},{24,16},{32,40},{40,32},{48,56},{56,48},{64,72... | collective-permute-start | bytes 786440 | tf_op jit(solution)/shard_map/ppermute | solution.py:239

commit v5 on v4

--- a/solution.py
+++ b/solution.py
@@ -158,14 +158,33 @@
     lax.fori_loop(0, blocks // 2, part, 0)
 
 
+FINE, COARSE, TOP, KNEE = 1500.0, 64.0, 32767.0, 40.0
+BEND = TOP - FINE * (KNEE - 1.0)
+NOTHING = -32768
+
+
+def encode(value):
+    octave = jnp.log2(jnp.maximum(value, 1e-37))
+    code = jnp.maximum(TOP + FINE * (octave + 1.0), BEND + COARSE * (octave + KNEE))
+    code = jnp.round(jnp.minimum(code, TOP)).astype(jnp.int32)
+    return jnp.where(value > 1e-37, code, NOTHING).astype(jnp.int16)
+
+
+def decode(code):
+    code = code.astype(jnp.int32)
+    wide = code.astype(jnp.float32)
+    octave = jnp.minimum((wide - TOP) * (1.0 / FINE) - 1.0, (wide - BEND) * (1.0 / COARSE) - KNEE)
+    return jnp.where(code > NOTHING, jnp.exp2(octave), 0.0)
+
+
 def join(per, mine, other, out):
     odd = lax.axis_index("depth") % 2
     for pair in range(mine.shape[0]):
         a, b = mine[pair], other[pair]
         front, back = jnp.where(odd == 0, a, b), jnp.where(odd == 0, b, a)
         clear = 1.0 - front[-per:, :]
-        for i in range(0, front.shape[0], per):
-            out[pair, i : i + per, :] = front[i : i + per, :] + clear * back[i : i + per, :]
+        both = [front[i : i + per, :] + clear * back[i : i + per, :] for i in range(0, front.shape[0], per)]
+        out[pair] = encode(jnp.concatenate(both, axis=0))
 
 
 def composite(parts, out):
@@ -176,9 +195,10 @@
     keep = jnp.ones((per, LANES), jnp.float32)
     total = [jnp.zeros((per, LANES), jnp.float32) for _ in range(channels)]
     for brick in range(bricks):
-        part = [parts[brick, c * per : (c + 1) * per, :] for c in range(channels)]
-        total = [total[c] + keep * part[c] for c in range(channels)]
-        keep = keep * (1.0 - part[channels - 1])
+        part = decode(parts[brick])
+        for c in range(channels):
+            total[c] = total[c] + keep * part[c * per : (c + 1) * per, :]
+        keep = keep * (1.0 - part[(channels - 1) * per :, :])
     for c in range(channels):
         for e in range(energies):
             out[e, c] = total[c][e * lines : (e + 1) * lines, :]
@@ -239,7 +259,7 @@
     other = lax.ppermute(sent, "depth", [(i, i ^ 1) for i in range(depth)])
     joined = pl.pallas_call(
         functools.partial(join, energies * lines),
-        out_shape=real(pairs, kinds, LANES),
+        out_shape=jax.ShapeDtypeStruct((pairs, kinds, LANES), jnp.int16),
         in_specs=[vmem, vmem],
         out_specs=vmem,
         compiler_params=limit(2),

time: 39.4 us -> 37.8 us (0.959)
  blocking collectives: 20.4 us -> 18.7 us
    all_to_all x1, blocking collectives: 20.4 us -> 18.7 us  [body(): lax.all_to_all(joined, 'depth', 0, 0, axis_index_groups=same_core, tiled=...]
  transfers between devices with their start and end apart: 5 -> 5, of which waited for: 2 -> 2; matrix products, arithmetic and copies ran while one was open for 0% -> 0% of each run, Pallas kernels for 9% -> 10%
where the time goes in v5:
time: 37.8 us; the launch traced here: 37.2 us
  blocking collectives  18.7 us (49%)
  starting transfers between devices  6.7 us (18%)
  Pallas kernels  6.59 us (17%)
  waiting for transfers between devices  3.78 us (10%)
  local copies, waits for them, and re-layouts  1.36 us (4%)
    all_to_all x1, blocking collectives, body(): lax.all_to_all(joined, 'depth', 0, 0, axis_index_groups=same_core, tiled=...  18.7 us
    ppermute x1, starting transfers between devices, body(): tile_b = lax.ppermute(row(True), 'tile', partners('tile', 1))  4.87 us
    pallas_call x1, Pallas kernels, body(): pl.pallas_call(functools.partial(lookup, planes * depth), out_shape=(real...  2.74 us
    ppermute x1, waiting for transfers between devices, body(): tile_b = lax.ppermute(row(True), 'tile', partners('tile', 1))  2.61 us
    pallas_call x1, Pallas kernels, body(): pl.pallas_call(shade, out_shape=(real(pairs, kinds, LANES),) * 2, in_spec...  2.13 us
    reshape x1, local copies, waits for them, and re-layouts, body(): cells = density.reshape(mats, planes, lines, blocks, LANES)  1.32 us
    ppermute x1, waiting for transfers between devices, body(): other = lax.ppermute(sent, 'depth', [(i, i ^ 1) for i in range(depth)])  1.16 us
    pallas_call x1, Pallas kernels, body(): pl.pallas_call(widen, out_shape=(real(*cells.shape),) * 2 + (short(mats,...  0.81 us
  transfers between devices with their start and end apart: 5, of which 2 were waited for; matrix products, arithmetic and copies ran while one was open for 0% of the time, Pallas kernels for 10%

profile of v5, /device:TPU:4, one launch (start us, length us, event | category | flops | bytes accessed | tf_op | source)
XLA Modules:
  0.0 37.2 jit_solution(4037696182710969082)
XLA Ops:
  0.0 0.0 copy-start
  0.0 0.0 copy-start.1
  0.0 1.3 %reshape.3.cells = bf16[3,8,2,32,128]{4,3,2,1,0:T(8,128)(2,1)S(1)} reshape(bf16[3,8,2,4096]{3,2,1,0:T(2,128)(2,1)} %param.3) | data formatting | bytes 786432 | tf_op jit(solution)/shard_map/reshape | solution.py:222
  1.4 4.9 %collective-permute-start.3 = (bf16[3,8,32,128]{3,2,1,0:T(8,128)(2,1)S(1)}, bf16[3,8,32,128]{3,2,1,0:T(8,128)(2,1)S(1)}, u32[]{:S(2)}, u32[]{:S(2)}) collective-permute-start(bf16[3,8,32,128]{3,2,1,0:T(8,128)(2,1)S(1)} %get-tuple-element.21), channel_id=1, source_target_pairs={{1,2},{2,1},{3,4},{4,3},{5,6},{6,5},{9,10},{10,9},{11,12},{12,11},... | collective-permute-start | bytes 589832 | tf_op jit(solution)/shard_map/ppermute | solution.py:225
  6.3 0.3 collective-permute-start.2
  6.5 0.8 %widen.1 = (f32[3,8,2,32,128]{4,3,2,1,0:T(8,128)S(1)}, f32[3,8,2,32,128]{4,3,2,1,0:T(8,128)S(1)}, bf16[3,2,32,128]{3,2,1,0:T(8,128)(2,1)S(1)}, bf16[3,2,32,128]{3,2,1,0:T(8,128)(2,1)S(1)}) custom-call(bf16[3,8,2,32,128]{4,3,2,1,0:T(8,128)(2,1)S(1)} %reshape.3.cells), custom_call_target="tpu_custom_call" | custom-call | flops 1000000000 | bytes 2000000 | tf_op jit(solution)/shard_map/widen/pallas_call | solution.py:226
  7.4 0.1 collective-permute-start
  7.5 0.7 %collective-permute-start.1 = (bf16[3,2,32,128]{3,2,1,0:T(8,128)(2,1)S(1)}, bf16[3,2,32,128]{3,2,1,0:T(8,128)(2,1)S(1)}, u32[]{:S(2)}, u32[]{:S(2)}) collective-permute-start(bf16[3,2,32,128]{3,2,1,0:T(8,128)(2,1)S(1)} %get-tuple-element.18), channel_id=1, source_target_pairs={{8,16},{16,8},{24,32},{32,24},{40,48},{48,40},{56,64},{64,56},{72,... | collective-permute-start | bytes 147464 | tf_op jit(solution)/shard_map/ppermute | solution.py:236
  8.1 0.0 copy-done
  8.1 0.0 copy-done.1
  8.2 2.7 %lookup.1 = (f32[8,8,16,8,128]{4,3,2,1,0:T(8,128)S(1)}, f32[12,8,128]{2,1,0:T(8,128)S(1)}) custom-call(f32[4,3]{1,0:T(4,128)S(1)} %copy-done.1, s32[4,4,256]{2,1,0:T(4,128)S(1)} %copy-done, f32[3,8,2,32,128]{4,3,2,1,0:T(8,128)S(1)} %get-tuple-element.13.field), custom_call_target="tpu_custom_call" | custom-call | flops 4000000000 | bytes 8000000 | tf_op jit(solution)/shard_map/lookup/pallas_call | solution.py:237
  10.9 0.0 collective-permute-done.depth_a
  10.9 0.0 collective-permute-done.1.depth_b
  10.9 2.6 %collective-permute-done.3.tile_b = bf16[3,8,32,128]{3,2,1,0:T(8,128)(2,1)S(1)} collective-permute-done((bf16[3,8,32,128]{3,2,1,0:T(8,128)(2,1)S(1)}, bf16[3,8,32,128]{3,2,1,0:T(8,128)(2,1)S(1)}, u32[]{:S(2)}, u32[]{:S(2)}) %collective-permute-start.3) | collective-permute-done | bytes 196640 | tf_op jit(solution)/shard_map/ppermute | solution.py:225
  13.5 0.0 collective-permute-done.2.tile_a
  13.5 2.1 %shade.1 = (f32[16,32,128]{2,1,0:T(8,128)S(1)}, f32[16,32,128]{2,1,0:T(8,128)S(1)}) custom-call(f32[12,8,128]{2,1,0:T(8,128)S(1)} %get-tuple-element.14.factor, f32[8,8,16,8,128]{4,3,2,1,0:T(8,128)S(1)} %get-tuple-element.15.hues, f32[3,8,2,32,128]{4,3,2,1,0:T(8,128)S(1)} %get-tuple-element.13.field, f32[3,8,2,32,128]{4,3,2,1,0:T(8,128)S(1)} %get-tuple-element.16.slope_x, ...), custom_call_target="tpu_custom_call" | custom-call | tf_op jit(solution)/shard_map/shade/pallas_call | solution.py:250
  15.7 0.8 %collective-permute-start.4 = (f32[16,32,128]{2,1,0:T(8,128)S(1)}, f32[16,32,128]{2,1,0:T(8,128)S(1)}, u32[]{:S(2)}, u32[]{:S(2)}) collective-permute-start(f32[16,32,128]{2,1,0:T(8,128)S(1)} %get-tuple-element.20), channel_id=1, source_target_pairs={{0,8},{8,0},{16,24},{24,16},{32,40},{40,32},{48,56},{56,48},{64,72... | collective-permute-start | bytes 786440 | tf_op jit(solution)/shard_map/ppermute | solution.py:259
  16.5 1.2 %collective-permute-done.4.other = f32[16,32,128]{2,1,0:T(8,128)S(1)} collective-permute-done((f32[16,32,128]{2,1,0:T(8,128)S(1)}, f32[16,32,128]{2,1,0:T(8,128)S(1)}, u32[]{:S(2)}, u32[]{:S(2)}) %collective-permute-start.4) | collective-permute-done | bytes 262176 | tf_op jit(solution)/shard_map/ppermute | solution.py:259
  17.6 0.2 join.1
  17.8 18.7 %all_to_all.5.parts = s16[16,32,128]{2,1,0:T(8,128)(2,1)S(1)} all-to-all(s16[16,32,128]{2,1,0:T(8,128)(2,1)S(1)} %join.1), channel_id=1, replica_groups={{0,16,32,48,64,80,96,112,128,144,160,176,192,208,224,240},{8,24,40,56,7..., dimensions={0} | all-to-all | bytes 262144 | tf_op jit(solution)/shard_map/all_to_all | solution.py:269
  36.5 0.7 %composite.1 = f32[4,4,2,128]{3,2,1,0:T(2,128)} custom-call(s16[16,32,128]{2,1,0:T(8,128)(2,1)S(1)} %all_to_all.5.parts), custom_call_target="tpu_custom_call" | custom-call | tf_op jit(solution)/shard_map/composite/pallas_call | solution.py:270
  (1 shorter events, 0.0 us)
Async XLA Ops:
  0.0 8.1 %copy-start = (s32[4,4,256]{2,1,0:T(4,128)S(1)}, s32[4,4,256]{2,1,0:T(4,128)}, u32[]{:S(2)}) copy-start(s32[4,4,256]{2,1,0:T(4,128)} %color_table.1) | copy-start | bytes 49156
  0.0 8.1 %copy-start.1 = (f32[4,3]{1,0:T(4,128)S(1)}, f32[4,3]{1,0:T(4,128)}, u32[]{:S(2)}) copy-start(f32[4,3]{1,0:T(4,128)} %weight.1) | copy-start | bytes 148
  1.4 12.1 %collective-permute-start.3 = (bf16[3,8,32,128]{3,2,1,0:T(8,128)(2,1)S(1)}, bf16[3,8,32,128]{3,2,1,0:T(8,128)(2,1)S(1)}, u32[]{:S(2)}, u32[]{:S(2)}) collective-permute-start(bf16[3,8,32,128]{3,2,1,0:T(8,128)(2,1)S(1)} %get-tuple-element.21), channel_id=1, source_target_pairs={{1,2},{2,1},{3,4},{4,3},{5,6},{6,5},{9,10},{10,9},{11,12},{12,11},... | collective-permute-start | bytes 589832 | tf_op jit(solution)/shard_map/ppermute | solution.py:225
  6.3 7.3 %collective-permute-start.2 = (bf16[3,8,32,128]{3,2,1,0:T(8,128)(2,1)S(1)}, bf16[3,8,32,128]{3,2,1,0:T(8,128)(2,1)S(1)}, u32[]{:S(2)}, u32[]{:S(2)}) collective-permute-start(bf16[3,8,32,128]{3,2,1,0:T(8,128)(2,1)S(1)} %get-tuple-element.22), channel_id=1, source_target_pairs={{0,1},{1,0},{2,3},{3,2},{4,5},{5,4},{6,7},{7,6},{8,9},{9,8},{10,11... | collective-permute-start | bytes 589832 | tf_op jit(solution)/shard_map/ppermute | solution.py:224
  7.4 3.5 %collective-permute-start = (bf16[3,2,32,128]{3,2,1,0:T(8,128)(2,1)S(1)}, bf16[3,2,32,128]{3,2,1,0:T(8,128)(2,1)S(1)}, u32[]{:S(2)}, u32[]{:S(2)}) collective-permute-start(bf16[3,2,32,128]{3,2,1,0:T(8,128)(2,1)S(1)} %get-tuple-element.17), channel_id=1, source_target_pairs={{0,8},{8,0},{16,24},{24,16},{32,40},{40,32},{48,56},{56,48},{64,72... | collective-permute-start | bytes 147464 | tf_op jit(solution)/shard_map/ppermute | solution.py:235
  7.5 3.5 %collective-permute-start.1 = (bf16[3,2,32,128]{3,2,1,0:T(8,128)(2,1)S(1)}, bf16[3,2,32,128]{3,2,1,0:T(8,128)(2,1)S(1)}, u32[]{:S(2)}, u32[]{:S(2)}) collective-permute-start(bf16[3,2,32,128]{3,2,1,0:T(8,128)(2,1)S(1)} %get-tuple-element.18), channel_id=1, source_target_pairs={{8,16},{16,8},{24,32},{32,24},{40,48},{48,40},{56,64},{64,56},{72,... | collective-permute-start | bytes 147464 | tf_op jit(solution)/shard_map/ppermute | solution.py:236
  15.7 2.0 %collective-permute-start.4 = (f32[16,32,128]{2,1,0:T(8,128)S(1)}, f32[16,32,128]{2,1,0:T(8,128)S(1)}, u32[]{:S(2)}, u32[]{:S(2)}) collective-permute-start(f32[16,32,128]{2,1,0:T(8,128)S(1)} %get-tuple-element.20), channel_id=1, source_target_pairs={{0,8},{8,0},{16,24},{24,16},{32,40},{40,32},{48,56},{56,48},{64,72... | collective-permute-start | bytes 786440 | tf_op jit(solution)/shard_map/ppermute | solution.py:259

commit v6 on v5

--- a/solution.py
+++ b/solution.py
@@ -1,4 +1,5 @@
 import functools
+import math
 
 import jax
 import jax.numpy as jnp
@@ -28,80 +29,74 @@
     return total
 
 
-def widen(cells, field, slope_x, low, high):
+def plane_to_send(high, cells, *refs):
+    mats, planes, lines, _, _ = cells.shape
+    for m in range(mats):
+        for y in range(lines):
+            refs[-1][m, y] = cells[m, end("depth", high, planes - 1), y]
+
+
+def rounded(x):
+    big = x * 65537.0
+    return big - (big - x)
+
+
+def lookup(depth_total, weight, color_table, cells, hues, field, slope_x, half, power, even, odd):
     mats, planes, lines, blocks, _ = cells.shape
+    groups = blocks // ROWS
+    energies, channels, bins = color_table.shape
+
+    channel = lax.broadcasted_iota(jnp.int32, (channels, bins), 0)
+    words = [jnp.sum(color_table[e] << (8 * channel), axis=0, keepdims=True) for e in range(energies)]
+    word = jnp.concatenate(words + words[: ROWS - energies], axis=0)
+    place = lax.broadcasted_iota(jnp.int32, (ROWS, LANES), 1)
+    twice = (2 * place) & (LANES - 1)
+    pick = lambda row, spot: jnp.take_along_axis(row, spot, axis=1, mode="promise_in_bounds")
+    for table, spot in ((even, twice), (odd, twice + 1)):
+        table[...] = jnp.where(place < LANES // 2, pick(word[:, :LANES], spot), pick(word[:, LANES:], spot))
+    for e in range(energies):
+        for m in range(mats):
+            value = 0.5 * jnp.broadcast_to(weight[e : e + 1, m : m + 1], (ROWS, LANES))
+            half[mats * e + m] = value
+            power[mats * e + m] = value * (-math.log2(math.e))
+
     lane = lax.broadcasted_iota(jnp.int32, (blocks, LANES), 1)
     block = lax.broadcasted_iota(jnp.int32, (blocks, LANES), 0)
     zero = jnp.zeros((blocks, LANES), jnp.float32)
-    for m in range(mats):
-        for y in range(lines):
-            low[m, y] = cells[m, end("depth", False, planes - 1), y]
-            high[m, y] = cells[m, end("depth", True, planes - 1), y]
-
-    def one(plane, _):
+
+    def line(step, _):
+        plane, y = step // lines, step % lines
+        here = [cells[m, plane, y].astype(jnp.float32) for m in range(mats)]
         for m in range(mats):
-            for y in range(lines):
-                here = cells[m, plane, y].astype(jnp.float32)
-                field[m, plane, y] = here
-                before = jnp.where(block == 0, zero, pltpu.roll(here, 1, 0))
-                after = jnp.where(block == blocks - 1, zero, pltpu.roll(here, blocks - 1, 0))
-                left = pltpu.roll(jnp.where(lane == LANES - 1, before, here), 1, 1)
-                right = pltpu.roll(jnp.where(lane == 0, after, here), LANES - 1, 1)
-                slope_x[m, plane, y] = right - left
-        return 0
-
-    lax.fori_loop(0, planes, one, 0)
-
-
-def lookup(depth_total, weight, color_table, field, hues, factor, table):
-    mats, planes, lines, blocks, _ = field.shape
-    groups = blocks // ROWS
-    energies, channels, bins = color_table.shape
-
-    channel = lax.broadcasted_iota(jnp.int32, (channels, bins), 0)
-    words = [jnp.sum(color_table[e] << (8 * channel), axis=0, keepdims=True) for e in range(energies)]
-    word = jnp.concatenate(words + words[: ROWS - energies], axis=0)
-    next_word = pltpu.roll(word, bins - 1, 1)
-    for e in range(energies):
-        for i in range(bins // LANES):
-            table[4 * e + i : 4 * e + i + 1, :] = word[e : e + 1, i * LANES : (i + 1) * LANES]
-            table[4 * e + 2 + i : 4 * e + 3 + i, :] = next_word[e : e + 1, i * LANES : (i + 1) * LANES]
-        for m in range(mats):
-            factor[mats * e + m] = jnp.broadcast_to(weight[e : e + 1, m : m + 1], (ROWS, LANES))
-
-    def chunk(step, _):
-        y, group = step // groups, step % groups
-        rows = pl.ds(pl.multiple_of(group * ROWS, ROWS), ROWS)
-        for plane in range(planes):
-            middle = [field[m, plane, y, rows] for m in range(mats)]
+            field[m, plane, y] = here[m]
+            before = jnp.where(block == 0, zero, pltpu.roll(here[m], 1, 0))
+            after = jnp.where(block == blocks - 1, zero, pltpu.roll(here[m], blocks - 1, 0))
+            left = pltpu.roll(jnp.where(lane == LANES - 1, before, here[m]), 1, 1)
+            right = pltpu.roll(jnp.where(lane == 0, after, here[m]), LANES - 1, 1)
+            slope_x[m, plane, y] = right - left
+        for group in range(groups):
+            middle = [here[m][group * ROWS : (group + 1) * ROWS] for m in range(mats)]
             for e in range(energies):
-                level = 255.0 * (1.0 - jnp.exp(-0.5 * mix([factor[mats * e + m] for m in range(mats)], middle)))
-                bin_ = level.astype(jnp.int32)
-                past = level - bin_.astype(jnp.float32)
-                first = (1.0 - past).astype(jnp.bfloat16).astype(jnp.float32)
-                second = past.astype(jnp.bfloat16).astype(jnp.float32)
-                high = bin_ >= LANES
-                spot = bin_ & (LANES - 1)
-
-                def look(row):
-                    pick = lambda r: jnp.take_along_axis(
-                        jnp.broadcast_to(table[r : r + 1, :], (ROWS, LANES)), spot, axis=1, mode="promise_in_bounds"
-                    )
-                    return jnp.where(high, pick(row + 1), pick(row))
-
-                here, next_ = look(4 * e), look(4 * e + 2)
+                fall = jnp.exp2(mix([power[mats * e + m] for m in range(mats)], middle))
+                level = 127.5 - 127.5 * fall
+                next_even = (level + 0.5).astype(jnp.int32)
+                away = jnp.abs(level - next_even.astype(jnp.float32))
+                away = away + away
+                at_odd, at_even = rounded(away), rounded(1.0 - away)
+                word_odd = pick(jnp.broadcast_to(odd[e : e + 1, :], (ROWS, LANES)), level.astype(jnp.int32))
+                word_even = pick(jnp.broadcast_to(even[e : e + 1, :], (ROWS, LANES)), next_even)
                 level_of = lambda word, c: (lax.shift_right_logical(word, 8 * c) & 255).astype(jnp.float32)
                 for c in range(4):
-                    hue = first * level_of(here, c) + second * level_of(next_, c)
-                    hues[plane, step, 4 * e + c] = hue if c < 3 else hue * (6.0 / (255.0 * depth_total))
+                    hue = at_even * level_of(word_even, c) + at_odd * level_of(word_odd, c)
+                    hues[plane, y * groups + group, 4 * e + c] = hue if c < 3 else hue * (6.0 / (255.0 * depth_total))
         return 0
 
-    lax.fori_loop(0, lines * groups, chunk, 0)
-
-
-def shade(factor, hues, field, slope_x, depth_a, depth_b, tile_a, tile_b, kept, sent, image):
+    lax.fori_loop(0, planes * lines, line, 0)
+
+
+def shade(half, hues, field, slope_x, depth_a, depth_b, tile_a, tile_b, kept, sent, image):
     mats, planes, lines, blocks, _ = field.shape
-    energies = factor.shape[0] // mats
+    energies = half.shape[0] // mats
     groups = blocks // ROWS
     kinds = 4 * energies * lines
     tile_odd, depth_odd = lax.axis_index("tile") % 2, lax.axis_index("depth") % 2
@@ -128,8 +123,8 @@
                     dy.append(below - above)
                     dx.append(slope_x[m, plane, y, rows])
                 for e in range(energies):
-                    half = [0.5 * factor[mats * e + m] for m in range(mats)]
-                    grad_z, grad_y, grad_x = mix(half, dz), mix(half, dy), mix(half, dx)
+                    share = [half[mats * e + m] for m in range(mats)]
+                    grad_z, grad_y, grad_x = mix(share, dz), mix(share, dy), mix(share, dx)
                     slope_sq = grad_z * grad_z + grad_y * grad_y + grad_x * grad_x
                     root = lax.rsqrt(slope_sq + 1.0)
                     shading = 0.3 + jnp.abs(0.56 * grad_z + 0.336 * grad_y + 0.252 * grad_x) * root
@@ -220,33 +215,43 @@
     short = lambda *shape: jax.ShapeDtypeStruct(shape, density.dtype)
 
     cells = density.reshape(mats, planes, lines, blocks, LANES)
-    row = lambda high: lax.dynamic_index_in_dim(cells, end("tile", high, lines - 1), 2, keepdims=False)
-    tile_a = lax.ppermute(row(False), "tile", partners("tile", 0))
-    tile_b = lax.ppermute(row(True), "tile", partners("tile", 1))
-    field, slope_x, low, high = pl.pallas_call(
-        widen,
-        out_shape=(real(*cells.shape),) * 2 + (short(mats, lines, blocks, LANES),) * 2,
-        in_specs=[vmem],
-        out_specs=(vmem,) * 4,
-        compiler_params=limit(4),
-        cost_estimate=pl.CostEstimate(flops=1_000_000_000, bytes_accessed=2_000_000, transcendentals=0),
-        name="widen",
-    )(cells)
-    depth_a = lax.ppermute(low, "depth", partners("depth", 0))
-    depth_b = lax.ppermute(high, "depth", partners("depth", 1))
-    hues, factor = pl.pallas_call(
+    rows = [lax.dynamic_index_in_dim(cells, end("tile", high, lines - 1), 2, keepdims=False) for high in (False, True)]
+    tile_a = lax.ppermute(rows[0], "tile", partners("tile", 0))
+    tile_b = lax.ppermute(rows[1], "tile", partners("tile", 1))
+
+    def send(high, *before):
+        return pl.pallas_call(
+            functools.partial(plane_to_send, high),
+            out_shape=short(mats, lines, blocks, LANES),
+            in_specs=[vmem] + [pl.BlockSpec(memory_space=pl.ANY)] * len(before),
+            out_specs=vmem,
+            compiler_params=limit(2),
+            cost_estimate=pl.CostEstimate(flops=1_000_000_000, bytes_accessed=2_000_000, transcendentals=0),
+            name="plane_to_send",
+        )(cells, *before)
+
+    plane_b = send(True, *rows)
+    depth_b = lax.ppermute(plane_b, "depth", partners("depth", 1))
+    depth_a = lax.ppermute(send(False, plane_b), "depth", partners("depth", 0))
+    hues, field, slope_x, half = pl.pallas_call(
         functools.partial(lookup, planes * depth),
         out_shape=(
             real(planes, lines * blocks // ROWS, 4 * energies, ROWS, LANES),
+            real(*cells.shape),
+            real(*cells.shape),
             real(energies * mats, ROWS, LANES),
         ),
         in_specs=[vmem] * 3,
-        out_specs=(vmem,) * 2,
-        scratch_shapes=[pltpu.VMEM((energies * 2 * color_table.shape[2] // LANES, LANES), jnp.int32)],
+        out_specs=(vmem,) * 4,
+        scratch_shapes=[
+            pltpu.VMEM((energies * mats, ROWS, LANES), jnp.float32),
+            pltpu.VMEM((ROWS, LANES), jnp.int32),
+            pltpu.VMEM((ROWS, LANES), jnp.int32),
+        ],
         compiler_params=limit(8),
         cost_estimate=pl.CostEstimate(flops=4_000_000_000, bytes_accessed=8_000_000, transcendentals=300_000),
         name="lookup",
-    )(material_weight, color_table, field)
+    )(material_weight, color_table, cells)
     kept, sent = pl.pallas_call(
         shade,
         out_shape=(real(pairs, kinds, LANES),) * 2,
@@ -255,7 +260,7 @@
         scratch_shapes=[pltpu.VMEM((blocks * kinds, LANES), jnp.float32)],
         compiler_params=limit(8),
         name="shade",
-    )(factor, hues, field, slope_x, depth_a, depth_b, tile_a, tile_b)
+    )(half, hues, field, slope_x, depth_a, depth_b, tile_a, tile_b)
     other = lax.ppermute(sent, "depth", [(i, i ^ 1) for i in range(depth)])
     joined = pl.pallas_call(
         functools.partial(join, energies * lines),

time: 37.8 us -> 36.8 us (0.974)
  starting transfers between devices: 6.7 us -> 9.28 us
  waiting for transfers between devices: 3.78 us -> 1.52 us
  blocking collectives: 18.7 us -> 17.8 us
  Pallas kernels: 6.59 us -> 6.13 us
    ppermute x4, starting transfers between devices: 5.9 us -> 9.16 us  [the longest x1 4.87 us: body(): tile_b = lax.ppermute(rows[1], 'tile', partners('tile', 1))]
    ppermute x4, waiting for transfers between devices: 2.62 us -> 0.01 us  [the longest x1 0.01 us: body(): depth_a = lax.ppermute(send(False, plane_b), 'depth', partners('depth', 0))]
    all_to_all x1, blocking collectives: 18.7 us -> 17.8 us  [body(): lax.all_to_all(joined, 'depth', 0, 0, axis_index_groups=same_core, tiled=...]
    pallas_call x1 -> x2, Pallas kernels: 0.81 us -> 0.03 us  [send(): pl.pallas_call(functools.partial(plane_to_send, high), out_shape=short(ma...]
    ppermute x1, starting transfers between devices: 0.79 us -> 0.12 us  [body(): other = lax.ppermute(sent, 'depth', [(i, i ^ 1) for i in range(depth)])]
    pallas_call x1, Pallas kernels: 2.74 us -> 3.16 us  [body(): pl.pallas_call(functools.partial(lookup, planes * depth), out_shape=(real...]
  transfers between devices with their start and end apart: 5 -> 5, of which waited for: 2 -> 1; matrix products, arithmetic and copies ran while one was open for 0% -> 0% of each run, Pallas kernels for 10% -> 9%
where the time goes in v6:
time: 36.8 us; the launch traced here: 36.2 us
  blocking collectives  17.8 us (48%)
  starting transfers between devices  9.28 us (25%)
  Pallas kernels  6.13 us (17%)
  waiting for transfers between devices  1.52 us (4%)
  local copies, waits for them, and re-layouts  1.34 us (4%)
    all_to_all x1, blocking collectives, body(): lax.all_to_all(joined, 'depth', 0, 0, axis_index_groups=same_core, tiled=...  17.8 us
    ppermute x1, starting transfers between devices, body(): tile_b = lax.ppermute(rows[1], 'tile', partners('tile', 1))  4.87 us
    ppermute x1, starting transfers between devices, body(): depth_a = lax.ppermute(send(False, plane_b), 'depth', partners('depth', 0))  3.36 us
    pallas_call x1, Pallas kernels, body(): pl.pallas_call(functools.partial(lookup, planes * depth), out_shape=(real...  3.16 us
    pallas_call x1, Pallas kernels, body(): pl.pallas_call(shade, out_shape=(real(pairs, kinds, LANES),) * 2, in_spec...  2.03 us
    ppermute x1, waiting for transfers between devices, body(): other = lax.ppermute(sent, 'depth', [(i, i ^ 1) for i in range(depth)])  1.51 us
    reshape x1, local copies, waits for them, and re-layouts, body(): cells = density.reshape(mats, planes, lines, blocks, LANES)  1.29 us
    pallas_call x1, Pallas kernels, body(): pl.pallas_call(composite, out_shape=real(energies, 4, lines, columns // d...  0.74 us
  transfers between devices with their start and end apart: 5, of which 1 were waited for; matrix products, arithmetic and copies ran while one was open for 0% of the time, Pallas kernels for 9%

profile of v6, /device:TPU:4, one launch (start us, length us, event | category | flops | bytes accessed | tf_op | source)
XLA Modules:
  0.0 36.2 jit_solution(10333243721771828489)
XLA Ops:
  0.0 1.3 %reshape.3.cells = bf16[3,8,2,32,128]{4,3,2,1,0:T(8,128)(2,1)S(1)} reshape(bf16[3,8,2,4096]{3,2,1,0:T(2,128)(2,1)} %param.3) | data formatting | bytes 786432 | tf_op jit(solution)/shard_map/reshape | solution.py:217
  1.3 0.0 copy-start
  1.3 0.0 copy-start.1
  1.4 4.9 %collective-permute-start.3 = (bf16[3,8,32,128]{3,2,1,0:T(8,128)(2,1)S(1)}, bf16[3,8,32,128]{3,2,1,0:T(8,128)(2,1)S(1)}, u32[]{:S(2)}, u32[]{:S(2)}) collective-permute-start(bf16[3,8,32,128]{3,2,1,0:T(8,128)(2,1)S(1)} %get-tuple-element.17.refs_1_), channel_id=1, source_target_pairs={{1,2},{2,1},{3,4},{4,3},{5,6},{6,5},{9,10},{10,9},{11,12},{12,11},... | collective-permute-start | bytes 589832 | tf_op jit(solution)/shard_map/ppermute | solution.py:220
  6.2 0.3 collective-permute-start.2
  6.5 0.7 %collective-permute-start.1 = (bf16[3,2,32,128]{3,2,1,0:T(8,128)(2,1)S(1)}, bf16[3,2,32,128]{3,2,1,0:T(8,128)(2,1)S(1)}, u32[]{:S(2)}, u32[]{:S(2)}) collective-permute-start(bf16[3,2,32,128]{3,2,1,0:T(8,128)(2,1)S(1)} %plane_to_send.2.refs_0_), channel_id=1, source_target_pairs={{8,16},{16,8},{24,32},{32,24},{40,48},{48,40},{56,64},{64,56},{72,... | collective-permute-start | bytes 147464 | tf_op jit(solution)/shard_map/ppermute | solution.py:234
  7.2 3.4 %collective-permute-start = (bf16[3,2,32,128]{3,2,1,0:T(8,128)(2,1)S(1)}, bf16[3,2,32,128]{3,2,1,0:T(8,128)(2,1)S(1)}, u32[]{:S(2)}, u32[]{:S(2)}) collective-permute-start(bf16[3,2,32,128]{3,2,1,0:T(8,128)(2,1)S(1)} %plane_to_send.3), channel_id=1, source_target_pairs={{0,8},{8,0},{16,24},{24,16},{32,40},{40,32},{48,56},{56,48},{64,72... | collective-permute-start | bytes 147464 | tf_op jit(solution)/shard_map/ppermute | solution.py:235
  10.6 0.0 copy-done
  10.6 0.0 copy-done.1
  10.6 3.2 %lookup.1 = (f32[8,8,16,8,128]{4,3,2,1,0:T(8,128)S(1)}, f32[3,8,2,32,128]{4,3,2,1,0:T(8,128)S(1)}, f32[3,8,2,32,128]{4,3,2,1,0:T(8,128)S(1)}, f32[12,8,128]{2,1,0:T(8,128)S(1)}) custom-call(f32[4,3]{1,0:T(4,128)S(1)} %copy-done.1, s32[4,4,256]{2,1,0:T(4,128)S(1)} %copy-done, bf16[3,8,2,32,128]{4,3,2,1,0:T(8,128)(2,1)S(1)} %reshape.3.cells), custom_call_target="tpu_custom_call" | custom-call | flops 4000000000 | bytes 8000000 | tf_op jit(solution)/shard_map/lookup/pallas_call | solution.py:236
  13.8 0.0 collective-permute-done.depth_a
  13.8 0.0 collective-permute-done.1.depth_b
  13.8 0.0 collective-permute-done.3.tile_b
  13.8 0.0 collective-permute-done.2.tile_a
  13.8 2.0 %shade.1 = (f32[16,32,128]{2,1,0:T(8,128)S(1)}, f32[16,32,128]{2,1,0:T(8,128)S(1)}) custom-call(f32[12,8,128]{2,1,0:T(8,128)S(1)} %get-tuple-element.11.half, f32[8,8,16,8,128]{4,3,2,1,0:T(8,128)S(1)} %get-tuple-element.12.hues, f32[3,8,2,32,128]{4,3,2,1,0:T(8,128)S(1)} %get-tuple-element.13.field, f32[3,8,2,32,128]{4,3,2,1,0:T(8,128)S(1)} %get-tuple-element.14.slope_x, ...), custom_call_target="tpu_custom_call" | custom-call | tf_op jit(solution)/shard_map/shade/pallas_call | solution.py:255
  15.8 0.1 collective-permute-start.4
  16.0 1.5 %collective-permute-done.4.other = f32[16,32,128]{2,1,0:T(8,128)S(1)} collective-permute-done((f32[16,32,128]{2,1,0:T(8,128)S(1)}, f32[16,32,128]{2,1,0:T(8,128)S(1)}, u32[]{:S(2)}, u32[]{:S(2)}) %collective-permute-start.4) | collective-permute-done | bytes 262176 | tf_op jit(solution)/shard_map/ppermute | solution.py:264
  17.5 0.2 join.1
  17.6 17.8 %all_to_all.5.parts = s16[16,32,128]{2,1,0:T(8,128)(2,1)S(1)} all-to-all(s16[16,32,128]{2,1,0:T(8,128)(2,1)S(1)} %join.1), channel_id=1, replica_groups={{0,16,32,48,64,80,96,112,128,144,160,176,192,208,224,240},{8,24,40,56,7..., dimensions={0} | all-to-all | bytes 262144 | tf_op jit(solution)/shard_map/all_to_all | solution.py:274
  35.5 0.7 %composite.1 = f32[4,4,2,128]{3,2,1,0:T(2,128)} custom-call(s16[16,32,128]{2,1,0:T(8,128)(2,1)S(1)} %all_to_all.5.parts), custom_call_target="tpu_custom_call" | custom-call | tf_op jit(solution)/shard_map/composite/pallas_call | solution.py:275
  (3 shorter events, 0.1 us)
Async XLA Ops:
  1.3 9.3 %copy-start = (s32[4,4,256]{2,1,0:T(4,128)S(1)}, s32[4,4,256]{2,1,0:T(4,128)}, u32[]{:S(2)}) copy-start(s32[4,4,256]{2,1,0:T(4,128)} %color_table.1) | copy-start | bytes 49156
  1.3 9.3 %copy-start.1 = (f32[4,3]{1,0:T(4,128)S(1)}, f32[4,3]{1,0:T(4,128)}, u32[]{:S(2)}) copy-start(f32[4,3]{1,0:T(4,128)} %weight.1) | copy-start | bytes 148
  1.4 12.4 %collective-permute-start.3 = (bf16[3,8,32,128]{3,2,1,0:T(8,128)(2,1)S(1)}, bf16[3,8,32,128]{3,2,1,0:T(8,128)(2,1)S(1)}, u32[]{:S(2)}, u32[]{:S(2)}) collective-permute-start(bf16[3,8,32,128]{3,2,1,0:T(8,128)(2,1)S(1)} %get-tuple-element.17.refs_1_), channel_id=1, source_target_pairs={{1,2},{2,1},{3,4},{4,3},{5,6},{6,5},{9,10},{10,9},{11,12},{12,11},... | collective-permute-start | bytes 589832 | tf_op jit(solution)/shard_map/ppermute | solution.py:220
  6.2 7.6 %collective-permute-start.2 = (bf16[3,8,32,128]{3,2,1,0:T(8,128)(2,1)S(1)}, bf16[3,8,32,128]{3,2,1,0:T(8,128)(2,1)S(1)}, u32[]{:S(2)}, u32[]{:S(2)}) collective-permute-start(bf16[3,8,32,128]{3,2,1,0:T(8,128)(2,1)S(1)} %get-tuple-element.18.refs_0_), channel_id=1, source_target_pairs={{0,1},{1,0},{2,3},{3,2},{4,5},{5,4},{6,7},{7,6},{8,9},{9,8},{10,11... | collective-permute-start | bytes 589832 | tf_op jit(solution)/shard_map/ppermute | solution.py:219
  6.5 7.2 %collective-permute-start.1 = (bf16[3,2,32,128]{3,2,1,0:T(8,128)(2,1)S(1)}, bf16[3,2,32,128]{3,2,1,0:T(8,128)(2,1)S(1)}, u32[]{:S(2)}, u32[]{:S(2)}) collective-permute-start(bf16[3,2,32,128]{3,2,1,0:T(8,128)(2,1)S(1)} %plane_to_send.2.refs_0_), channel_id=1, source_target_pairs={{8,16},{16,8},{24,32},{32,24},{40,48},{48,40},{56,64},{64,56},{72,... | collective-permute-start | bytes 147464 | tf_op jit(solution)/shard_map/ppermute | solution.py:234
  7.2 6.5 %collective-permute-start = (bf16[3,2,32,128]{3,2,1,0:T(8,128)(2,1)S(1)}, bf16[3,2,32,128]{3,2,1,0:T(8,128)(2,1)S(1)}, u32[]{:S(2)}, u32[]{:S(2)}) collective-permute-start(bf16[3,2,32,128]{3,2,1,0:T(8,128)(2,1)S(1)} %plane_to_send.3), channel_id=1, source_target_pairs={{0,8},{8,0},{16,24},{24,16},{32,40},{40,32},{48,56},{56,48},{64,72... | collective-permute-start | bytes 147464 | tf_op jit(solution)/shard_map/ppermute | solution.py:235
  15.8 1.6 %collective-permute-start.4 = (f32[16,32,128]{2,1,0:T(8,128)S(1)}, f32[16,32,128]{2,1,0:T(8,128)S(1)}, u32[]{:S(2)}, u32[]{:S(2)}) collective-permute-start(f32[16,32,128]{2,1,0:T(8,128)S(1)} %get-tuple-element.16), channel_id=1, source_target_pairs={{0,8},{8,0},{16,24},{24,16},{32,40},{40,32},{48,56},{56,48},{64,72... | collective-permute-start | bytes 786440 | tf_op jit(solution)/shard_map/ppermute | solution.py:264

commit v7 on v6

--- a/solution.py
+++ b/solution.py
@@ -14,7 +14,13 @@
 
 def partners(axis, start):
     count = lax.axis_size(axis)
-    return [p for i in range(start, count - 1, 2) for p in ((i, i + 1), (i + 1, i))]
+    ends = [(0, count - 1), (count - 1, 0)] if start else []
+    return ends + [p for i in range(start, count - 1, 2) for p in ((i, i + 1), (i + 1, i))]
+
+
+def inside(axis):
+    place = lax.axis_index(axis)
+    return (place > 0) & (place < lax.axis_size(axis) - 1)
 
 
 def end(axis, high, last):
@@ -91,7 +97,7 @@
                     hues[plane, y * groups + group, 4 * e + c] = hue if c < 3 else hue * (6.0 / (255.0 * depth_total))
         return 0
 
-    lax.fori_loop(0, planes * lines, line, 0)
+    lax.fori_loop(0, planes * lines, line, 0, unroll=4)
 
 
 def shade(half, hues, field, slope_x, depth_a, depth_b, tile_a, tile_b, kept, sent, image):
@@ -99,7 +105,9 @@
     energies = half.shape[0] // mats
     groups = blocks // ROWS
     kinds = 4 * energies * lines
+    pitch = image.shape[0] // blocks
     tile_odd, depth_odd = lax.axis_index("tile") % 2, lax.axis_index("depth") % 2
+    tile_inside, depth_inside = inside("tile"), inside("depth")
 
     def chunk(group, _):
         rows = pl.ds(pl.multiple_of(group * ROWS, ROWS), ROWS)
@@ -109,6 +117,7 @@
             near, far = [], []
             for m in range(mats):
                 a, b = depth_a[m, y, rows], depth_b[m, y, rows]
+                b = jnp.where(depth_inside, b, jnp.zeros_like(b))
                 near.append(jnp.where(depth_odd == 1, a, b))
                 far.append(jnp.where(depth_odd == 1, b, a))
             for plane in range(planes):
@@ -118,6 +127,7 @@
                     after = far[m] if plane == planes - 1 else field[m, plane + 1, y, rows]
                     dz.append(after - before)
                     a, b = tile_a[m, plane, rows], tile_b[m, plane, rows]
+                    b = jnp.where(tile_inside, b, jnp.zeros_like(b))
                     above = jnp.where(tile_odd == 1, a, b) if y == 0 else field[m, plane, y - 1, rows]
                     below = jnp.where(tile_odd == 1, b, a) if y == lines - 1 else field[m, plane, y + 1, rows]
                     dy.append(below - above)
@@ -135,22 +145,21 @@
                     for c in range(3):
                         light[e][c] = light[e][c] + lit * hue[c]
                     light[e][3] = light[e][3] + taken
-            base = group * (ROWS * kinds) + y
+            base = group * (ROWS * pitch) + y
             for e in range(energies):
                 for c in range(4):
                     value = light[e][c] * (1.0 / 255.0) if c < 3 else light[e][c]
-                    image[pl.ds(base + (c * energies + e) * lines, ROWS, stride=kinds), :] = value
+                    image[pl.ds(base + (c * energies + e) * lines, ROWS, stride=pitch), :] = value
         return 0
 
     lax.fori_loop(0, groups, chunk, 0)
 
     def part(pair, _):
         for target, parity in ((kept, depth_odd), (sent, 1 - depth_odd)):
-            start = pl.multiple_of((2 * pair + parity) * kinds, kinds)
-            target[pair] = image[pl.ds(start, kinds), :]
+            target[pair] = image[pl.ds((2 * pair + parity) * pitch, kinds), :]
         return 0
 
-    lax.fori_loop(0, blocks // 2, part, 0)
+    lax.fori_loop(0, blocks // 2, part, 0, unroll=True)
 
 
 FINE, COARSE, TOP, KNEE = 1500.0, 64.0, 32767.0, 40.0
@@ -257,7 +266,7 @@
         out_shape=(real(pairs, kinds, LANES),) * 2,
         in_specs=[vmem] * 8,
         out_specs=(vmem, vmem),
-        scratch_shapes=[pltpu.VMEM((blocks * kinds, LANES), jnp.float32)],
+        scratch_shapes=[pltpu.VMEM((blocks * (kinds + 1), LANES), jnp.float32)],
         compiler_params=limit(8),
         name="shade",
     )(half, hues, field, slope_x, depth_a, depth_b, tile_a, tile_b)

time: 36.8 us -> 34.4 us (0.935)
  blocking collectives: 17.8 us -> 15.6 us
  starting transfers between devices: 9.28 us -> 10.3 us
  Pallas kernels: 6.13 us -> 5.32 us
    ppermute x1, starting transfers between devices: 0.65 us -> 6.44 us  [body(): depth_b = lax.ppermute(plane_b, 'depth', partners('depth', 1))]
    ppermute x1, starting transfers between devices: 3.36 us -> 0.01 us  [body(): depth_a = lax.ppermute(send(False, plane_b), 'depth', partners('depth', 0))]
    all_to_all x1, blocking collectives: 17.8 us -> 15.6 us  [body(): lax.all_to_all(joined, 'depth', 0, 0, axis_index_groups=same_core, tiled=...]
    ppermute x1, starting transfers between devices: 4.87 us -> 3.04 us  [body(): tile_b = lax.ppermute(rows[1], 'tile', partners('tile', 1))]
    pallas_call x1, Pallas kernels: 3.16 us -> 2.63 us  [body(): pl.pallas_call(functools.partial(lookup, planes * depth), out_shape=(real...]
    ppermute x1, starting transfers between devices: 0.12 us -> 0.58 us  [body(): other = lax.ppermute(sent, 'depth', [(i, i ^ 1) for i in range(depth)])]
  transfers between devices with their start and end apart: 5 -> 5, of which waited for: 1 -> 1; matrix products, arithmetic and copies ran while one was open for 0% -> 0% of each run, Pallas kernels for 9% -> 8%
where the time goes in v7:
time: 34.4 us; the launch traced here: 33.8 us
  blocking collectives  15.6 us (45%)
  starting transfers between devices  10.3 us (30%)
  Pallas kernels  5.32 us (15%)
  local copies, waits for them, and re-layouts  1.34 us (4%)
  waiting for transfers between devices  1.17 us (3%)
    all_to_all x1, blocking collectives, body(): lax.all_to_all(joined, 'depth', 0, 0, axis_index_groups=same_core, tiled=...  15.6 us
    ppermute x1, starting transfers between devices, body(): depth_b = lax.ppermute(plane_b, 'depth', partners('depth', 1))  6.44 us
    ppermute x1, starting transfers between devices, body(): tile_b = lax.ppermute(rows[1], 'tile', partners('tile', 1))  3.04 us
    pallas_call x1, Pallas kernels, body(): pl.pallas_call(functools.partial(lookup, planes * depth), out_shape=(real...  2.63 us
    pallas_call x1, Pallas kernels, body(): pl.pallas_call(shade, out_shape=(real(pairs, kinds, LANES),) * 2, in_spec...  1.78 us
    reshape x1, local copies, waits for them, and re-layouts, body(): cells = density.reshape(mats, planes, lines, blocks, LANES)  1.29 us
    ppermute x1, waiting for transfers between devices, body(): other = lax.ppermute(sent, 'depth', [(i, i ^ 1) for i in range(depth)])  1.16 us
    pallas_call x1, Pallas kernels, body(): pl.pallas_call(composite, out_shape=real(energies, 4, lines, columns // d...  0.74 us
  transfers between devices with their start and end apart: 5, of which 1 were waited for; matrix products, arithmetic and copies ran while one was open for 0% of the time, Pallas kernels for 8%

profile of v7, /device:TPU:4, one launch (start us, length us, event | category | flops | bytes accessed | tf_op | source)
XLA Modules:
  0.0 33.8 jit_solution(8953924605161667359)
XLA Ops:
  0.0 1.3 %reshape.3.cells = bf16[3,8,2,32,128]{4,3,2,1,0:T(8,128)(2,1)S(1)} reshape(bf16[3,8,2,4096]{3,2,1,0:T(2,128)(2,1)} %param.3) | data formatting | bytes 786432 | tf_op jit(solution)/shard_map/reshape | solution.py:226
  1.3 0.0 copy-start
  1.3 0.0 copy-start.1
  1.4 3.0 %collective-permute-start.3 = (bf16[3,8,32,128]{3,2,1,0:T(8,128)(2,1)S(1)}, bf16[3,8,32,128]{3,2,1,0:T(8,128)(2,1)S(1)}, u32[]{:S(2)}, u32[]{:S(2)}) collective-permute-start(bf16[3,8,32,128]{3,2,1,0:T(8,128)(2,1)S(1)} %get-tuple-element.17.refs_1_), channel_id=1, source_target_pairs={{0,7},{7,0},{1,2},{2,1},{3,4},{4,3},{5,6},{6,5},{8,15},{15,8},{9,1... | collective-permute-start | bytes 589832 | tf_op jit(solution)/shard_map/ppermute | solution.py:229
  4.4 0.2 collective-permute-start.2
  4.6 6.4 %collective-permute-start.1 = (bf16[3,2,32,128]{3,2,1,0:T(8,128)(2,1)S(1)}, bf16[3,2,32,128]{3,2,1,0:T(8,128)(2,1)S(1)}, u32[]{:S(2)}, u32[]{:S(2)}) collective-permute-start(bf16[3,2,32,128]{3,2,1,0:T(8,128)(2,1)S(1)} %plane_to_send.2.refs_0_), channel_id=1, source_target_pairs={{0,248},{248,0},{8,16},{16,8},{24,32},{32,24},{40,48},{48,40},{56,... | collective-permute-start | bytes 147464 | tf_op jit(solution)/shard_map/ppermute | solution.py:243
  11.1 0.0 collective-permute-start
  11.1 0.0 copy-done
  11.1 0.0 copy-done.1
  11.1 2.6 %lookup.1 = (f32[8,8,16,8,128]{4,3,2,1,0:T(8,128)S(1)}, f32[3,8,2,32,128]{4,3,2,1,0:T(8,128)S(1)}, f32[3,8,2,32,128]{4,3,2,1,0:T(8,128)S(1)}, f32[12,8,128]{2,1,0:T(8,128)S(1)}) custom-call(f32[4,3]{1,0:T(4,128)S(1)} %copy-done.1, s32[4,4,256]{2,1,0:T(4,128)S(1)} %copy-done, bf16[3,8,2,32,128]{4,3,2,1,0:T(8,128)(2,1)S(1)} %reshape.3.cells), custom_call_target="tpu_custom_call" | custom-call | flops 4000000000 | bytes 8000000 | tf_op jit(solution)/shard_map/lookup/pallas_call | solution.py:245
  13.7 0.0 collective-permute-done.depth_a
  13.7 0.0 collective-permute-done.1.depth_b
  13.7 0.0 collective-permute-done.3.tile_b
  13.7 0.0 collective-permute-done.2.tile_a
  13.8 1.8 %shade.1 = (f32[16,32,128]{2,1,0:T(8,128)S(1)}, f32[16,32,128]{2,1,0:T(8,128)S(1)}) custom-call(f32[12,8,128]{2,1,0:T(8,128)S(1)} %get-tuple-element.11.half, f32[8,8,16,8,128]{4,3,2,1,0:T(8,128)S(1)} %get-tuple-element.12.hues, f32[3,8,2,32,128]{4,3,2,1,0:T(8,128)S(1)} %get-tuple-element.13.field, f32[3,8,2,32,128]{4,3,2,1,0:T(8,128)S(1)} %get-tuple-element.14.slope_x, ...), custom_call_target="tpu_custom_call" | custom-call | tf_op jit(solution)/shard_map/shade/pallas_call | solution.py:264
  15.5 0.6 %collective-permute-start.4 = (f32[16,32,128]{2,1,0:T(8,128)S(1)}, f32[16,32,128]{2,1,0:T(8,128)S(1)}, u32[]{:S(2)}, u32[]{:S(2)}) collective-permute-start(f32[16,32,128]{2,1,0:T(8,128)S(1)} %get-tuple-element.16), channel_id=1, source_target_pairs={{0,8},{8,0},{16,24},{24,16},{32,40},{40,32},{48,56},{56,48},{64,72... | collective-permute-start | bytes 786440 | tf_op jit(solution)/shard_map/ppermute | solution.py:273
  16.1 1.2 %collective-permute-done.4.other = f32[16,32,128]{2,1,0:T(8,128)S(1)} collective-permute-done((f32[16,32,128]{2,1,0:T(8,128)S(1)}, f32[16,32,128]{2,1,0:T(8,128)S(1)}, u32[]{:S(2)}, u32[]{:S(2)}) %collective-permute-start.4) | collective-permute-done | bytes 262176 | tf_op jit(solution)/shard_map/ppermute | solution.py:273
  17.3 0.2 join.1
  17.5 15.6 %all_to_all.5.parts = s16[16,32,128]{2,1,0:T(8,128)(2,1)S(1)} all-to-all(s16[16,32,128]{2,1,0:T(8,128)(2,1)S(1)} %join.1), channel_id=1, replica_groups={{0,16,32,48,64,80,96,112,128,144,160,176,192,208,224,240},{8,24,40,56,7..., dimensions={0} | all-to-all | bytes 262144 | tf_op jit(solution)/shard_map/all_to_all | solution.py:283
  33.0 0.7 %composite.1 = f32[4,4,2,128]{3,2,1,0:T(2,128)} custom-call(s16[16,32,128]{2,1,0:T(8,128)(2,1)S(1)} %all_to_all.5.parts), custom_call_target="tpu_custom_call" | custom-call | tf_op jit(solution)/shard_map/composite/pallas_call | solution.py:284
  (3 shorter events, 0.0 us)
Async XLA Ops:
  1.3 9.8 %copy-start = (s32[4,4,256]{2,1,0:T(4,128)S(1)}, s32[4,4,256]{2,1,0:T(4,128)}, u32[]{:S(2)}) copy-start(s32[4,4,256]{2,1,0:T(4,128)} %color_table.1) | copy-start | bytes 49156
  1.3 9.8 %copy-start.1 = (f32[4,3]{1,0:T(4,128)S(1)}, f32[4,3]{1,0:T(4,128)}, u32[]{:S(2)}) copy-start(f32[4,3]{1,0:T(4,128)} %weight.1) | copy-start | bytes 148
  1.4 12.4 %collective-permute-start.3 = (bf16[3,8,32,128]{3,2,1,0:T(8,128)(2,1)S(1)}, bf16[3,8,32,128]{3,2,1,0:T(8,128)(2,1)S(1)}, u32[]{:S(2)}, u32[]{:S(2)}) collective-permute-start(bf16[3,8,32,128]{3,2,1,0:T(8,128)(2,1)S(1)} %get-tuple-element.17.refs_1_), channel_id=1, source_target_pairs={{0,7},{7,0},{1,2},{2,1},{3,4},{4,3},{5,6},{6,5},{8,15},{15,8},{9,1... | collective-permute-start | bytes 589832 | tf_op jit(solution)/shard_map/ppermute | solution.py:229
  4.4 9.3 %collective-permute-start.2 = (bf16[3,8,32,128]{3,2,1,0:T(8,128)(2,1)S(1)}, bf16[3,8,32,128]{3,2,1,0:T(8,128)(2,1)S(1)}, u32[]{:S(2)}, u32[]{:S(2)}) collective-permute-start(bf16[3,8,32,128]{3,2,1,0:T(8,128)(2,1)S(1)} %get-tuple-element.18.refs_0_), channel_id=1, source_target_pairs={{0,1},{1,0},{2,3},{3,2},{4,5},{5,4},{6,7},{7,6},{8,9},{9,8},{10,11... | collective-permute-start | bytes 589832 | tf_op jit(solution)/shard_map/ppermute | solution.py:228
  4.6 9.1 %collective-permute-start.1 = (bf16[3,2,32,128]{3,2,1,0:T(8,128)(2,1)S(1)}, bf16[3,2,32,128]{3,2,1,0:T(8,128)(2,1)S(1)}, u32[]{:S(2)}, u32[]{:S(2)}) collective-permute-start(bf16[3,2,32,128]{3,2,1,0:T(8,128)(2,1)S(1)} %plane_to_send.2.refs_0_), channel_id=1, source_target_pairs={{0,248},{248,0},{8,16},{16,8},{24,32},{32,24},{40,48},{48,40},{56,... | collective-permute-start | bytes 147464 | tf_op jit(solution)/shard_map/ppermute | solution.py:243
  11.1 2.7 %collective-permute-start = (bf16[3,2,32,128]{3,2,1,0:T(8,128)(2,1)S(1)}, bf16[3,2,32,128]{3,2,1,0:T(8,128)(2,1)S(1)}, u32[]{:S(2)}, u32[]{:S(2)}) collective-permute-start(bf16[3,2,32,128]{3,2,1,0:T(8,128)(2,1)S(1)} %plane_to_send.3), channel_id=1, source_target_pairs={{0,8},{8,0},{16,24},{24,16},{32,40},{40,32},{48,56},{56,48},{64,72... | collective-permute-start | bytes 147464 | tf_op jit(solution)/shard_map/ppermute | solution.py:244
  15.5 1.7 %collective-permute-start.4 = (f32[16,32,128]{2,1,0:T(8,128)S(1)}, f32[16,32,128]{2,1,0:T(8,128)S(1)}, u32[]{:S(2)}, u32[]{:S(2)}) collective-permute-start(f32[16,32,128]{2,1,0:T(8,128)S(1)} %get-tuple-element.16), channel_id=1, source_target_pairs={{0,8},{8,0},{16,24},{24,16},{32,40},{40,32},{48,56},{56,48},{64,72... | collective-permute-start | bytes 786440 | tf_op jit(solution)/shard_map/ppermute | solution.py:273

commit v8 on v7

--- a/solution.py
+++ b/solution.py
@@ -12,10 +12,22 @@
 ROWS = 8
 
 
+AXES = ("depth", "tile")
+
+
 def partners(axis, start):
-    count = lax.axis_size(axis)
-    ends = [(0, count - 1), (count - 1, 0)] if start else []
-    return ends + [p for i in range(start, count - 1, 2) for p in ((i, i + 1), (i + 1, i))]
+    depth, tile = (lax.axis_size(name) for name in AXES)
+    pairs = []
+    for d in range(depth):
+        for t in range(tile):
+            place, count = (d, depth) if axis == "depth" else (t, tile)
+            other = place + 1 if (place - start) % 2 == 0 else place - 1
+            if 0 <= other < count:
+                to = (other, t) if axis == "depth" else (d, other)
+            else:
+                to = (d, t ^ 1) if axis == "depth" else (d ^ 1, t)
+            pairs.append((d * tile + t, to[0] * tile + to[1]))
+    return pairs
 
 
 def inside(axis):
@@ -225,8 +237,8 @@
 
     cells = density.reshape(mats, planes, lines, blocks, LANES)
     rows = [lax.dynamic_index_in_dim(cells, end("tile", high, lines - 1), 2, keepdims=False) for high in (False, True)]
-    tile_a = lax.ppermute(rows[0], "tile", partners("tile", 0))
-    tile_b = lax.ppermute(rows[1], "tile", partners("tile", 1))
+    tile_a = lax.ppermute(rows[0], AXES, partners("tile", 0))
+    tile_b = lax.ppermute(rows[1], AXES, partners("tile", 1))
 
     def send(high, *before):
         return pl.pallas_call(
@@ -240,8 +252,8 @@
         )(cells, *before)
 
     plane_b = send(True, *rows)
-    depth_b = lax.ppermute(plane_b, "depth", partners("depth", 1))
-    depth_a = lax.ppermute(send(False, plane_b), "depth", partners("depth", 0))
+    depth_b = lax.ppermute(plane_b, AXES, partners("depth", 1))
+    depth_a = lax.ppermute(send(False, plane_b), AXES, partners("depth", 0))
     hues, field, slope_x, half = pl.pallas_call(
         functools.partial(lookup, planes * depth),
         out_shape=(

time: 34.4 us -> 34.2 us (level)
  starting transfers between devices: 10.3 us -> 5.36 us
  waiting for transfers between devices: 1.17 us -> 3.94 us
  blocking collectives: 15.6 us -> 17.8 us
    ppermute x4, starting transfers between devices: 9.68 us -> 5.27 us  [the longest x1 3.04 us: body(): tile_b = lax.ppermute(rows[1], AXES, partners('tile', 1))]
    ppermute x4, waiting for transfers between devices: 0.01 us -> 2.42 us  [the longest x1 2 us: body(): depth_b = lax.ppermute(plane_b, AXES, partners('depth', 1))]
    all_to_all x1, blocking collectives: 15.6 us -> 17.8 us  [body(): lax.all_to_all(joined, 'depth', 0, 0, axis_index_groups=same_core, tiled=...]
    ppermute x1, starting transfers between devices: 0.58 us -> 0.09 us  [body(): other = lax.ppermute(sent, 'depth', [(i, i ^ 1) for i in range(depth)])]
    ppermute x1, waiting for transfers between devices: 1.16 us -> 1.52 us  [body(): other = lax.ppermute(sent, 'depth', [(i, i ^ 1) for i in range(depth)])]
  transfers between devices with their start and end apart: 5 -> 5, of which waited for: 1 -> 3; matrix products, arithmetic and copies ran while one was open for 0% -> 0% of each run, Pallas kernels for 8% -> 8%
where the time goes in v8:
time: 34.2 us; the launch traced here: 33.8 us
  blocking collectives  17.8 us (52%)
  starting transfers between devices  5.36 us (16%)
  Pallas kernels  5.3 us (15%)
  waiting for transfers between devices  3.94 us (12%)
  local copies, waits for them, and re-layouts  1.34 us (4%)
    all_to_all x1, blocking collectives, body(): lax.all_to_all(joined, 'depth', 0, 0, axis_index_groups=same_core, tiled=...  17.8 us
    ppermute x1, starting transfers between devices, body(): tile_b = lax.ppermute(rows[1], AXES, partners('tile', 1))  3.04 us
    pallas_call x1, Pallas kernels, body(): pl.pallas_call(functools.partial(lookup, planes * depth), out_shape=(real...  2.63 us
    ppermute x1, waiting for transfers between devices, body(): depth_b = lax.ppermute(plane_b, AXES, partners('depth', 1))  2 us
    ppermute x1, starting transfers between devices, body(): depth_b = lax.ppermute(plane_b, AXES, partners('depth', 1))  1.83 us
    pallas_call x1, Pallas kernels, body(): pl.pallas_call(shade, out_shape=(real(pairs, kinds, LANES),) * 2, in_spec...  1.76 us
    ppermute x1, waiting for transfers between devices, body(): other = lax.ppermute(sent, 'depth', [(i, i ^ 1) for i in range(depth)])  1.52 us
    reshape x1, local copies, waits for them, and re-layouts, body(): cells = density.reshape(mats, planes, lines, blocks, LANES)  1.29 us
  transfers between devices with their start and end apart: 5, of which 3 were waited for; matrix products, arithmetic and copies ran while one was open for 0% of the time, Pallas kernels for 8%

profile of v8, /device:TPU:4, one launch (start us, length us, event | category | flops | bytes accessed | tf_op | source)
XLA Modules:
  0.0 33.8 jit_solution(10684200416987633096)
XLA Ops:
  0.0 1.3 %reshape.3.cells = bf16[3,8,2,32,128]{4,3,2,1,0:T(8,128)(2,1)S(1)} reshape(bf16[3,8,2,4096]{3,2,1,0:T(2,128)(2,1)} %param.3) | data formatting | bytes 786432 | tf_op jit(solution)/shard_map/reshape | solution.py:238
  1.3 0.0 copy-start
  1.3 0.0 copy-start.1
  1.4 3.0 %collective-permute-start.3 = (bf16[3,8,32,128]{3,2,1,0:T(8,128)(2,1)S(1)}, bf16[3,8,32,128]{3,2,1,0:T(8,128)(2,1)S(1)}, u32[]{:S(2)}, u32[]{:S(2)}) collective-permute-start(bf16[3,8,32,128]{3,2,1,0:T(8,128)(2,1)S(1)} %get-tuple-element.17.refs_1_), channel_id=1, source_target_pairs={{0,8},{1,2},{2,1},{3,4},{4,3},{5,6},{6,5},{7,15},{8,0},{9,10},{10,... | collective-permute-start | bytes 589832 | tf_op jit(solution)/shard_map/ppermute | solution.py:241
  4.4 0.2 collective-permute-start.2
  4.6 1.8 %collective-permute-start.1 = (bf16[3,2,32,128]{3,2,1,0:T(8,128)(2,1)S(1)}, bf16[3,2,32,128]{3,2,1,0:T(8,128)(2,1)S(1)}, u32[]{:S(2)}, u32[]{:S(2)}) collective-permute-start(bf16[3,2,32,128]{3,2,1,0:T(8,128)(2,1)S(1)} %plane_to_send.2.refs_0_), channel_id=1, source_target_pairs={{0,1},{1,0},{2,3},{3,2},{4,5},{5,4},{6,7},{7,6},{8,16},{9,17},{10,... | collective-permute-start | bytes 147464 | tf_op jit(solution)/shard_map/ppermute | solution.py:255
  6.5 0.2 collective-permute-start
  6.7 0.0 copy-done
  6.7 0.0 copy-done.1
  6.7 2.6 %lookup.1 = (f32[8,8,16,8,128]{4,3,2,1,0:T(8,128)S(1)}, f32[3,8,2,32,128]{4,3,2,1,0:T(8,128)S(1)}, f32[3,8,2,32,128]{4,3,2,1,0:T(8,128)S(1)}, f32[12,8,128]{2,1,0:T(8,128)S(1)}) custom-call(f32[4,3]{1,0:T(4,128)S(1)} %copy-done.1, s32[4,4,256]{2,1,0:T(4,128)S(1)} %copy-done, bf16[3,8,2,32,128]{4,3,2,1,0:T(8,128)(2,1)S(1)} %reshape.3.cells), custom_call_target="tpu_custom_call" | custom-call | flops 4000000000 | bytes 8000000 | tf_op jit(solution)/shard_map/lookup/pallas_call | solution.py:257
  9.3 0.0 collective-permute-done.depth_a
  9.3 2.0 %collective-permute-done.1.depth_b = bf16[3,2,32,128]{3,2,1,0:T(8,128)(2,1)S(1)} collective-permute-done((bf16[3,2,32,128]{3,2,1,0:T(8,128)(2,1)S(1)}, bf16[3,2,32,128]{3,2,1,0:T(8,128)(2,1)S(1)}, u32[]{:S(2)}, u32[]{:S(2)}) %collective-permute-start.1) | collective-permute-done | bytes 49184 | tf_op jit(solution)/shard_map/ppermute | solution.py:255
  11.3 0.4 %collective-permute-done.3.tile_b = bf16[3,8,32,128]{3,2,1,0:T(8,128)(2,1)S(1)} collective-permute-done((bf16[3,8,32,128]{3,2,1,0:T(8,128)(2,1)S(1)}, bf16[3,8,32,128]{3,2,1,0:T(8,128)(2,1)S(1)}, u32[]{:S(2)}, u32[]{:S(2)}) %collective-permute-start.3) | collective-permute-done | bytes 196640 | tf_op jit(solution)/shard_map/ppermute | solution.py:241
  11.7 0.0 collective-permute-done.2.tile_a
  11.7 1.8 %shade.1 = (f32[16,32,128]{2,1,0:T(8,128)S(1)}, f32[16,32,128]{2,1,0:T(8,128)S(1)}) custom-call(f32[12,8,128]{2,1,0:T(8,128)S(1)} %get-tuple-element.11.half, f32[8,8,16,8,128]{4,3,2,1,0:T(8,128)S(1)} %get-tuple-element.12.hues, f32[3,8,2,32,128]{4,3,2,1,0:T(8,128)S(1)} %get-tuple-element.13.field, f32[3,8,2,32,128]{4,3,2,1,0:T(8,128)S(1)} %get-tuple-element.14.slope_x, ...), custom_call_target="tpu_custom_call" | custom-call | tf_op jit(solution)/shard_map/shade/pallas_call | solution.py:276
  13.5 0.1 collective-permute-start.4
  13.6 1.5 %collective-permute-done.4.other = f32[16,32,128]{2,1,0:T(8,128)S(1)} collective-permute-done((f32[16,32,128]{2,1,0:T(8,128)S(1)}, f32[16,32,128]{2,1,0:T(8,128)S(1)}, u32[]{:S(2)}, u32[]{:S(2)}) %collective-permute-start.4) | collective-permute-done | bytes 262176 | tf_op jit(solution)/shard_map/ppermute | solution.py:285
  15.1 0.2 join.1
  15.3 17.8 %all_to_all.5.parts = s16[16,32,128]{2,1,0:T(8,128)(2,1)S(1)} all-to-all(s16[16,32,128]{2,1,0:T(8,128)(2,1)S(1)} %join.1), channel_id=1, replica_groups={{0,16,32,48,64,80,96,112,128,144,160,176,192,208,224,240},{8,24,40,56,7..., dimensions={0} | all-to-all | bytes 262144 | tf_op jit(solution)/shard_map/all_to_all | solution.py:295
  33.0 0.7 %composite.1 = f32[4,4,2,128]{3,2,1,0:T(2,128)} custom-call(s16[16,32,128]{2,1,0:T(8,128)(2,1)S(1)} %all_to_all.5.parts), custom_call_target="tpu_custom_call" | custom-call | tf_op jit(solution)/shard_map/composite/pallas_call | solution.py:296
  (3 shorter events, 0.0 us)
Async XLA Ops:
  1.3 5.4 %copy-start = (s32[4,4,256]{2,1,0:T(4,128)S(1)}, s32[4,4,256]{2,1,0:T(4,128)}, u32[]{:S(2)}) copy-start(s32[4,4,256]{2,1,0:T(4,128)} %color_table.1) | copy-start | bytes 49156
  1.3 5.4 %copy-start.1 = (f32[4,3]{1,0:T(4,128)S(1)}, f32[4,3]{1,0:T(4,128)}, u32[]{:S(2)}) copy-start(f32[4,3]{1,0:T(4,128)} %weight.1) | copy-start | bytes 148
  1.4 10.3 %collective-permute-start.3 = (bf16[3,8,32,128]{3,2,1,0:T(8,128)(2,1)S(1)}, bf16[3,8,32,128]{3,2,1,0:T(8,128)(2,1)S(1)}, u32[]{:S(2)}, u32[]{:S(2)}) collective-permute-start(bf16[3,8,32,128]{3,2,1,0:T(8,128)(2,1)S(1)} %get-tuple-element.17.refs_1_), channel_id=1, source_target_pairs={{0,8},{1,2},{2,1},{3,4},{4,3},{5,6},{6,5},{7,15},{8,0},{9,10},{10,... | collective-permute-start | bytes 589832 | tf_op jit(solution)/shard_map/ppermute | solution.py:241
  4.4 7.3 %collective-permute-start.2 = (bf16[3,8,32,128]{3,2,1,0:T(8,128)(2,1)S(1)}, bf16[3,8,32,128]{3,2,1,0:T(8,128)(2,1)S(1)}, u32[]{:S(2)}, u32[]{:S(2)}) collective-permute-start(bf16[3,8,32,128]{3,2,1,0:T(8,128)(2,1)S(1)} %get-tuple-element.18.refs_0_), channel_id=1, source_target_pairs={{0,1},{1,0},{2,3},{3,2},{4,5},{5,4},{6,7},{7,6},{8,9},{9,8},{10,11... | collective-permute-start | bytes 589832 | tf_op jit(solution)/shard_map/ppermute | solution.py:240
  4.6 6.7 %collective-permute-start.1 = (bf16[3,2,32,128]{3,2,1,0:T(8,128)(2,1)S(1)}, bf16[3,2,32,128]{3,2,1,0:T(8,128)(2,1)S(1)}, u32[]{:S(2)}, u32[]{:S(2)}) collective-permute-start(bf16[3,2,32,128]{3,2,1,0:T(8,128)(2,1)S(1)} %plane_to_send.2.refs_0_), channel_id=1, source_target_pairs={{0,1},{1,0},{2,3},{3,2},{4,5},{5,4},{6,7},{7,6},{8,16},{9,17},{10,... | collective-permute-start | bytes 147464 | tf_op jit(solution)/shard_map/ppermute | solution.py:255
  6.5 2.8 %collective-permute-start = (bf16[3,2,32,128]{3,2,1,0:T(8,128)(2,1)S(1)}, bf16[3,2,32,128]{3,2,1,0:T(8,128)(2,1)S(1)}, u32[]{:S(2)}, u32[]{:S(2)}) collective-permute-start(bf16[3,2,32,128]{3,2,1,0:T(8,128)(2,1)S(1)} %plane_to_send.3), channel_id=1, source_target_pairs={{0,8},{1,9},{2,10},{3,11},{4,12},{5,13},{6,14},{7,15},{8,0},{9,1},... | collective-permute-start | bytes 147464 | tf_op jit(solution)/shard_map/ppermute | solution.py:256
  13.5 1.6 %collective-permute-start.4 = (f32[16,32,128]{2,1,0:T(8,128)S(1)}, f32[16,32,128]{2,1,0:T(8,128)S(1)}, u32[]{:S(2)}, u32[]{:S(2)}) collective-permute-start(f32[16,32,128]{2,1,0:T(8,128)S(1)} %get-tuple-element.16), channel_id=1, source_target_pairs={{0,8},{8,0},{16,24},{24,16},{32,40},{40,32},{48,56},{56,48},{64,72... | collective-permute-start | bytes 786440 | tf_op jit(solution)/shard_map/ppermute | solution.py:285

commit v9 on v8

--- a/solution.py
+++ b/solution.py
@@ -112,66 +112,68 @@
     lax.fori_loop(0, planes * lines, line, 0, unroll=4)
 
 
-def shade(half, hues, field, slope_x, depth_a, depth_b, tile_a, tile_b, kept, sent, image):
+def shade(second, half, hues, field, slope_x, depth_a, depth_b, halo, *refs):
+    image = refs[-1]
     mats, planes, lines, blocks, _ = field.shape
     energies = half.shape[0] // mats
     groups = blocks // ROWS
-    kinds = 4 * energies * lines
+    kinds = 4 * energies
     pitch = image.shape[0] // blocks
     tile_odd, depth_odd = lax.axis_index("tile") % 2, lax.axis_index("depth") % 2
-    tile_inside, depth_inside = inside("tile"), inside("depth")
+    below = tile_odd if second else 1 - tile_odd
+    here, beside = below, 1 - below
+    sign = jnp.where(below == 1, 1.0, -1.0)
+    halo_inside, depth_inside = inside("tile") if second else True, inside("depth")
 
     def chunk(group, _):
         rows = pl.ds(pl.multiple_of(group * ROWS, ROWS), ROWS)
-        for y in range(lines):
-            light = [[jnp.zeros((ROWS, LANES), jnp.float32) for _ in range(4)] for _ in range(energies)]
-            keep = [jnp.ones((ROWS, LANES), jnp.float32) for _ in range(energies)]
-            near, far = [], []
+        light = [[jnp.zeros((ROWS, LANES), jnp.float32) for _ in range(4)] for _ in range(energies)]
+        keep = [jnp.ones((ROWS, LANES), jnp.float32) for _ in range(energies)]
+        near, far = [], []
+        for m in range(mats):
+            a, b = depth_a[m, here, rows], depth_b[m, here, rows]
+            b = jnp.where(depth_inside, b, jnp.zeros_like(b))
+            near.append(jnp.where(depth_odd == 1, a, b))
+            far.append(jnp.where(depth_odd == 1, b, a))
+        for plane in range(planes):
+            dx, dy, dz = [], [], []
             for m in range(mats):
-                a, b = depth_a[m, y, rows], depth_b[m, y, rows]
-                b = jnp.where(depth_inside, b, jnp.zeros_like(b))
-                near.append(jnp.where(depth_odd == 1, a, b))
-                far.append(jnp.where(depth_odd == 1, b, a))
-            for plane in range(planes):
-                dx, dy, dz = [], [], []
-                for m in range(mats):
-                    before = near[m] if plane == 0 else field[m, plane - 1, y, rows]
-                    after = far[m] if plane == planes - 1 else field[m, plane + 1, y, rows]
-                    dz.append(after - before)
-                    a, b = tile_a[m, plane, rows], tile_b[m, plane, rows]
-                    b = jnp.where(tile_inside, b, jnp.zeros_like(b))
-                    above = jnp.where(tile_odd == 1, a, b) if y == 0 else field[m, plane, y - 1, rows]
-                    below = jnp.where(tile_odd == 1, b, a) if y == lines - 1 else field[m, plane, y + 1, rows]
-                    dy.append(below - above)
-                    dx.append(slope_x[m, plane, y, rows])
-                for e in range(energies):
-                    share = [half[mats * e + m] for m in range(mats)]
-                    grad_z, grad_y, grad_x = mix(share, dz), mix(share, dy), mix(share, dx)
-                    slope_sq = grad_z * grad_z + grad_y * grad_y + grad_x * grad_x
-                    root = lax.rsqrt(slope_sq + 1.0)
-                    shading = 0.3 + jnp.abs(0.56 * grad_z + 0.336 * grad_y + 0.252 * grad_x) * root
-                    hue = [hues[plane, y * groups + group, 4 * e + c] for c in range(4)]
-                    taken = keep[e] * (hue[3] * (slope_sq * (root * root)))
-                    keep[e] = keep[e] - taken
-                    lit = taken * shading
-                    for c in range(3):
-                        light[e][c] = light[e][c] + lit * hue[c]
-                    light[e][3] = light[e][3] + taken
-            base = group * (ROWS * pitch) + y
+                before = near[m] if plane == 0 else field[m, plane - 1, here, rows]
+                after = far[m] if plane == planes - 1 else field[m, plane + 1, here, rows]
+                dz.append(after - before)
+                outer = halo[m, plane, rows]
+                if second:
+                    outer = jnp.where(halo_inside, outer, jnp.zeros_like(outer))
+                dy.append((outer - field[m, plane, beside, rows]) * sign)
+                dx.append(slope_x[m, plane, here, rows])
             for e in range(energies):
-                for c in range(4):
-                    value = light[e][c] * (1.0 / 255.0) if c < 3 else light[e][c]
-                    image[pl.ds(base + (c * energies + e) * lines, ROWS, stride=pitch), :] = value
+                share = [half[mats * e + m] for m in range(mats)]
+                grad_z, grad_y, grad_x = mix(share, dz), mix(share, dy), mix(share, dx)
+                slope_sq = grad_z * grad_z + grad_y * grad_y + grad_x * grad_x
+                root = lax.rsqrt(slope_sq + 1.0)
+                shading = 0.3 + jnp.abs(0.56 * grad_z + 0.336 * grad_y + 0.252 * grad_x) * root
+                hue = [hues[plane, here * groups + group, 4 * e + c] for c in range(4)]
+                taken = keep[e] * (hue[3] * (slope_sq * (root * root)))
+                keep[e] = keep[e] - taken
+                lit = taken * shading
+                for c in range(3):
+                    light[e][c] = light[e][c] + lit * hue[c]
+                light[e][3] = light[e][3] + taken
+        for e in range(energies):
+            for c in range(4):
+                value = light[e][c] * (1.0 / 255.0) if c < 3 else light[e][c]
+                image[pl.ds(group * (ROWS * pitch) + c * energies + e, ROWS, stride=pitch), :] = value
         return 0
 
     lax.fori_loop(0, groups, chunk, 0)
 
-    def part(pair, _):
-        for target, parity in ((kept, depth_odd), (sent, 1 - depth_odd)):
-            target[pair] = image[pl.ds((2 * pair + parity) * pitch, kinds), :]
-        return 0
-
-    lax.fori_loop(0, blocks // 2, part, 0, unroll=True)
+    if second:
+        first_image, kept, sent, _ = refs
+        for pair in range(blocks // 2):
+            for target, parity in ((kept, depth_odd), (sent, 1 - depth_odd)):
+                rows = pl.ds((2 * pair + parity) * pitch, kinds)
+                target[pair, :kinds] = first_image[rows, :]
+                target[pair, kinds:] = image[rows, :]
 
 
 FINE, COARSE, TOP, KNEE = 1500.0, 64.0, 32767.0, 40.0
@@ -193,31 +195,45 @@
     return jnp.where(code > NOTHING, jnp.exp2(octave), 0.0)
 
 
+def opacity(value, per):
+    last = value[2 * per :]
+    row = lax.broadcasted_iota(jnp.int32, last.shape, 0)
+    return jnp.where(row < per, pltpu.roll(last, per, 0), last)
+
+
 def join(per, mine, other, out):
     odd = lax.axis_index("depth") % 2
     for pair in range(mine.shape[0]):
         a, b = mine[pair], other[pair]
         front, back = jnp.where(odd == 0, a, b), jnp.where(odd == 0, b, a)
-        clear = 1.0 - front[-per:, :]
-        both = [front[i : i + per, :] + clear * back[i : i + per, :] for i in range(0, front.shape[0], per)]
+        both = []
+        for line in range(0, front.shape[0], 4 * per):
+            clear = 1.0 - opacity(front[line : line + 4 * per], per)
+            for i in range(line, line + 4 * per, 2 * per):
+                both.append(front[i : i + 2 * per] + clear * back[i : i + 2 * per])
         out[pair] = encode(jnp.concatenate(both, axis=0))
 
 
 def composite(parts, out):
     bricks, kinds, _ = parts.shape
     energies, channels, lines, _ = out.shape
-    per = kinds // channels
-
-    keep = jnp.ones((per, LANES), jnp.float32)
-    total = [jnp.zeros((per, LANES), jnp.float32) for _ in range(channels)]
+    each = channels * energies
+
+    keep = [jnp.ones((2 * energies, LANES), jnp.float32) for _ in range(lines)]
+    total = [[jnp.zeros((2 * energies, LANES), jnp.float32) for _ in range(2)] for _ in range(lines)]
     for brick in range(bricks):
         part = decode(parts[brick])
-        for c in range(channels):
-            total[c] = total[c] + keep * part[c * per : (c + 1) * per, :]
-        keep = keep * (1.0 - part[(channels - 1) * per :, :])
+        for k in range(lines):
+            line = part[k * each : (k + 1) * each]
+            for i in range(2):
+                total[k][i] = total[k][i] + keep[k] * line[2 * energies * i : 2 * energies * (i + 1)]
+            keep[k] = keep[k] * (1.0 - opacity(line, energies))
+    odd = lax.axis_index("tile") % 2
+    upper, lower = ([jnp.where(odd == at, *halves) for halves in zip(*total)] for at in (1, 0))
     for c in range(channels):
         for e in range(energies):
-            out[e, c] = total[c][e * lines : (e + 1) * lines, :]
+            row = (c % 2) * energies + e
+            out[e, c] = jnp.concatenate([upper[c // 2][row : row + 1], lower[c // 2][row : row + 1]], axis=0)
 
 
 def limit(mib):
@@ -273,18 +289,30 @@
         cost_estimate=pl.CostEstimate(flops=4_000_000_000, bytes_accessed=8_000_000, transcendentals=300_000),
         name="lookup",
     )(material_weight, color_table, cells)
+    half_kinds = 4 * energies
+    tall = real(blocks * (half_kinds + 1), LANES)
+    shared = (half, hues, field, slope_x, depth_a, depth_b)
+    first_image = pl.pallas_call(
+        functools.partial(shade, False),
+        out_shape=tall,
+        in_specs=[vmem] * 7,
+        out_specs=vmem,
+        compiler_params=limit(8),
+        cost_estimate=pl.CostEstimate(flops=2_000_000_000, bytes_accessed=4_000_000, transcendentals=100_000),
+        name="shade_first",
+    )(*shared, tile_a)
     kept, sent = pl.pallas_call(
-        shade,
+        functools.partial(shade, True),
         out_shape=(real(pairs, kinds, LANES),) * 2,
         in_specs=[vmem] * 8,
         out_specs=(vmem, vmem),
-        scratch_shapes=[pltpu.VMEM((blocks * (kinds + 1), LANES), jnp.float32)],
+        scratch_shapes=[pltpu.VMEM(tall.shape, jnp.float32)],
         compiler_params=limit(8),
-        name="shade",
-    )(half, hues, field, slope_x, depth_a, depth_b, tile_a, tile_b)
+        name="shade_second",
+    )(*shared, tile_b, first_image)
     other = lax.ppermute(sent, "depth", [(i, i ^ 1) for i in range(depth)])
     joined = pl.pallas_call(
-        functools.partial(join, energies * lines),
+        functools.partial(join, energies),
         out_shape=jax.ShapeDtypeStruct((pairs, kinds, LANES), jnp.int16),
         in_specs=[vmem, vmem],
         out_specs=vmem,

time: 34.2 us -> 33.9 us (level)
  waiting for transfers between devices: 3.94 us -> 3.53 us
    ppermute x1, waiting for transfers between devices: 0.41 us -> 0.01 us  [body(): tile_b = lax.ppermute(rows[1], AXES, partners('tile', 1))]
    all_to_all x1, blocking collectives: 17.8 us -> 18.1 us  [body(): lax.all_to_all(joined, 'depth', 0, 0, axis_index_groups=same_core, tiled=...]
    pallas_call x2 -> x3, Pallas kernels: 1.92 us -> 1.95 us  [the longest x1 0.92 us: body(): pl.pallas_call(functools.partial(shade, True), out_shape=(real(pairs, kin...]
  transfers between devices with their start and end apart: 5 -> 5, of which waited for: 3 -> 2; matrix products, arithmetic and copies ran while one was open for 0% -> 0% of each run, Pallas kernels for 8% -> 10%
where the time goes in v9:
time: 33.9 us; the launch traced here: 33.8 us
  blocking collectives  18.1 us (53%)
  starting transfers between devices  5.36 us (16%)
  Pallas kernels  5.35 us (16%)
  waiting for transfers between devices  3.53 us (10%)
  local copies, waits for them, and re-layouts  1.34 us (4%)
    all_to_all x1, blocking collectives, body(): lax.all_to_all(joined, 'depth', 0, 0, axis_index_groups=same_core, tiled=...  18.1 us
    ppermute x1, starting transfers between devices, body(): tile_b = lax.ppermute(rows[1], AXES, partners('tile', 1))  3.04 us
    pallas_call x1, Pallas kernels, body(): pl.pallas_call(functools.partial(lookup, planes * depth), out_shape=(real...  2.63 us
    ppermute x1, waiting for transfers between devices, body(): depth_b = lax.ppermute(plane_b, AXES, partners('depth', 1))  2 us
    ppermute x1, starting transfers between devices, body(): depth_b = lax.ppermute(plane_b, AXES, partners('depth', 1))  1.83 us
    ppermute x1, waiting for transfers between devices, body(): other = lax.ppermute(sent, 'depth', [(i, i ^ 1) for i in range(depth)])  1.52 us
    reshape x1, local copies, waits for them, and re-layouts, body(): cells = density.reshape(mats, planes, lines, blocks, LANES)  1.29 us
    pallas_call x1, Pallas kernels, body(): pl.pallas_call(functools.partial(shade, True), out_shape=(real(pairs, kin...  0.92 us
  transfers between devices with their start and end apart: 5, of which 2 were waited for; matrix products, arithmetic and copies ran while one was open for 0% of the time, Pallas kernels for 10%

profile of v9, /device:TPU:4, one launch (start us, length us, event | category | flops | bytes accessed | tf_op | source)
XLA Modules:
  0.0 33.8 jit_solution(17762282428640900375)
XLA Ops:
  0.0 1.3 %reshape.3.cells = bf16[3,8,2,32,128]{4,3,2,1,0:T(8,128)(2,1)S(1)} reshape(bf16[3,8,2,4096]{3,2,1,0:T(2,128)(2,1)} %param.3) | data formatting | bytes 786432 | tf_op jit(solution)/shard_map/reshape | solution.py:254
  1.3 0.0 copy-start
  1.3 0.0 copy-start.1
  1.4 3.0 %collective-permute-start.2 = (bf16[3,8,32,128]{3,2,1,0:T(8,128)(2,1)S(1)}, bf16[3,8,32,128]{3,2,1,0:T(8,128)(2,1)S(1)}, u32[]{:S(2)}, u32[]{:S(2)}) collective-permute-start(bf16[3,8,32,128]{3,2,1,0:T(8,128)(2,1)S(1)} %get-tuple-element.17.refs_1_), channel_id=1, source_target_pairs={{0,8},{1,2},{2,1},{3,4},{4,3},{5,6},{6,5},{7,15},{8,0},{9,10},{10,... | collective-permute-start | bytes 589832 | tf_op jit(solution)/shard_map/ppermute | solution.py:257
  4.4 0.2 collective-permute-start.3
  4.6 1.8 %collective-permute-start.1 = (bf16[3,2,32,128]{3,2,1,0:T(8,128)(2,1)S(1)}, bf16[3,2,32,128]{3,2,1,0:T(8,128)(2,1)S(1)}, u32[]{:S(2)}, u32[]{:S(2)}) collective-permute-start(bf16[3,2,32,128]{3,2,1,0:T(8,128)(2,1)S(1)} %plane_to_send.2.refs_0_), channel_id=1, source_target_pairs={{0,1},{1,0},{2,3},{3,2},{4,5},{5,4},{6,7},{7,6},{8,16},{9,17},{10,... | collective-permute-start | bytes 147464 | tf_op jit(solution)/shard_map/ppermute | solution.py:271
  6.5 0.2 collective-permute-start
  6.7 0.0 copy-done
  6.7 0.0 copy-done.1
  6.7 2.6 %lookup.1 = (f32[8,8,16,8,128]{4,3,2,1,0:T(8,128)S(1)}, f32[3,8,2,32,128]{4,3,2,1,0:T(8,128)S(1)}, f32[3,8,2,32,128]{4,3,2,1,0:T(8,128)S(1)}, f32[12,8,128]{2,1,0:T(8,128)S(1)}) custom-call(f32[4,3]{1,0:T(4,128)S(1)} %copy-done.1, s32[4,4,256]{2,1,0:T(4,128)S(1)} %copy-done, bf16[3,8,2,32,128]{4,3,2,1,0:T(8,128)(2,1)S(1)} %reshape.3.cells), custom_call_target="tpu_custom_call" | custom-call | flops 4000000000 | bytes 8000000 | tf_op jit(solution)/shard_map/lookup/pallas_call | solution.py:273
  9.3 0.0 collective-permute-done.depth_a
  9.3 2.0 %collective-permute-done.1.depth_b = bf16[3,2,32,128]{3,2,1,0:T(8,128)(2,1)S(1)} collective-permute-done((bf16[3,2,32,128]{3,2,1,0:T(8,128)(2,1)S(1)}, bf16[3,2,32,128]{3,2,1,0:T(8,128)(2,1)S(1)}, u32[]{:S(2)}, u32[]{:S(2)}) %collective-permute-start.1) | collective-permute-done | bytes 49184 | tf_op jit(solution)/shard_map/ppermute | solution.py:271
  11.3 0.0 collective-permute-done.3.halo
  11.3 0.9 %shade_first.1.refs_0_ = f32[544,128]{1,0:T(8,128)S(1)} custom-call(f32[12,8,128]{2,1,0:T(8,128)S(1)} %get-tuple-element.11.half, f32[8,8,16,8,128]{4,3,2,1,0:T(8,128)S(1)} %get-tuple-element.12.hues, f32[3,8,2,32,128]{4,3,2,1,0:T(8,128)S(1)} %get-tuple-element.13.field, f32[3,8,2,32,128]{4,3,2,1,0:T(8,128)S(1)} %get-tuple-element.14.slope_x, ...), custom_call_target="tpu_custom_call" | custom-call | flops 2000000000 | bytes 4000000 | tf_op jit(solution)/shard_map/shade_first/pallas_call | solution.py:295
  12.2 0.0 collective-permute-done.2.halo
  12.2 0.9 %shade_second.1 = (f32[16,32,128]{2,1,0:T(8,128)S(1)}, f32[16,32,128]{2,1,0:T(8,128)S(1)}) custom-call(f32[12,8,128]{2,1,0:T(8,128)S(1)} %get-tuple-element.11.half, f32[8,8,16,8,128]{4,3,2,1,0:T(8,128)S(1)} %get-tuple-element.12.hues, f32[3,8,2,32,128]{4,3,2,1,0:T(8,128)S(1)} %get-tuple-element.13.field, ...), custom_call_target="tpu_custom_call" | custom-call | tf_op jit(solution)/shard_map/shade_second/pallas_call | solution.py:304
  13.1 0.1 collective-permute-start.4
  13.2 1.5 %collective-permute-done.4.other = f32[16,32,128]{2,1,0:T(8,128)S(1)} collective-permute-done((f32[16,32,128]{2,1,0:T(8,128)S(1)}, f32[16,32,128]{2,1,0:T(8,128)S(1)}, u32[]{:S(2)}, u32[]{:S(2)}) %collective-permute-start.4) | collective-permute-done | bytes 262176 | tf_op jit(solution)/shard_map/ppermute | solution.py:313
  14.7 0.2 join.1
  14.9 18.1 %all_to_all.5.parts = s16[16,32,128]{2,1,0:T(8,128)(2,1)S(1)} all-to-all(s16[16,32,128]{2,1,0:T(8,128)(2,1)S(1)} %join.1), channel_id=1, replica_groups={{0,16,32,48,64,80,96,112,128,144,160,176,192,208,224,240},{8,24,40,56,7..., dimensions={0} | all-to-all | bytes 262144 | tf_op jit(solution)/shard_map/all_to_all | solution.py:323
  33.0 0.8 %composite.1 = f32[4,4,2,128]{3,2,1,0:T(2,128)} custom-call(s16[16,32,128]{2,1,0:T(8,128)(2,1)S(1)} %all_to_all.5.parts), custom_call_target="tpu_custom_call" | custom-call | tf_op jit(solution)/shard_map/composite/pallas_call | solution.py:324
  (3 shorter events, 0.0 us)
Async XLA Ops:
  1.3 5.4 %copy-start = (s32[4,4,256]{2,1,0:T(4,128)S(1)}, s32[4,4,256]{2,1,0:T(4,128)}, u32[]{:S(2)}) copy-start(s32[4,4,256]{2,1,0:T(4,128)} %color_table.1) | copy-start | bytes 49156
  1.3 5.4 %copy-start.1 = (f32[4,3]{1,0:T(4,128)S(1)}, f32[4,3]{1,0:T(4,128)}, u32[]{:S(2)}) copy-start(f32[4,3]{1,0:T(4,128)} %weight.1) | copy-start | bytes 148
  1.4 10.8 %collective-permute-start.2 = (bf16[3,8,32,128]{3,2,1,0:T(8,128)(2,1)S(1)}, bf16[3,8,32,128]{3,2,1,0:T(8,128)(2,1)S(1)}, u32[]{:S(2)}, u32[]{:S(2)}) collective-permute-start(bf16[3,8,32,128]{3,2,1,0:T(8,128)(2,1)S(1)} %get-tuple-element.17.refs_1_), channel_id=1, source_target_pairs={{0,8},{1,2},{2,1},{3,4},{4,3},{5,6},{6,5},{7,15},{8,0},{9,10},{10,... | collective-permute-start | bytes 589832 | tf_op jit(solution)/shard_map/ppermute | solution.py:257
  4.4 6.9 %collective-permute-start.3 = (bf16[3,8,32,128]{3,2,1,0:T(8,128)(2,1)S(1)}, bf16[3,8,32,128]{3,2,1,0:T(8,128)(2,1)S(1)}, u32[]{:S(2)}, u32[]{:S(2)}) collective-permute-start(bf16[3,8,32,128]{3,2,1,0:T(8,128)(2,1)S(1)} %get-tuple-element.18.refs_0_), channel_id=1, source_target_pairs={{0,1},{1,0},{2,3},{3,2},{4,5},{5,4},{6,7},{7,6},{8,9},{9,8},{10,11... | collective-permute-start | bytes 589832 | tf_op jit(solution)/shard_map/ppermute | solution.py:256
  4.6 6.7 %collective-permute-start.1 = (bf16[3,2,32,128]{3,2,1,0:T(8,128)(2,1)S(1)}, bf16[3,2,32,128]{3,2,1,0:T(8,128)(2,1)S(1)}, u32[]{:S(2)}, u32[]{:S(2)}) collective-permute-start(bf16[3,2,32,128]{3,2,1,0:T(8,128)(2,1)S(1)} %plane_to_send.2.refs_0_), channel_id=1, source_target_pairs={{0,1},{1,0},{2,3},{3,2},{4,5},{5,4},{6,7},{7,6},{8,16},{9,17},{10,... | collective-permute-start | bytes 147464 | tf_op jit(solution)/shard_map/ppermute | solution.py:271
  6.5 2.8 %collective-permute-start = (bf16[3,2,32,128]{3,2,1,0:T(8,128)(2,1)S(1)}, bf16[3,2,32,128]{3,2,1,0:T(8,128)(2,1)S(1)}, u32[]{:S(2)}, u32[]{:S(2)}) collective-permute-start(bf16[3,2,32,128]{3,2,1,0:T(8,128)(2,1)S(1)} %plane_to_send.3), channel_id=1, source_target_pairs={{0,8},{1,9},{2,10},{3,11},{4,12},{5,13},{6,14},{7,15},{8,0},{9,1},... | collective-permute-start | bytes 147464 | tf_op jit(solution)/shard_map/ppermute | solution.py:272
  13.1 1.6 %collective-permute-start.4 = (f32[16,32,128]{2,1,0:T(8,128)S(1)}, f32[16,32,128]{2,1,0:T(8,128)S(1)}, u32[]{:S(2)}, u32[]{:S(2)}) collective-permute-start(f32[16,32,128]{2,1,0:T(8,128)S(1)} %get-tuple-element.16), channel_id=1, source_target_pairs={{0,8},{8,0},{16,24},{24,16},{32,40},{40,32},{48,56},{56,48},{64,72... | collective-permute-start | bytes 786440 | tf_op jit(solution)/shard_map/ppermute | solution.py:313

commit v10 on v9

--- a/solution.py
+++ b/solution.py
@@ -167,13 +167,11 @@
 
     lax.fori_loop(0, groups, chunk, 0)
 
-    if second:
-        first_image, kept, sent, _ = refs
-        for pair in range(blocks // 2):
-            for target, parity in ((kept, depth_odd), (sent, 1 - depth_odd)):
-                rows = pl.ds((2 * pair + parity) * pitch, kinds)
-                target[pair, :kinds] = first_image[rows, :]
-                target[pair, kinds:] = image[rows, :]
+    kept, sent = refs[-3:-1]
+    part = pl.ds(kinds if second else 0, kinds)
+    for pair in range(blocks // 2):
+        for target, parity in ((kept, depth_odd), (sent, 1 - depth_odd)):
+            target[pair, part] = image[pl.ds((2 * pair + parity) * pitch, kinds), :]
 
 
 FINE, COARSE, TOP, KNEE = 1500.0, 64.0, 32767.0, 40.0
@@ -290,26 +288,22 @@
         name="lookup",
     )(material_weight, color_table, cells)
     half_kinds = 4 * energies
-    tall = real(blocks * (half_kinds + 1), LANES)
+    tall = real(blocks * (half_kinds + 1) + 3 * ROWS, LANES)
     shared = (half, hues, field, slope_x, depth_a, depth_b)
-    first_image = pl.pallas_call(
-        functools.partial(shade, False),
-        out_shape=tall,
-        in_specs=[vmem] * 7,
-        out_specs=vmem,
-        compiler_params=limit(8),
-        cost_estimate=pl.CostEstimate(flops=2_000_000_000, bytes_accessed=4_000_000, transcendentals=100_000),
-        name="shade_first",
-    )(*shared, tile_a)
-    kept, sent = pl.pallas_call(
-        functools.partial(shade, True),
-        out_shape=(real(pairs, kinds, LANES),) * 2,
-        in_specs=[vmem] * 8,
-        out_specs=(vmem, vmem),
-        scratch_shapes=[pltpu.VMEM(tall.shape, jnp.float32)],
-        compiler_params=limit(8),
-        name="shade_second",
-    )(*shared, tile_b, first_image)
+    kept = sent = None
+    for second, halo in ((False, tile_a), (True, tile_b)):
+        filled = (kept, sent) if second else ()
+        kept, sent = pl.pallas_call(
+            functools.partial(shade, second),
+            out_shape=(real(pairs, kinds, LANES),) * 2,
+            in_specs=[vmem] * (7 + len(filled)),
+            out_specs=(vmem, vmem),
+            scratch_shapes=[pltpu.VMEM(tall.shape, jnp.float32)],
+            input_output_aliases={7: 0, 8: 1} if second else {},
+            compiler_params=limit(8),
+            cost_estimate=pl.CostEstimate(flops=2_000_000_000, bytes_accessed=4_000_000, transcendentals=100_000),
+            name="shade_second" if second else "shade_first",
+        )(*shared, halo, *filled)
     other = lax.ppermute(sent, "depth", [(i, i ^ 1) for i in range(depth)])
     joined = pl.pallas_call(
         functools.partial(join, energies),

time: 33.9 us -> 33.9 us (level)
  no operation moved by 1% of the time
where the time goes in v10:
time: 33.9 us; the launch traced here: 33.8 us
  blocking collectives  18.1 us (53%)
  starting transfers between devices  5.36 us (16%)
  Pallas kernels  5.35 us (16%)
  waiting for transfers between devices  3.53 us (10%)
  local copies, waits for them, and re-layouts  1.34 us (4%)
    all_to_all x1, blocking collectives, body(): lax.all_to_all(joined, 'depth', 0, 0, axis_index_groups=same_core, tiled=...  18.1 us
    ppermute x1, starting transfers between devices, body(): tile_b = lax.ppermute(rows[1], AXES, partners('tile', 1))  3.04 us
    pallas_call x1, Pallas kernels, body(): pl.pallas_call(functools.partial(lookup, planes * depth), out_shape=(real...  2.63 us
    ppermute x1, waiting for transfers between devices, body(): depth_b = lax.ppermute(plane_b, AXES, partners('depth', 1))  2 us
    ppermute x1, starting transfers between devices, body(): depth_b = lax.ppermute(plane_b, AXES, partners('depth', 1))  1.83 us
    pallas_call x2, Pallas kernels, body(): pl.pallas_call(functools.partial(shade, second), out_shape=(real(pairs, k...  1.78 us
    ppermute x1, waiting for transfers between devices, body(): other = lax.ppermute(sent, 'depth', [(i, i ^ 1) for i in range(depth)])  1.52 us
    reshape x1, local copies, waits for them, and re-layouts, body(): cells = density.reshape(mats, planes, lines, blocks, LANES)  1.29 us
  transfers between devices with their start and end apart: 5, of which 2 were waited for; matrix products, arithmetic and copies ran while one was open for 0% of the time, Pallas kernels for 10%

profile of v10, /device:TPU:4, one launch (start us, length us, event | category | flops | bytes accessed | tf_op | source)
XLA Modules:
  0.0 33.8 jit_solution(2060702023944753441)
XLA Ops:
  0.0 1.3 %reshape.3.cells = bf16[3,8,2,32,128]{4,3,2,1,0:T(8,128)(2,1)S(1)} reshape(bf16[3,8,2,4096]{3,2,1,0:T(2,128)(2,1)} %param.3) | data formatting | bytes 786432 | tf_op jit(solution)/shard_map/reshape | solution.py:252
  1.3 0.0 copy-start
  1.3 0.0 copy-start.1
  1.4 3.0 %collective-permute-start.2 = (bf16[3,8,32,128]{3,2,1,0:T(8,128)(2,1)S(1)}, bf16[3,8,32,128]{3,2,1,0:T(8,128)(2,1)S(1)}, u32[]{:S(2)}, u32[]{:S(2)}) collective-permute-start(bf16[3,8,32,128]{3,2,1,0:T(8,128)(2,1)S(1)} %get-tuple-element.21.refs_1_), channel_id=1, source_target_pairs={{0,8},{1,2},{2,1},{3,4},{4,3},{5,6},{6,5},{7,15},{8,0},{9,10},{10,... | collective-permute-start | bytes 589832 | tf_op jit(solution)/shard_map/ppermute | solution.py:255
  4.4 0.2 collective-permute-start.3
  4.6 1.8 %collective-permute-start.1 = (bf16[3,2,32,128]{3,2,1,0:T(8,128)(2,1)S(1)}, bf16[3,2,32,128]{3,2,1,0:T(8,128)(2,1)S(1)}, u32[]{:S(2)}, u32[]{:S(2)}) collective-permute-start(bf16[3,2,32,128]{3,2,1,0:T(8,128)(2,1)S(1)} %plane_to_send.2.refs_0_), channel_id=1, source_target_pairs={{0,1},{1,0},{2,3},{3,2},{4,5},{5,4},{6,7},{7,6},{8,16},{9,17},{10,... | collective-permute-start | bytes 147464 | tf_op jit(solution)/shard_map/ppermute | solution.py:269
  6.5 0.2 collective-permute-start
  6.7 0.0 copy-done
  6.7 0.0 copy-done.1
  6.7 2.6 %lookup.1 = (f32[8,8,16,8,128]{4,3,2,1,0:T(8,128)S(1)}, f32[3,8,2,32,128]{4,3,2,1,0:T(8,128)S(1)}, f32[3,8,2,32,128]{4,3,2,1,0:T(8,128)S(1)}, f32[12,8,128]{2,1,0:T(8,128)S(1)}) custom-call(f32[4,3]{1,0:T(4,128)S(1)} %copy-done.1, s32[4,4,256]{2,1,0:T(4,128)S(1)} %copy-done, bf16[3,8,2,32,128]{4,3,2,1,0:T(8,128)(2,1)S(1)} %reshape.3.cells), custom_call_target="tpu_custom_call" | custom-call | flops 4000000000 | bytes 8000000 | tf_op jit(solution)/shard_map/lookup/pallas_call | solution.py:271
  9.3 0.0 collective-permute-done.depth_a
  9.3 2.0 %collective-permute-done.1.depth_b = bf16[3,2,32,128]{3,2,1,0:T(8,128)(2,1)S(1)} collective-permute-done((bf16[3,2,32,128]{3,2,1,0:T(8,128)(2,1)S(1)}, bf16[3,2,32,128]{3,2,1,0:T(8,128)(2,1)S(1)}, u32[]{:S(2)}, u32[]{:S(2)}) %collective-permute-start.1) | collective-permute-done | bytes 49184 | tf_op jit(solution)/shard_map/ppermute | solution.py:269
  11.3 0.0 collective-permute-done.3.halo
  11.3 0.9 %shade_first.1 = (f32[16,32,128]{2,1,0:T(8,128)S(1)}, f32[16,32,128]{2,1,0:T(8,128)S(1)}) custom-call(f32[12,8,128]{2,1,0:T(8,128)S(1)} %get-tuple-element.13.half, f32[8,8,16,8,128]{4,3,2,1,0:T(8,128)S(1)} %get-tuple-element.14.hues, f32[3,8,2,32,128]{4,3,2,1,0:T(8,128)S(1)} %get-tuple-element.15.field, ...), custom_call_target="tpu_custom_call" | custom-call | flops 2000000000 | bytes 4000000 | tf_op jit(solution)/shard_map/shade_first/pallas_call | solution.py:296
  12.2 0.0 collective-permute-done.2.halo
  12.2 0.9 %shade_second.1 = (f32[16,32,128]{2,1,0:T(8,128)S(1)}, f32[16,32,128]{2,1,0:T(8,128)S(1)}) custom-call(f32[12,8,128]{2,1,0:T(8,128)S(1)} %get-tuple-element.13.half, f32[8,8,16,8,128]{4,3,2,1,0:T(8,128)S(1)} %get-tuple-element.14.hues, f32[3,8,2,32,128]{4,3,2,1,0:T(8,128)S(1)} %get-tuple-element.15.field, ...), custom_call_target="tpu_custom_call", output_to_operand_aliasing={{0}: (7, {}), {1}: (8, {})} | custom-call | flops 2000000000 | bytes 4000000 | tf_op jit(solution)/shard_map/shade_second/pallas_call | solution.py:296
  13.1 0.1 collective-permute-start.4
  13.2 1.5 %collective-permute-done.4.other = f32[16,32,128]{2,1,0:T(8,128)S(1)} collective-permute-done((f32[16,32,128]{2,1,0:T(8,128)S(1)}, f32[16,32,128]{2,1,0:T(8,128)S(1)}, u32[]{:S(2)}, u32[]{:S(2)}) %collective-permute-start.4) | collective-permute-done | bytes 262176 | tf_op jit(solution)/shard_map/ppermute | solution.py:307
  14.7 0.2 join.1
  14.9 18.1 %all_to_all.5.parts = s16[16,32,128]{2,1,0:T(8,128)(2,1)S(1)} all-to-all(s16[16,32,128]{2,1,0:T(8,128)(2,1)S(1)} %join.1), channel_id=1, replica_groups={{0,16,32,48,64,80,96,112,128,144,160,176,192,208,224,240},{8,24,40,56,7..., dimensions={0} | all-to-all | bytes 262144 | tf_op jit(solution)/shard_map/all_to_all | solution.py:317
  33.0 0.8 %composite.1 = f32[4,4,2,128]{3,2,1,0:T(2,128)} custom-call(s16[16,32,128]{2,1,0:T(8,128)(2,1)S(1)} %all_to_all.5.parts), custom_call_target="tpu_custom_call" | custom-call | tf_op jit(solution)/shard_map/composite/pallas_call | solution.py:318
  (3 shorter events, 0.0 us)
Async XLA Ops:
  1.3 5.4 %copy-start = (s32[4,4,256]{2,1,0:T(4,128)S(1)}, s32[4,4,256]{2,1,0:T(4,128)}, u32[]{:S(2)}) copy-start(s32[4,4,256]{2,1,0:T(4,128)} %color_table.1) | copy-start | bytes 49156
  1.3 5.4 %copy-start.1 = (f32[4,3]{1,0:T(4,128)S(1)}, f32[4,3]{1,0:T(4,128)}, u32[]{:S(2)}) copy-start(f32[4,3]{1,0:T(4,128)} %weight.1) | copy-start | bytes 148
  1.4 10.8 %collective-permute-start.2 = (bf16[3,8,32,128]{3,2,1,0:T(8,128)(2,1)S(1)}, bf16[3,8,32,128]{3,2,1,0:T(8,128)(2,1)S(1)}, u32[]{:S(2)}, u32[]{:S(2)}) collective-permute-start(bf16[3,8,32,128]{3,2,1,0:T(8,128)(2,1)S(1)} %get-tuple-element.21.refs_1_), channel_id=1, source_target_pairs={{0,8},{1,2},{2,1},{3,4},{4,3},{5,6},{6,5},{7,15},{8,0},{9,10},{10,... | collective-permute-start | bytes 589832 | tf_op jit(solution)/shard_map/ppermute | solution.py:255
  4.4 6.9 %collective-permute-start.3 = (bf16[3,8,32,128]{3,2,1,0:T(8,128)(2,1)S(1)}, bf16[3,8,32,128]{3,2,1,0:T(8,128)(2,1)S(1)}, u32[]{:S(2)}, u32[]{:S(2)}) collective-permute-start(bf16[3,8,32,128]{3,2,1,0:T(8,128)(2,1)S(1)} %get-tuple-element.22.refs_0_), channel_id=1, source_target_pairs={{0,1},{1,0},{2,3},{3,2},{4,5},{5,4},{6,7},{7,6},{8,9},{9,8},{10,11... | collective-permute-start | bytes 589832 | tf_op jit(solution)/shard_map/ppermute | solution.py:254
  4.6 6.7 %collective-permute-start.1 = (bf16[3,2,32,128]{3,2,1,0:T(8,128)(2,1)S(1)}, bf16[3,2,32,128]{3,2,1,0:T(8,128)(2,1)S(1)}, u32[]{:S(2)}, u32[]{:S(2)}) collective-permute-start(bf16[3,2,32,128]{3,2,1,0:T(8,128)(2,1)S(1)} %plane_to_send.2.refs_0_), channel_id=1, source_target_pairs={{0,1},{1,0},{2,3},{3,2},{4,5},{5,4},{6,7},{7,6},{8,16},{9,17},{10,... | collective-permute-start | bytes 147464 | tf_op jit(solution)/shard_map/ppermute | solution.py:269
  6.5 2.8 %collective-permute-start = (bf16[3,2,32,128]{3,2,1,0:T(8,128)(2,1)S(1)}, bf16[3,2,32,128]{3,2,1,0:T(8,128)(2,1)S(1)}, u32[]{:S(2)}, u32[]{:S(2)}) collective-permute-start(bf16[3,2,32,128]{3,2,1,0:T(8,128)(2,1)S(1)} %plane_to_send.3), channel_id=1, source_target_pairs={{0,8},{1,9},{2,10},{3,11},{4,12},{5,13},{6,14},{7,15},{8,0},{9,1},... | collective-permute-start | bytes 147464 | tf_op jit(solution)/shard_map/ppermute | solution.py:270
  13.1 1.6 %collective-permute-start.4 = (f32[16,32,128]{2,1,0:T(8,128)S(1)}, f32[16,32,128]{2,1,0:T(8,128)S(1)}, u32[]{:S(2)}, u32[]{:S(2)}) collective-permute-start(f32[16,32,128]{2,1,0:T(8,128)S(1)} %get-tuple-element.20), channel_id=1, source_target_pairs={{0,8},{8,0},{16,24},{24,16},{32,40},{40,32},{48,56},{56,48},{64,72... | collective-permute-start | bytes 786440 | tf_op jit(solution)/shard_map/ppermute | solution.py:307

commit v11 on v10

--- a/solution.py
+++ b/solution.py
@@ -103,13 +103,14 @@
                 at_odd, at_even = rounded(away), rounded(1.0 - away)
                 word_odd = pick(jnp.broadcast_to(odd[e : e + 1, :], (ROWS, LANES)), level.astype(jnp.int32))
                 word_even = pick(jnp.broadcast_to(even[e : e + 1, :], (ROWS, LANES)), next_even)
-                level_of = lambda word, c: (lax.shift_right_logical(word, 8 * c) & 255).astype(jnp.float32)
+                shift = lambda word, c: lax.shift_right_logical(word, 8 * c) if c else word
+                level_of = lambda word, c: (shift(word, c) & 255 if c < 3 else shift(word, c)).astype(jnp.float32)
                 for c in range(4):
                     hue = at_even * level_of(word_even, c) + at_odd * level_of(word_odd, c)
                     hues[plane, y * groups + group, 4 * e + c] = hue if c < 3 else hue * (6.0 / (255.0 * depth_total))
         return 0
 
-    lax.fori_loop(0, planes * lines, line, 0, unroll=4)
+    lax.fori_loop(0, planes * lines, line, 0, unroll=8)
 
 
 def shade(second, half, hues, field, slope_x, depth_a, depth_b, halo, *refs):

time: 33.9 us -> 33.9 us (level)
  no operation moved by 1% of the time
where the time goes in v11:
time: 33.9 us; the launch traced here: 33.8 us
  blocking collectives  18.1 us (53%)
  starting transfers between devices  5.36 us (16%)
  Pallas kernels  5.31 us (16%)
  waiting for transfers between devices  3.58 us (11%)
  local copies, waits for them, and re-layouts  1.34 us (4%)
    all_to_all x1, blocking collectives, body(): lax.all_to_all(joined, 'depth', 0, 0, axis_index_groups=same_core, tiled=...  18.1 us
    ppermute x1, starting transfers between devices, body(): tile_b = lax.ppermute(rows[1], AXES, partners('tile', 1))  3.04 us
    pallas_call x1, Pallas kernels, body(): pl.pallas_call(functools.partial(lookup, planes * depth), out_shape=(real...  2.58 us
    ppermute x1, waiting for transfers between devices, body(): depth_b = lax.ppermute(plane_b, AXES, partners('depth', 1))  2.05 us
    ppermute x1, starting transfers between devices, body(): depth_b = lax.ppermute(plane_b, AXES, partners('depth', 1))  1.83 us
    pallas_call x2, Pallas kernels, body(): pl.pallas_call(functools.partial(shade, second), out_shape=(real(pairs, k...  1.78 us
    ppermute x1, waiting for transfers between devices, body(): other = lax.ppermute(sent, 'depth', [(i, i ^ 1) for i in range(depth)])  1.52 us
    reshape x1, local copies, waits for them, and re-layouts, body(): cells = density.reshape(mats, planes, lines, blocks, LANES)  1.29 us
  transfers between devices with their start and end apart: 5, of which 2 were waited for; matrix products, arithmetic and copies ran while one was open for 0% of the time, Pallas kernels for 10%

profile of v11, /device:TPU:4, one launch (start us, length us, event | category | flops | bytes accessed | tf_op | source)
XLA Modules:
  0.0 33.8 jit_solution(13284709834610441591)
XLA Ops:
  0.0 1.3 %reshape.3.cells = bf16[3,8,2,32,128]{4,3,2,1,0:T(8,128)(2,1)S(1)} reshape(bf16[3,8,2,4096]{3,2,1,0:T(2,128)(2,1)} %param.3) | data formatting | bytes 786432 | tf_op jit(solution)/shard_map/reshape | solution.py:253
  1.3 0.0 copy-start
  1.3 0.0 copy-start.1
  1.4 3.0 %collective-permute-start.2 = (bf16[3,8,32,128]{3,2,1,0:T(8,128)(2,1)S(1)}, bf16[3,8,32,128]{3,2,1,0:T(8,128)(2,1)S(1)}, u32[]{:S(2)}, u32[]{:S(2)}) collective-permute-start(bf16[3,8,32,128]{3,2,1,0:T(8,128)(2,1)S(1)} %get-tuple-element.21.refs_1_), channel_id=1, source_target_pairs={{0,8},{1,2},{2,1},{3,4},{4,3},{5,6},{6,5},{7,15},{8,0},{9,10},{10,... | collective-permute-start | bytes 589832 | tf_op jit(solution)/shard_map/ppermute | solution.py:256
  4.4 0.2 collective-permute-start.3
  4.6 1.8 %collective-permute-start.1 = (bf16[3,2,32,128]{3,2,1,0:T(8,128)(2,1)S(1)}, bf16[3,2,32,128]{3,2,1,0:T(8,128)(2,1)S(1)}, u32[]{:S(2)}, u32[]{:S(2)}) collective-permute-start(bf16[3,2,32,128]{3,2,1,0:T(8,128)(2,1)S(1)} %plane_to_send.2.refs_0_), channel_id=1, source_target_pairs={{0,1},{1,0},{2,3},{3,2},{4,5},{5,4},{6,7},{7,6},{8,16},{9,17},{10,... | collective-permute-start | bytes 147464 | tf_op jit(solution)/shard_map/ppermute | solution.py:270
  6.5 0.2 collective-permute-start
  6.7 0.0 copy-done
  6.7 0.0 copy-done.1
  6.7 2.6 %lookup.1 = (f32[8,8,16,8,128]{4,3,2,1,0:T(8,128)S(1)}, f32[3,8,2,32,128]{4,3,2,1,0:T(8,128)S(1)}, f32[3,8,2,32,128]{4,3,2,1,0:T(8,128)S(1)}, f32[12,8,128]{2,1,0:T(8,128)S(1)}) custom-call(f32[4,3]{1,0:T(4,128)S(1)} %copy-done.1, s32[4,4,256]{2,1,0:T(4,128)S(1)} %copy-done, bf16[3,8,2,32,128]{4,3,2,1,0:T(8,128)(2,1)S(1)} %reshape.3.cells), custom_call_target="tpu_custom_call" | custom-call | flops 4000000000 | bytes 8000000 | tf_op jit(solution)/shard_map/lookup/pallas_call | solution.py:272
  9.2 0.0 collective-permute-done.depth_a
  9.3 2.0 %collective-permute-done.1.depth_b = bf16[3,2,32,128]{3,2,1,0:T(8,128)(2,1)S(1)} collective-permute-done((bf16[3,2,32,128]{3,2,1,0:T(8,128)(2,1)S(1)}, bf16[3,2,32,128]{3,2,1,0:T(8,128)(2,1)S(1)}, u32[]{:S(2)}, u32[]{:S(2)}) %collective-permute-start.1) | collective-permute-done | bytes 49184 | tf_op jit(solution)/shard_map/ppermute | solution.py:270
  11.3 0.0 collective-permute-done.3.halo
  11.3 0.9 %shade_first.1 = (f32[16,32,128]{2,1,0:T(8,128)S(1)}, f32[16,32,128]{2,1,0:T(8,128)S(1)}) custom-call(f32[12,8,128]{2,1,0:T(8,128)S(1)} %get-tuple-element.13.half, f32[8,8,16,8,128]{4,3,2,1,0:T(8,128)S(1)} %get-tuple-element.14.hues, f32[3,8,2,32,128]{4,3,2,1,0:T(8,128)S(1)} %get-tuple-element.15.field, ...), custom_call_target="tpu_custom_call" | custom-call | flops 2000000000 | bytes 4000000 | tf_op jit(solution)/shard_map/shade_first/pallas_call | solution.py:297
  12.2 0.0 collective-permute-done.2.halo
  12.2 0.9 %shade_second.1 = (f32[16,32,128]{2,1,0:T(8,128)S(1)}, f32[16,32,128]{2,1,0:T(8,128)S(1)}) custom-call(f32[12,8,128]{2,1,0:T(8,128)S(1)} %get-tuple-element.13.half, f32[8,8,16,8,128]{4,3,2,1,0:T(8,128)S(1)} %get-tuple-element.14.hues, f32[3,8,2,32,128]{4,3,2,1,0:T(8,128)S(1)} %get-tuple-element.15.field, ...), custom_call_target="tpu_custom_call", output_to_operand_aliasing={{0}: (7, {}), {1}: (8, {})} | custom-call | flops 2000000000 | bytes 4000000 | tf_op jit(solution)/shard_map/shade_second/pallas_call | solution.py:297
  13.1 0.1 collective-permute-start.4
  13.2 1.5 %collective-permute-done.4.other = f32[16,32,128]{2,1,0:T(8,128)S(1)} collective-permute-done((f32[16,32,128]{2,1,0:T(8,128)S(1)}, f32[16,32,128]{2,1,0:T(8,128)S(1)}, u32[]{:S(2)}, u32[]{:S(2)}) %collective-permute-start.4) | collective-permute-done | bytes 262176 | tf_op jit(solution)/shard_map/ppermute | solution.py:308
  14.7 0.2 join.1
  14.9 18.1 %all_to_all.5.parts = s16[16,32,128]{2,1,0:T(8,128)(2,1)S(1)} all-to-all(s16[16,32,128]{2,1,0:T(8,128)(2,1)S(1)} %join.1), channel_id=1, replica_groups={{0,16,32,48,64,80,96,112,128,144,160,176,192,208,224,240},{8,24,40,56,7..., dimensions={0} | all-to-all | bytes 262144 | tf_op jit(solution)/shard_map/all_to_all | solution.py:318
  33.0 0.8 %composite.1 = f32[4,4,2,128]{3,2,1,0:T(2,128)} custom-call(s16[16,32,128]{2,1,0:T(8,128)(2,1)S(1)} %all_to_all.5.parts), custom_call_target="tpu_custom_call" | custom-call | tf_op jit(solution)/shard_map/composite/pallas_call | solution.py:319
  (3 shorter events, 0.0 us)
Async XLA Ops:
  1.3 5.4 %copy-start = (s32[4,4,256]{2,1,0:T(4,128)S(1)}, s32[4,4,256]{2,1,0:T(4,128)}, u32[]{:S(2)}) copy-start(s32[4,4,256]{2,1,0:T(4,128)} %color_table.1) | copy-start | bytes 49156
  1.3 5.4 %copy-start.1 = (f32[4,3]{1,0:T(4,128)S(1)}, f32[4,3]{1,0:T(4,128)}, u32[]{:S(2)}) copy-start(f32[4,3]{1,0:T(4,128)} %weight.1) | copy-start | bytes 148
  1.4 10.8 %collective-permute-start.2 = (bf16[3,8,32,128]{3,2,1,0:T(8,128)(2,1)S(1)}, bf16[3,8,32,128]{3,2,1,0:T(8,128)(2,1)S(1)}, u32[]{:S(2)}, u32[]{:S(2)}) collective-permute-start(bf16[3,8,32,128]{3,2,1,0:T(8,128)(2,1)S(1)} %get-tuple-element.21.refs_1_), channel_id=1, source_target_pairs={{0,8},{1,2},{2,1},{3,4},{4,3},{5,6},{6,5},{7,15},{8,0},{9,10},{10,... | collective-permute-start | bytes 589832 | tf_op jit(solution)/shard_map/ppermute | solution.py:256
  4.4 6.9 %collective-permute-start.3 = (bf16[3,8,32,128]{3,2,1,0:T(8,128)(2,1)S(1)}, bf16[3,8,32,128]{3,2,1,0:T(8,128)(2,1)S(1)}, u32[]{:S(2)}, u32[]{:S(2)}) collective-permute-start(bf16[3,8,32,128]{3,2,1,0:T(8,128)(2,1)S(1)} %get-tuple-element.22.refs_0_), channel_id=1, source_target_pairs={{0,1},{1,0},{2,3},{3,2},{4,5},{5,4},{6,7},{7,6},{8,9},{9,8},{10,11... | collective-permute-start | bytes 589832 | tf_op jit(solution)/shard_map/ppermute | solution.py:255
  4.6 6.7 %collective-permute-start.1 = (bf16[3,2,32,128]{3,2,1,0:T(8,128)(2,1)S(1)}, bf16[3,2,32,128]{3,2,1,0:T(8,128)(2,1)S(1)}, u32[]{:S(2)}, u32[]{:S(2)}) collective-permute-start(bf16[3,2,32,128]{3,2,1,0:T(8,128)(2,1)S(1)} %plane_to_send.2.refs_0_), channel_id=1, source_target_pairs={{0,1},{1,0},{2,3},{3,2},{4,5},{5,4},{6,7},{7,6},{8,16},{9,17},{10,... | collective-permute-start | bytes 147464 | tf_op jit(solution)/shard_map/ppermute | solution.py:270
  6.5 2.8 %collective-permute-start = (bf16[3,2,32,128]{3,2,1,0:T(8,128)(2,1)S(1)}, bf16[3,2,32,128]{3,2,1,0:T(8,128)(2,1)S(1)}, u32[]{:S(2)}, u32[]{:S(2)}) collective-permute-start(bf16[3,2,32,128]{3,2,1,0:T(8,128)(2,1)S(1)} %plane_to_send.3), channel_id=1, source_target_pairs={{0,8},{1,9},{2,10},{3,11},{4,12},{5,13},{6,14},{7,15},{8,0},{9,1},... | collective-permute-start | bytes 147464 | tf_op jit(solution)/shard_map/ppermute | solution.py:271
  13.1 1.6 %collective-permute-start.4 = (f32[16,32,128]{2,1,0:T(8,128)S(1)}, f32[16,32,128]{2,1,0:T(8,128)S(1)}, u32[]{:S(2)}, u32[]{:S(2)}) collective-permute-start(f32[16,32,128]{2,1,0:T(8,128)S(1)} %get-tuple-element.20), channel_id=1, source_target_pairs={{0,8},{8,0},{16,24},{24,16},{32,40},{40,32},{48,56},{56,48},{64,72... | collective-permute-start | bytes 786440 | tf_op jit(solution)/shard_map/ppermute | solution.py:308

commit v12 on v11

--- a/solution.py
+++ b/solution.py
@@ -166,7 +166,7 @@
                 image[pl.ds(group * (ROWS * pitch) + c * energies + e, ROWS, stride=pitch), :] = value
         return 0
 
-    lax.fori_loop(0, groups, chunk, 0)
+    lax.fori_loop(0, groups, chunk, 0, unroll=2)
 
     kept, sent = refs[-3:-1]
     part = pl.ds(kinds if second else 0, kinds)

time: 33.9 us -> 33.9 us (level)
  no operation moved by 1% of the time
where the time goes in v12:
time: 33.9 us; the launch traced here: 33.7 us
  blocking collectives  18.1 us (53%)
  starting transfers between devices  5.36 us (16%)
  Pallas kernels  5.25 us (15%)
  waiting for transfers between devices  3.58 us (11%)
  local copies, waits for them, and re-layouts  1.34 us (4%)
    all_to_all x1, blocking collectives, body(): lax.all_to_all(joined, 'depth', 0, 0, axis_index_groups=same_core, tiled=...  18.1 us
    ppermute x1, starting transfers between devices, body(): tile_b = lax.ppermute(rows[1], AXES, partners('tile', 1))  3.04 us
    pallas_call x1, Pallas kernels, body(): pl.pallas_call(functools.partial(lookup, planes * depth), out_shape=(real...  2.58 us
    ppermute x1, waiting for transfers between devices, body(): depth_b = lax.ppermute(plane_b, AXES, partners('depth', 1))  2.05 us
    ppermute x1, starting transfers between devices, body(): depth_b = lax.ppermute(plane_b, AXES, partners('depth', 1))  1.83 us
    pallas_call x2, Pallas kernels, body(): pl.pallas_call(functools.partial(shade, second), out_shape=(real(pairs, k...  1.72 us
    ppermute x1, waiting for transfers between devices, body(): other = lax.ppermute(sent, 'depth', [(i, i ^ 1) for i in range(depth)])  1.52 us
    reshape x1, local copies, waits for them, and re-layouts, body(): cells = density.reshape(mats, planes, lines, blocks, LANES)  1.29 us
  transfers between devices with their start and end apart: 5, of which 2 were waited for; matrix products, arithmetic and copies ran while one was open for 0% of the time, Pallas kernels for 10%

profile of v12, /device:TPU:4, one launch (start us, length us, event | category | flops | bytes accessed | tf_op | source)
XLA Modules:
  0.0 33.7 jit_solution(968332770956836127)
XLA Ops:
  0.0 1.3 %reshape.3.cells = bf16[3,8,2,32,128]{4,3,2,1,0:T(8,128)(2,1)S(1)} reshape(bf16[3,8,2,4096]{3,2,1,0:T(2,128)(2,1)} %param.3) | data formatting | bytes 786432 | tf_op jit(solution)/shard_map/reshape | solution.py:253
  1.3 0.0 copy-start
  1.3 0.0 copy-start.1
  1.4 3.0 %collective-permute-start.2 = (bf16[3,8,32,128]{3,2,1,0:T(8,128)(2,1)S(1)}, bf16[3,8,32,128]{3,2,1,0:T(8,128)(2,1)S(1)}, u32[]{:S(2)}, u32[]{:S(2)}) collective-permute-start(bf16[3,8,32,128]{3,2,1,0:T(8,128)(2,1)S(1)} %get-tuple-element.21.refs_1_), channel_id=1, source_target_pairs={{0,8},{1,2},{2,1},{3,4},{4,3},{5,6},{6,5},{7,15},{8,0},{9,10},{10,... | collective-permute-start | bytes 589832 | tf_op jit(solution)/shard_map/ppermute | solution.py:256
  4.4 0.2 collective-permute-start.3
  4.6 1.8 %collective-permute-start.1 = (bf16[3,2,32,128]{3,2,1,0:T(8,128)(2,1)S(1)}, bf16[3,2,32,128]{3,2,1,0:T(8,128)(2,1)S(1)}, u32[]{:S(2)}, u32[]{:S(2)}) collective-permute-start(bf16[3,2,32,128]{3,2,1,0:T(8,128)(2,1)S(1)} %plane_to_send.2.refs_0_), channel_id=1, source_target_pairs={{0,1},{1,0},{2,3},{3,2},{4,5},{5,4},{6,7},{7,6},{8,16},{9,17},{10,... | collective-permute-start | bytes 147464 | tf_op jit(solution)/shard_map/ppermute | solution.py:270
  6.5 0.2 collective-permute-start
  6.7 0.0 copy-done
  6.7 0.0 copy-done.1
  6.7 2.6 %lookup.1 = (f32[8,8,16,8,128]{4,3,2,1,0:T(8,128)S(1)}, f32[3,8,2,32,128]{4,3,2,1,0:T(8,128)S(1)}, f32[3,8,2,32,128]{4,3,2,1,0:T(8,128)S(1)}, f32[12,8,128]{2,1,0:T(8,128)S(1)}) custom-call(f32[4,3]{1,0:T(4,128)S(1)} %copy-done.1, s32[4,4,256]{2,1,0:T(4,128)S(1)} %copy-done, bf16[3,8,2,32,128]{4,3,2,1,0:T(8,128)(2,1)S(1)} %reshape.3.cells), custom_call_target="tpu_custom_call" | custom-call | flops 4000000000 | bytes 8000000 | tf_op jit(solution)/shard_map/lookup/pallas_call | solution.py:272
  9.2 0.0 collective-permute-done.depth_a
  9.3 2.0 %collective-permute-done.1.depth_b = bf16[3,2,32,128]{3,2,1,0:T(8,128)(2,1)S(1)} collective-permute-done((bf16[3,2,32,128]{3,2,1,0:T(8,128)(2,1)S(1)}, bf16[3,2,32,128]{3,2,1,0:T(8,128)(2,1)S(1)}, u32[]{:S(2)}, u32[]{:S(2)}) %collective-permute-start.1) | collective-permute-done | bytes 49184 | tf_op jit(solution)/shard_map/ppermute | solution.py:270
  11.3 0.0 collective-permute-done.3.halo
  11.3 0.8 %shade_first.1 = (f32[16,32,128]{2,1,0:T(8,128)S(1)}, f32[16,32,128]{2,1,0:T(8,128)S(1)}) custom-call(f32[12,8,128]{2,1,0:T(8,128)S(1)} %get-tuple-element.13.half, f32[8,8,16,8,128]{4,3,2,1,0:T(8,128)S(1)} %get-tuple-element.14.hues, f32[3,8,2,32,128]{4,3,2,1,0:T(8,128)S(1)} %get-tuple-element.15.field, ...), custom_call_target="tpu_custom_call" | custom-call | flops 2000000000 | bytes 4000000 | tf_op jit(solution)/shard_map/shade_first/pallas_call | solution.py:297
  12.2 0.0 collective-permute-done.2.halo
  12.2 0.9 %shade_second.1 = (f32[16,32,128]{2,1,0:T(8,128)S(1)}, f32[16,32,128]{2,1,0:T(8,128)S(1)}) custom-call(f32[12,8,128]{2,1,0:T(8,128)S(1)} %get-tuple-element.13.half, f32[8,8,16,8,128]{4,3,2,1,0:T(8,128)S(1)} %get-tuple-element.14.hues, f32[3,8,2,32,128]{4,3,2,1,0:T(8,128)S(1)} %get-tuple-element.15.field, ...), custom_call_target="tpu_custom_call", output_to_operand_aliasing={{0}: (7, {}), {1}: (8, {})} | custom-call | flops 2000000000 | bytes 4000000 | tf_op jit(solution)/shard_map/shade_second/pallas_call | solution.py:297
  13.1 0.1 collective-permute-start.4
  13.2 1.5 %collective-permute-done.4.other = f32[16,32,128]{2,1,0:T(8,128)S(1)} collective-permute-done((f32[16,32,128]{2,1,0:T(8,128)S(1)}, f32[16,32,128]{2,1,0:T(8,128)S(1)}, u32[]{:S(2)}, u32[]{:S(2)}) %collective-permute-start.4) | collective-permute-done | bytes 262176 | tf_op jit(solution)/shard_map/ppermute | solution.py:308
  14.7 0.2 join.1
  14.9 18.1 %all_to_all.5.parts = s16[16,32,128]{2,1,0:T(8,128)(2,1)S(1)} all-to-all(s16[16,32,128]{2,1,0:T(8,128)(2,1)S(1)} %join.1), channel_id=1, replica_groups={{0,16,32,48,64,80,96,112,128,144,160,176,192,208,224,240},{8,24,40,56,7..., dimensions={0} | all-to-all | bytes 262144 | tf_op jit(solution)/shard_map/all_to_all | solution.py:318
  33.0 0.8 %composite.1 = f32[4,4,2,128]{3,2,1,0:T(2,128)} custom-call(s16[16,32,128]{2,1,0:T(8,128)(2,1)S(1)} %all_to_all.5.parts), custom_call_target="tpu_custom_call" | custom-call | tf_op jit(solution)/shard_map/composite/pallas_call | solution.py:319
  (3 shorter events, 0.0 us)
Async XLA Ops:
  1.3 5.4 %copy-start = (s32[4,4,256]{2,1,0:T(4,128)S(1)}, s32[4,4,256]{2,1,0:T(4,128)}, u32[]{:S(2)}) copy-start(s32[4,4,256]{2,1,0:T(4,128)} %color_table.1) | copy-start | bytes 49156
  1.3 5.4 %copy-start.1 = (f32[4,3]{1,0:T(4,128)S(1)}, f32[4,3]{1,0:T(4,128)}, u32[]{:S(2)}) copy-start(f32[4,3]{1,0:T(4,128)} %weight.1) | copy-start | bytes 148
  1.4 10.8 %collective-permute-start.2 = (bf16[3,8,32,128]{3,2,1,0:T(8,128)(2,1)S(1)}, bf16[3,8,32,128]{3,2,1,0:T(8,128)(2,1)S(1)}, u32[]{:S(2)}, u32[]{:S(2)}) collective-permute-start(bf16[3,8,32,128]{3,2,1,0:T(8,128)(2,1)S(1)} %get-tuple-element.21.refs_1_), channel_id=1, source_target_pairs={{0,8},{1,2},{2,1},{3,4},{4,3},{5,6},{6,5},{7,15},{8,0},{9,10},{10,... | collective-permute-start | bytes 589832 | tf_op jit(solution)/shard_map/ppermute | solution.py:256
  4.4 6.9 %collective-permute-start.3 = (bf16[3,8,32,128]{3,2,1,0:T(8,128)(2,1)S(1)}, bf16[3,8,32,128]{3,2,1,0:T(8,128)(2,1)S(1)}, u32[]{:S(2)}, u32[]{:S(2)}) collective-permute-start(bf16[3,8,32,128]{3,2,1,0:T(8,128)(2,1)S(1)} %get-tuple-element.22.refs_0_), channel_id=1, source_target_pairs={{0,1},{1,0},{2,3},{3,2},{4,5},{5,4},{6,7},{7,6},{8,9},{9,8},{10,11... | collective-permute-start | bytes 589832 | tf_op jit(solution)/shard_map/ppermute | solution.py:255
  4.6 6.7 %collective-permute-start.1 = (bf16[3,2,32,128]{3,2,1,0:T(8,128)(2,1)S(1)}, bf16[3,2,32,128]{3,2,1,0:T(8,128)(2,1)S(1)}, u32[]{:S(2)}, u32[]{:S(2)}) collective-permute-start(bf16[3,2,32,128]{3,2,1,0:T(8,128)(2,1)S(1)} %plane_to_send.2.refs_0_), channel_id=1, source_target_pairs={{0,1},{1,0},{2,3},{3,2},{4,5},{5,4},{6,7},{7,6},{8,16},{9,17},{10,... | collective-permute-start | bytes 147464 | tf_op jit(solution)/shard_map/ppermute | solution.py:270
  6.5 2.8 %collective-permute-start = (bf16[3,2,32,128]{3,2,1,0:T(8,128)(2,1)S(1)}, bf16[3,2,32,128]{3,2,1,0:T(8,128)(2,1)S(1)}, u32[]{:S(2)}, u32[]{:S(2)}) collective-permute-start(bf16[3,2,32,128]{3,2,1,0:T(8,128)(2,1)S(1)} %plane_to_send.3), channel_id=1, source_target_pairs={{0,8},{1,9},{2,10},{3,11},{4,12},{5,13},{6,14},{7,15},{8,0},{9,1},... | collective-permute-start | bytes 147464 | tf_op jit(solution)/shard_map/ppermute | solution.py:271
  13.1 1.6 %collective-permute-start.4 = (f32[16,32,128]{2,1,0:T(8,128)S(1)}, f32[16,32,128]{2,1,0:T(8,128)S(1)}, u32[]{:S(2)}, u32[]{:S(2)}) collective-permute-start(f32[16,32,128]{2,1,0:T(8,128)S(1)} %get-tuple-element.20), channel_id=1, source_target_pairs={{0,8},{8,0},{16,24},{24,16},{32,40},{40,32},{48,56},{56,48},{64,72... | collective-permute-start | bytes 786440 | tf_op jit(solution)/shard_map/ppermute | solution.py:308
